TPU v7x, 32 devices: a whole 2x2x4 slice. The times are simulated.
32 devices in a mesh: dp: 4 (over x, core), expert: 8 (over z, y).
Axes of the slice: x: 2, y: 2, z: 4, core: 2. Of those that a mesh axis runs over, the one named last changes fastest.
Arguments:
- inputs: bfloat16 [2, 16384, 768], P(None, ('dp', 'expert')), may hold values from -6 to 6
- gain_one: bfloat16 [768], P('dp'), may hold values from 0.5 to 1.5
- w_qkv: bfloat16 [768, 2304], P('dp'), may hold values from -0.21875 to 0.21875
- w_out: bfloat16 [768, 768], P('dp'), may hold values from -1.75 to 1.75
- rel_table: bfloat16 [32, 12], P('dp'), may hold values from -4 to 4
- second_norm_gain: bfloat16 [768], P('dp'), may hold values from 0.5 to 1.5
- w_router: bfloat16 [768, 8], P('dp'), may hold values from -0.15625 to 0.15625
- w_in: bfloat16 [8, 768, 3072], P('expert'), may hold values from -0.21875 to 0.21875
- w_back: bfloat16 [8, 3072, 768], P('expert'), may hold values from -0.109375 to 0.109375
- expert_ids: int32 [2, 16384, 2], P(None, ('dp', 'expert')), may hold values from 0 to 7, all different within a row; in each aligned block of 512 rows (0 to 511, 512 to 1023, ..., all dimensions but the last counted through in order) at most 192 rows name the same one
- block_ids: int32 [2, 32, 512], P(None, ('dp', 'expert')), may hold values from 0 to 3, never falling along the last dimension, each value on 1 to 256 neighbouring positions
- cotangent: bfloat16 [2, 16384, 768], P(None, ('dp', 'expert')), may hold values from -6 to 6
Outputs:
- out: bfloat16 [2, 16384, 768], P(None, ('dp', 'expert'))
- grad_inputs: bfloat16 [2, 16384, 768], P(None, ('dp', 'expert'))
- grad_gain_one: float32 [768], P('dp')
- grad_w_qkv: float32 [768, 2304], P('dp')
- grad_w_out: float32 [768, 768], P('dp')
- grad_rel_table: float32 [32, 12], P('dp')
- grad_gain_two: float32 [768], P('dp')
- grad_w_router: float32 [768, 8], P('dp')
- grad_w_in: float32 [8, 768, 3072], P('expert')
- grad_w_back: float32 [8, 3072, 768], P('expert')
Inputs may be any that keep to these rules, and one draw needn't show every extreme that they name: `expert_ids`: each token names two different experts; among the tokens of one sequence no expert is named more than 192 times. `block_ids`: along each sequence block ids never fall; each block holds 1 to 256 tokens, one of them exactly 256.
All inputs are finite; a program needn't handle non-finite values.
Results may differ from a plain program's by a relative error of at most 0.02.
Values may be sent and summed in bfloat16 or wider, within the bound.
No kernel may reach another device: no remote copies, remote signals or barrier semaphores. Data moves between devices by JAX's collectives and lax.ppermute only.
A program may use at most 192 MiB of HBM per device.

v0:
```python
import jax
import jax.numpy as jnp
from jax import lax
from jax.sharding import PartitionSpec as P

HEADS = 12
HEAD = 64


epsilon = 1e-06
bucket_edges = (12, 16, 23, 32, 46, 64, 91)
largest_value = lax.Precision.HIGHEST
masked_score = -1e30


def shortened(x):

    def short(part):
        return part.astype(jnp.bfloat16) if part.dtype == jnp.float32 else part

    return jax.tree.map(short, x)


def buckets(offset):
    distance = jnp.abs(offset)
    far_bucket = 8 + sum(
        ((distance >= edge_value).astype(jnp.int32) for edge_value in bucket_edges)
    )
    return jnp.where(distance < 8, distance, far_bucket) + 16 * (offset > 0).astype(jnp.int32)


def rms_norm(values, gain_vector):
    return (
        values
        * lax.rsqrt(jnp.mean(values * values, axis=-1, keepdims=True) + epsilon)
        * gain_vector
    )


def gelu_tanh(values):
    return jax.nn.gelu(values, approximate=True)


def position_bias(first_row, row_count, length, position_bias_lookup):
    query_pos = first_row + lax.broadcasted_iota(jnp.int32, (row_count, length), 0)
    key_pos = lax.broadcasted_iota(jnp.int32, (row_count, length), 1)
    bucket_ids = buckets(key_pos - query_pos)
    levels = lax.broadcasted_iota(jnp.int32, (position_bias_lookup.shape[0], row_count, length), 0)
    expert_indicator = (bucket_ids[None] == levels).astype(position_bias_lookup.dtype)
    return (
        expert_indicator,
        jnp.einsum("mty,md->dty", expert_indicator, position_bias_lookup, precision=largest_value),
    )


def score_block(first_row, query_block, key_rows, query_ids, key_ids, position_bias_lookup):
    row_count = query_block.shape[0]
    length = key_rows.shape[0]
    expert_indicator, bias_block = position_bias(first_row, row_count, length, position_bias_lookup)
    products = jnp.einsum(
        "qhd,khd->hqk",
        query_block.reshape(row_count, HEADS, HEAD),
        key_rows.reshape(length, HEADS, HEAD),
        preferred_element_type=jnp.float32,
    )
    scores = products * HEAD ** (-0.5) + bias_block
    allowed = key_ids[None, :] <= query_ids[:, None]
    return (expert_indicator, jnp.where(allowed[None], scores, masked_score))


def attend(queries, key_rows, values, block_row, position_bias_lookup):
    length = queries.shape[0]
    row_count = min(length, 512)
    block_count = length // row_count
    value_heads = values.reshape(length, HEADS, HEAD)

    def forward_block(block_index):
        first_row = block_index * row_count
        scores = score_block(
            first_row, queries, key_rows, block_row, block_row, position_bias_lookup
        )[1]
        highest_score = jnp.max(scores, axis=-1, keepdims=True)
        exponent = jnp.exp(scores - highest_score)
        row_total = jnp.sum(exponent, axis=-1, keepdims=True)
        weights = (exponent / row_total).astype(jnp.bfloat16)
        mixed_heads = jnp.einsum(
            "hqk,khd->qhd", weights, value_heads, preferred_element_type=jnp.float32
        )
        return (
            mixed_heads.reshape(row_count, -1).astype(jnp.bfloat16),
            (highest_score + jnp.log(row_total))[..., 0],
        )

    mixed_rows, log_total = lax.map(forward_block, jnp.arange(block_count, dtype=jnp.int32))
    return (mixed_rows.reshape(length, -1), log_total)


def attend_back(queries, key_rows, values, block_row, position_bias_lookup, log_total, grad_mixed):
    length = queries.shape[0]
    model_width = queries.shape[1]
    row_count = min(length, 512)
    block_count = length // row_count
    key_heads = key_rows.reshape(length, HEADS, HEAD)
    value_heads = values.reshape(length, HEADS, HEAD)
    score_scale = HEAD ** (-0.5)

    def backward_block(running, pieces):
        grad_keys, grad_values, bias_lookup_gradient = running
        block_index, block_total = pieces
        first_row = block_index * row_count
        grad_block = grad_mixed.reshape(row_count, HEADS, HEAD)
        expert_indicator, scores = score_block(
            first_row, queries, key_rows, block_row, block_row, position_bias_lookup
        )
        probabilities = jnp.exp(scores - block_total[..., None])
        grad_probs = jnp.einsum(
            "qhd,khd->hqk", grad_block, value_heads, preferred_element_type=jnp.float32
        )
        inner_sum = jnp.sum(probabilities * grad_probs, axis=-1, keepdims=True)
        attention_score_gradient = probabilities * (grad_probs - inner_sum)
        bias_lookup_gradient = bias_lookup_gradient + jnp.einsum(
            "jdi,gdi->jg", expert_indicator, attention_score_gradient, precision=largest_value
        )
        low_scores = attention_score_gradient.astype(jnp.bfloat16)
        grad_query = (
            jnp.einsum("hqk,khd->qhd", low_scores, key_heads, preferred_element_type=jnp.float32)
            * score_scale
        )
        key_part = jnp.einsum(
            "hqk,qhd->khd",
            low_scores,
            queries.reshape(row_count, HEADS, HEAD),
            preferred_element_type=jnp.float32,
        )
        value_part = jnp.einsum(
            "hqk,qhd->khd",
            probabilities.astype(jnp.bfloat16),
            grad_block,
            preferred_element_type=jnp.float32,
        )
        grad_keys = grad_keys + key_part.reshape(length, model_width) * score_scale
        grad_values = grad_values + value_part.reshape(length, model_width)
        return (
            (grad_keys, grad_values, bias_lookup_gradient),
            grad_query.reshape(row_count, model_width),
        )

    initial = (
        jnp.zeros((length, model_width), jnp.float32),
        jnp.zeros((length, model_width), jnp.float32),
        jnp.zeros(position_bias_lookup.shape, jnp.float32),
    )
    (grad_keys, grad_values, bias_lookup_gradient), grad_queries = lax.scan(
        backward_block, initial, (jnp.arange(block_count, dtype=jnp.int32), log_total)
    )
    return (grad_queries.reshape(length, model_width), grad_keys, grad_values, bias_lookup_gradient)


def body(
    inputs,
    gain_one,
    w_qkv,
    w_out,
    rel_table,
    second_norm_gain,
    w_router,
    w_in,
    w_back,
    expert_ids,
    block_ids,
    cotangent,
):
    token_count = inputs.shape[1]
    model_width = inputs.shape[2]
    expert_count = w_router.shape[1]
    capacity = 3 * token_count // expert_count
    assign = 2 * token_count
    first_in = w_in[0]
    last_out = w_back[0]

    def placement(route_ids):
        flat_ids = route_ids.reshape(-1)
        expert_indicator = (
            flat_ids[:, None] == lax.broadcasted_iota(jnp.int32, (assign, expert_count), 1)
        ).astype(jnp.int32)
        earlier = jnp.cumsum(expert_indicator, axis=0, dtype=jnp.int32) - expert_indicator
        slot_index = jnp.sum(earlier * expert_indicator, axis=1, dtype=jnp.int32)
        target = flat_ids * capacity + slot_index
        owner_index = (
            jnp.full((expert_count * capacity,), assign, jnp.int32)
            .at[target]
            .set(jnp.arange(assign, dtype=jnp.int32))
        )
        return (target, owner_index < assign, jnp.minimum(owner_index, assign - 1))

    def expert_forward(received):
        source_count, slot_count, _ = received.shape
        flat_rows = received.reshape(-1, model_width)
        up_values = jnp.dot(flat_rows, first_in, preferred_element_type=jnp.float32)
        activated = gelu_tanh(up_values).astype(jnp.bfloat16)
        produced = jnp.dot(activated, last_out, preferred_element_type=jnp.float32).astype(
            jnp.bfloat16
        )
        returned = lax.all_to_all(
            produced.reshape(source_count, slot_count, model_width),
            "expert",
            split_axis=0,
            concat_axis=0,
            tiled=True,
        )
        return (returned, received, up_values.reshape(source_count, slot_count, -1))

    def micro_step(running, micro_batch):
        dense_acc, first_acc, last_acc = running
        x_micro, route_ids, blocks_micro, cot_micro = micro_batch
        gain_a, qkv_weight, out_weight, table_weight, gain_b, router_weight = (
            lax.all_gather(gain_one, "dp", axis=0, tiled=True),
            lax.all_gather(w_qkv, "dp", axis=0, tiled=True),
            lax.all_gather(w_out, "dp", axis=0, tiled=True),
            lax.all_gather(rel_table, "dp", axis=0, tiled=True),
            lax.all_gather(second_norm_gain, "dp", axis=0, tiled=True),
            lax.all_gather(w_router, "dp", axis=0, tiled=True),
        )
        gain_a = gain_a.astype(jnp.float32)
        gain_b = gain_b.astype(jnp.float32)
        position_bias_lookup = table_weight.astype(jnp.float32)
        block_row = blocks_micro[0]
        residual_in = x_micro.astype(jnp.float32)
        normed, pull_one = jax.vjp(rms_norm, residual_in, gain_a)
        normed_low = normed.astype(jnp.bfloat16)
        projected = jnp.dot(normed_low, qkv_weight, preferred_element_type=jnp.float32).astype(
            jnp.bfloat16
        )
        queries = projected[:, :model_width]
        key_rows = projected[:, model_width : 2 * model_width]
        values = projected[:, 2 * model_width :]
        mixed_rows, log_total = attend(queries, key_rows, values, block_row, position_bias_lookup)
        hidden = residual_in + jnp.dot(mixed_rows, out_weight, preferred_element_type=jnp.float32)
        second, pull_two = jax.vjp(rms_norm, hidden, gain_b)
        second_low = second.astype(jnp.bfloat16)
        logits = jnp.dot(second_low, router_weight, preferred_element_type=jnp.float32)
        route_hot = (
            route_ids[:, :, None]
            == lax.broadcasted_iota(jnp.int32, (token_count, 2, expert_count), 2)
        ).astype(jnp.float32)
        chosen = jnp.sum(logits[:, None, :] * route_hot, axis=-1)
        gate_values = jax.nn.softmax(chosen, axis=-1)
        target, filled, picked = placement(route_ids)
        send_rows = jnp.where(
            filled[:, None], second_low[picked // 2], jnp.zeros((), jnp.bfloat16)
        ).reshape(expert_count, capacity, model_width)
        returned, kept_rows, kept_up = expert_forward(
            lax.all_to_all(send_rows, "expert", split_axis=0, concat_axis=0, tiled=True)
        )
        expert_values = (
            returned.reshape(-1, model_width)[target]
            .astype(jnp.float32)
            .reshape(token_count, 2, model_width)
        )
        branch = (
            gate_values[:, 0:1] * expert_values[:, 0] + gate_values[:, 1:2] * expert_values[:, 1]
        )
        result = (hidden + branch).astype(jnp.bfloat16)
        grad_out = cot_micro.astype(jnp.float32)
        grad_gates = jnp.sum(grad_out[:, None, :] * expert_values, axis=-1)
        flat_gates = gate_values.reshape(-1)
        grad_send = (
            jnp.where(filled[:, None], flat_gates[picked][:, None] * grad_out[picked // 2], 0.0)
            .astype(jnp.bfloat16)
            .reshape(expert_count, capacity, model_width)
        )
        grad_recv = lax.all_to_all(grad_send, "expert", split_axis=0, concat_axis=0, tiled=True)
        expert_rows = lax.all_to_all(
            send_rows, "expert", split_axis=0, concat_axis=0, tiled=True
        ).reshape(-1, model_width)
        up_values = jnp.dot(expert_rows, first_in, preferred_element_type=jnp.float32)
        activated, pull_gelu = jax.vjp(gelu_tanh, up_values)
        grad_flat = grad_recv.reshape(-1, model_width)
        grad_last = jnp.einsum(
            "rf,rd->fd",
            activated.astype(jnp.bfloat16),
            grad_flat,
            preferred_element_type=jnp.float32,
        )
        grad_act = jnp.einsum("rd,fd->rf", grad_flat, last_out, preferred_element_type=jnp.float32)
        grad_up = pull_gelu(grad_act)[0].astype(jnp.bfloat16)
        grad_first = jnp.einsum(
            "rd,rf->df", expert_rows, grad_up, preferred_element_type=jnp.float32
        )
        grad_expert_rows = jnp.einsum(
            "rf,df->rd", grad_up, first_in, preferred_element_type=jnp.float32
        ).astype(jnp.bfloat16)
        grad_returned = lax.all_to_all(
            grad_expert_rows.reshape(grad_recv.shape),
            "expert",
            split_axis=0,
            concat_axis=0,
            tiled=True,
        )
        grad_second = jnp.sum(
            grad_returned.reshape(-1, model_width)[target]
            .astype(jnp.float32)
            .reshape(token_count, 2, model_width),
            axis=1,
        )
        grad_chosen = gate_values * (
            grad_gates - jnp.sum(gate_values * grad_gates, axis=-1, keepdims=True)
        )
        router_logit_gradient = jnp.sum(route_hot * grad_chosen[:, :, None], axis=1).astype(
            jnp.bfloat16
        )
        grad_router = jnp.einsum(
            "sd,se->de", second_low, router_logit_gradient, preferred_element_type=jnp.float32
        )
        grad_second = grad_second + jnp.einsum(
            "se,de->sd", router_logit_gradient, router_weight, preferred_element_type=jnp.float32
        )
        grad_hidden_norm, grad_gain_b = pull_two(grad_second)
        grad_hidden = grad_out + grad_hidden_norm
        grad_branch = grad_hidden.astype(jnp.bfloat16)
        grad_out_weight = jnp.einsum(
            "sd,se->de", mixed_rows, grad_branch, preferred_element_type=jnp.float32
        )
        grad_mixed = jnp.einsum(
            "se,de->sd", grad_branch, out_weight, preferred_element_type=jnp.float32
        ).astype(jnp.bfloat16)
        grad_queries, grad_keys, grad_values, bias_lookup_gradient = attend_back(
            queries, key_rows, values, block_row, position_bias_lookup, log_total, grad_mixed
        )
        grad_projected = jnp.concatenate([grad_queries, grad_keys, grad_values], axis=1).astype(
            jnp.bfloat16
        )
        grad_qkv_weight = jnp.einsum(
            "sd,sf->df", normed_low, grad_projected, preferred_element_type=jnp.float32
        )
        grad_normed = jnp.einsum(
            "sf,df->sd", grad_projected, qkv_weight, preferred_element_type=jnp.float32
        )
        grad_input_norm, grad_gain_a = pull_one(grad_normed)
        grad_input = (grad_hidden + grad_input_norm).astype(jnp.bfloat16)
        dense_terms = (
            grad_gain_a,
            grad_qkv_weight,
            grad_out_weight,
            bias_lookup_gradient,
            grad_gain_b,
            grad_router,
        )
        shares = (
            lax.psum_scatter(
                dense_terms[0].astype(jnp.bfloat16), "dp", scatter_dimension=0, tiled=True
            ).astype(jnp.float32),
            lax.psum_scatter(
                dense_terms[1].astype(jnp.bfloat16), "dp", scatter_dimension=0, tiled=True
            ).astype(jnp.float32),
            lax.psum_scatter(
                dense_terms[2].astype(jnp.bfloat16), "dp", scatter_dimension=0, tiled=True
            ).astype(jnp.float32),
            lax.psum_scatter(
                dense_terms[3].astype(jnp.bfloat16), "dp", scatter_dimension=0, tiled=True
            ).astype(jnp.float32),
            lax.psum_scatter(
                dense_terms[4].astype(jnp.bfloat16), "dp", scatter_dimension=0, tiled=True
            ).astype(jnp.float32),
            lax.psum_scatter(
                dense_terms[5].astype(jnp.bfloat16), "dp", scatter_dimension=0, tiled=True
            ).astype(jnp.float32),
        )
        dense_acc = tuple((held + share for held, share in zip(dense_acc, shares)))
        return ((dense_acc, first_acc + grad_first, last_acc + grad_last), (result, grad_input))

    dense_init = tuple(
        (
            jnp.zeros(weight.shape, jnp.float32)
            for weight in (gain_one, w_qkv, w_out, rel_table, second_norm_gain, w_router)
        )
    )
    initial = (
        dense_init,
        jnp.zeros(first_in.shape, jnp.float32),
        jnp.zeros(last_out.shape, jnp.float32),
    )
    (dense_acc, first_acc, last_acc), (results, input_grads) = lax.scan(
        micro_step, initial, (inputs, expert_ids, block_ids, cotangent)
    )
    dense_total = jax.tree.map(
        lambda part: part.astype(jnp.float32), lax.psum(shortened(dense_acc), "expert")
    )
    first_total, last_total = (
        lax.psum(first_acc.astype(jnp.bfloat16), "dp").astype(jnp.float32),
        lax.psum(last_acc.astype(jnp.bfloat16), "dp").astype(jnp.float32),
    )
    return (
        results,
        input_grads,
        dense_total[0],
        dense_total[1],
        dense_total[2],
        dense_total[3],
        dense_total[4],
        dense_total[5],
        first_total[None],
        last_total[None],
    )


def solution(mesh):
    in_specs = (
        P(None, ("dp", "expert"), None),
        P("dp"),
        P("dp", None),
        P("dp", None),
        P("dp", None),
        P("dp"),
        P("dp", None),
        P("expert", None, None),
        P("expert", None, None),
        P(None, ("dp", "expert"), None),
        P(None, ("dp", "expert"), None),
        P(None, ("dp", "expert"), None),
    )
    out_specs = (
        P(None, ("dp", "expert"), None),
        P(None, ("dp", "expert"), None),
        P("dp"),
        P("dp", None),
        P("dp", None),
        P("dp", None),
        P("dp"),
        P("dp", None),
        P("expert", None, None),
        P("expert", None, None),
    )
    return jax.shard_map(body, mesh=mesh, in_specs=in_specs, out_specs=out_specs, check_vma=False)
```

profile of v0, /device:TPU:0, one launch (start us, length us, event | category | flops | bytes accessed | tf_op | source)
XLA Modules:
  0.0 1405.3 jit_solution(13229230267953924810)
XLA Ops:
  8.1 1121.3 %while.30 = (s32[]{:T(128)}, f32[192]{0:T(256)}, f32[192,2304]{1,0:T(8,128)}, f32[192,768]{1,0:T(8,128)}, f32[8,12]{1,0:T(8,128)}, /*index=5*/f32[192]{0:T(256)}...) while((s32[]{:T(128)}, f32[192]{0:T(256)}, ...), condition=%wide.region_27.28_spmd.clone, body=%wide.region_0.27_spmd.clone.sunk | while | flops 54905372672 | bytes 1019100800 | solution.py:383
  44.5 17.8 %copy.158 = f32[512,512,12]{0,1,2:T(8,128)} copy(f32[512,512,12]{1,2,0:T(8,128)} %fusion.232) | data formatting | bytes 25165824 | tf_op jit(solution)/shard_map/while/body/eval_jaxpr/while/body/eval_jaxpr/mty,md->dty/dot_general | solution.py:52
  95.3 60.5 %all_to_all.41 = bf16[8,192,768]{2,1,0:T(8,128)(2,1)S(1)} all-to-all(bf16[8,192,768]{2,1,0:T(8,128)(2,1)S(1)} %broadcast_select_fusion.2), channel_id=1, replica_groups=mesh['dp'=4,'expert'=8] {'expert'}, dimensions={0} | all-to-all | bytes 4718592 | tf_op jit(solution)/shard_map/while/body/eval_jaxpr/all_to_all | solution.py:273
  169.6 15.8 %convolution_convert_fusion.15 = bf16[1536,768]{1,0:T(8,128)(2,1)} fusion(bf16[3072,768]{1,0:T(8,128)(2,1)S(1)} %bitcast.335, f32[1536,3072]{1,0:T(8,128)} %fusion.239), kind=kOutput, calls=%fused_computation.38.clone.1 | convolution fusion | flops 7291404288 | bytes 25952256 | tf_op jit(solution)/shard_map/while/body/eval_jaxpr/dot_general | solution.py:201
  203.0 40.3 %all-to-all-done.1 = bf16[8,192,768]{2,1,0:T(8,128)(2,1)} async-done(((bf16[8,192,768]{2,1,0:T(8,128)(2,1)}), bf16[8,192,768]{2,1,0:T(8,128)(2,1)}, u32[]{:S(2)}, u32[]{:S(2)}) %all-to-all-start.1) | async-done | bytes 2359328 | tf_op jit(solution)/shard_map/while/body/eval_jaxpr/all_to_all | solution.py:204
  268.6 57.6 %all_to_all.42 = bf16[8,192,768]{2,1,0:T(8,128)(2,1)S(1)} all-to-all(bf16[8,192,768]{2,1,0:T(8,128)(2,1)S(1)} %select_convert_fusion.2), channel_id=1, replica_groups=mesh['dp'=4,'expert'=8] {'expert'}, dimensions={0} | all-to-all | bytes 4718592 | tf_op jit(solution)/shard_map/while/body/eval_jaxpr/all_to_all | solution.py:272
  326.2 22.2 %fusion.242 = bf16[1536,3072]{1,0:T(8,128)(2,1)S(1)} fusion(f32[1536,3072]{1,0:T(8,128)} %fusion.239, bf16[1536,768]{1,0:T(8,128)(2,1)S(1)} %bitcast.312, bf16[3072,768]{1,0:T(8,128)(2,1)} %get-tuple-element.926), kind=kOutput, calls=%fused_computation.17.clone.1 | convolution fusion | flops 7342129152 | bytes 35389440 | tf_op jit(solution)/shard_map/while/body/eval_jaxpr/rd,fd->rf/dot_general | solution.py:285
  385.4 29.0 %all-to-all-done.3 = bf16[8,192,768]{2,1,0:T(8,128)(2,1)S(1)} async-done(((bf16[8,192,768]{2,1,0:T(8,128)(2,1)}), bf16[8,192,768]{2,1,0:T(8,128)(2,1)S(1)}, u32[]{:S(2)}, u32[]{:S(2)}) %all-to-all-start.3) | async-done | bytes 2359328 | tf_op jit(solution)/shard_map/while/body/eval_jaxpr/all_to_all | solution.py:293
  490.0 16.8 %select_add_fusion.21 = f32[3072,768]{1,0:T(8,128)} fusion(f32[3072,768]{1,0:T(8,128)} %get-tuple-element.878, bf16[1536,768]{1,0:T(8,128)(2,1)S(1)} %bitcast.313, pred[]{:T(512)S(6)} %compare.7, f32[1536,3072]{1,0:T(8,128)} %fusion.239), kind=kOutput, calls=%fused_computation.30.clone.1 | convolution fusion | flops 7294943232 | bytes 40108032 | tf_op jit(solution)/shard_map/while/body/eval_jaxpr/rf,rd->fd/dot_general | solution.py:279
  506.8 18.6 %copy.167 = f32[12,512,512]{2,0,1:T(8,128)} copy(f32[12,512,512]{1,2,0:T(8,128)} %copy-done.1) | data formatting | bytes 25165824 | tf_op jit(solution)/shard_map/while/body/eval_jaxpr/while/body/eval_jaxpr/mul | solution.py:120
  533.3 17.7 %fusion.246 = bf16[32,12]{1,0:T(8,128)(2,1)S(1)} fusion(f32[12,512,512]{2,0,1:T(8,128)S(1)} %copy-done.2, s32[512,512]{1,0:T(8,128)S(1)} %copy-done.7), kind=kOutput, calls=%fused_computation.85.clone.1 | convolution fusion | flops 1216348544 | bytes 13632256 | tf_op jit(solution)/shard_map/while/body/eval_jaxpr/while/body/eval_jaxpr/jdi,gdi->jg/dot_general | solution.py:121
  602.3 17.8 %copy.158 = f32[512,512,12]{0,1,2:T(8,128)} copy(f32[512,512,12]{1,2,0:T(8,128)} %fusion.232) | data formatting | bytes 25165824 | tf_op jit(solution)/shard_map/while/body/eval_jaxpr/while/body/eval_jaxpr/mty,md->dty/dot_general | solution.py:52
  653.1 57.9 %all_to_all.41 = bf16[8,192,768]{2,1,0:T(8,128)(2,1)S(1)} all-to-all(bf16[8,192,768]{2,1,0:T(8,128)(2,1)S(1)} %broadcast_select_fusion.2), channel_id=1, replica_groups=mesh['dp'=4,'expert'=8] {'expert'}, dimensions={0} | all-to-all | bytes 4718592 | tf_op jit(solution)/shard_map/while/body/eval_jaxpr/all_to_all | solution.py:273
  724.8 15.8 %convolution_convert_fusion.15 = bf16[1536,768]{1,0:T(8,128)(2,1)} fusion(bf16[3072,768]{1,0:T(8,128)(2,1)S(1)} %bitcast.335, f32[1536,3072]{1,0:T(8,128)} %fusion.239), kind=kOutput, calls=%fused_computation.38.clone.1 | convolution fusion | flops 7291404288 | bytes 25952256 | tf_op jit(solution)/shard_map/while/body/eval_jaxpr/dot_general | solution.py:201
  757.8 40.8 %all-to-all-done.1 = bf16[8,192,768]{2,1,0:T(8,128)(2,1)} async-done(((bf16[8,192,768]{2,1,0:T(8,128)(2,1)}), bf16[8,192,768]{2,1,0:T(8,128)(2,1)}, u32[]{:S(2)}, u32[]{:S(2)}) %all-to-all-start.1) | async-done | bytes 2359328 | tf_op jit(solution)/shard_map/while/body/eval_jaxpr/all_to_all | solution.py:204
  823.8 57.6 %all_to_all.42 = bf16[8,192,768]{2,1,0:T(8,128)(2,1)S(1)} all-to-all(bf16[8,192,768]{2,1,0:T(8,128)(2,1)S(1)} %select_convert_fusion.2), channel_id=1, replica_groups=mesh['dp'=4,'expert'=8] {'expert'}, dimensions={0} | all-to-all | bytes 4718592 | tf_op jit(solution)/shard_map/while/body/eval_jaxpr/all_to_all | solution.py:272
  881.4 22.2 %fusion.242 = bf16[1536,3072]{1,0:T(8,128)(2,1)S(1)} fusion(f32[1536,3072]{1,0:T(8,128)} %fusion.239, bf16[1536,768]{1,0:T(8,128)(2,1)S(1)} %bitcast.312, bf16[3072,768]{1,0:T(8,128)(2,1)} %get-tuple-element.926), kind=kOutput, calls=%fused_computation.17.clone.1 | convolution fusion | flops 7342129152 | bytes 35389440 | tf_op jit(solution)/shard_map/while/body/eval_jaxpr/rd,fd->rf/dot_general | solution.py:285
  941.6 28.1 %all-to-all-done.3 = bf16[8,192,768]{2,1,0:T(8,128)(2,1)S(1)} async-done(((bf16[8,192,768]{2,1,0:T(8,128)(2,1)}), bf16[8,192,768]{2,1,0:T(8,128)(2,1)S(1)}, u32[]{:S(2)}, u32[]{:S(2)}) %all-to-all-start.3) | async-done | bytes 2359328 | tf_op jit(solution)/shard_map/while/body/eval_jaxpr/all_to_all | solution.py:293
  1046.0 18.2 %select_add_fusion.21 = f32[3072,768]{1,0:T(8,128)} fusion(f32[3072,768]{1,0:T(8,128)} %get-tuple-element.878, bf16[1536,768]{1,0:T(8,128)(2,1)S(1)} %bitcast.313, pred[]{:T(512)S(6)} %compare.7, f32[1536,3072]{1,0:T(8,128)} %fusion.239), kind=kOutput, calls=%fused_computation.30.clone.1 | convolution fusion | flops 7294943232 | bytes 40108032 | tf_op jit(solution)/shard_map/while/body/eval_jaxpr/rf,rd->fd/dot_general | solution.py:279
  1064.2 18.6 %copy.167 = f32[12,512,512]{2,0,1:T(8,128)} copy(f32[12,512,512]{1,2,0:T(8,128)} %copy-done.1) | data formatting | bytes 25165824 | tf_op jit(solution)/shard_map/while/body/eval_jaxpr/while/body/eval_jaxpr/mul | solution.py:120
  1090.6 17.9 %fusion.246 = bf16[32,12]{1,0:T(8,128)(2,1)S(1)} fusion(f32[12,512,512]{2,0,1:T(8,128)S(1)} %copy-done.2, s32[512,512]{1,0:T(8,128)S(1)} %copy-done.7), kind=kOutput, calls=%fused_computation.85.clone.1 | convolution fusion | flops 1216348544 | bytes 13632256 | tf_op jit(solution)/shard_map/while/body/eval_jaxpr/while/body/eval_jaxpr/jdi,gdi->jg/dot_general | solution.py:121
  1145.6 20.5 %all-reduce.9 = (bf16[192]{0:T(256)(128)(2,1)S(1)}, bf16[8,12]{1,0:T(8,128)(2,1)S(1)}, bf16[192]{0:T(256)(128)(2,1)S(1)}, bf16[192,8]{0,1:T(8,128)(2,1)S(1)}) all-reduce(bf16[192]{0:T(256)(128)(2,1)S(1)} %convert_element_type.426, bf16[8,12]{1,0:T(8,128)(2,1)S(1)} %convert_element_type.432, ...), channel_id=1, replica_groups=mesh['dp'=4,'expert'=8] {'expert'}, use_global_device_ids=true, to_apply=%region_28.29 | all-reduce | flops 2016 | bytes 8064 | tf_op jit(solution)/shard_map/psum | solution.py:387
  1168.4 44.8 %all-reduce.19.cloned.1.call-done = (bf16[192,2304]{1,0:T(8,128)(2,1)}, bf16[192,768]{1,0:T(8,128)(2,1)}) async-done(((bf16[192,2304]{1,0:T(8,128)(2,1)}, bf16[192,768]{1,0:T(8,128)(2,1)}), (bf16[192,2304]{1,0:T(8,128)(2,1)}, bf16[192,768]{1,0:T(8,128)(2,1)})) %all-reduce.19.cloned.1.call-update) | async-done | bytes 1179664 | tf_op jit(solution)/shard_map/psum | solution.py:387
  1217.6 168.1 %all-reduce.21.cloned.1.call-done = (bf16[1,768,3072]{2,1,0:T(8,128)(2,1)}, bf16[1,3072,768]{2,1,0:T(8,128)(2,1)}) async-done(((bf16[1,768,3072]{2,1,0:T(8,128)(2,1)}, bf16[1,3072,768]{2,1,0:T(8,128)(2,1)}), (bf16[1,768,3072]{2,1,0:T(8,128)(2,1)}, bf16[1,3072,768]{2,1,0:T(8,128)(2,1)})) %all-reduce.21.cloned.1.call-update) | async-done | bytes 9437200 | tf_op jit(solution)/shard_map/psum | solution.py:390
  (538 shorter events, 555.4 us)
Async XLA Ops:
  8.4 53.9 %all-gather.7.cloned.1.call-start = ((), (), s32[]{:S(2)}) async-start(), calls=%async_computation.9 | async-start | bytes 4423680 | tf_op jit(solution)/shard_map/while/body/eval_jaxpr/all_gather | solution.py:218
  9.1 77.0 %all-gather.9.cloned.1.call-start = ((), (), s32[]{:S(2)}) async-start(), calls=%async_computation.10 | async-start | bytes 1474560 | tf_op jit(solution)/shard_map/while/body/eval_jaxpr/all_gather | solution.py:219
  19.4 43.0 %copy-start.44 = (f32[512]{0:T(512)}, f32[512]{0:T(512)S(1)}, u32[]{:S(2)}) copy-start(f32[512]{0:T(512)S(1)} %fusion.229) | copy-start | bytes 6148 | tf_op jit(solution)/shard_map/while
  95.3 74.3 %slice-start.3 = ((s8[4718592]{0:T(1024)(128)(4,1)}), s8[4194304]{0:T(1024)(128)(4,1)S(1)}, s32[]{:S(2)}) async-start(s8[4718592]{0:T(1024)(128)(4,1)} %bitcast.334), calls=%async_computation.17 | async-start | bytes 8388608 | tf_op jit(solution)/shard_map/while
  185.4 58.0 %all-to-all-start.1 = ((bf16[8,192,768]{2,1,0:T(8,128)(2,1)}), bf16[8,192,768]{2,1,0:T(8,128)(2,1)}, u32[]{:S(2)}, u32[]{:S(2)}) async-start(bf16[8,192,768]{2,1,0:T(8,128)(2,1)} %bitcast.282), calls=%async_computation.1 | async-start | bytes 4718592 | tf_op jit(solution)/shard_map/while/body/eval_jaxpr/all_to_all | solution.py:204
  265.7 82.7 %slice-start.5 = ((s8[4718592]{0:T(1024)(128)(4,1)}), s8[4194304]{0:T(1024)(128)(4,1)S(1)}, s32[]{:S(2)}) async-start(s8[4718592]{0:T(1024)(128)(4,1)} %bitcast.337), calls=%async_computation.19 | async-start | bytes 8388608 | tf_op jit(solution)/shard_map/while
  357.2 57.1 %all-to-all-start.3 = ((bf16[8,192,768]{2,1,0:T(8,128)(2,1)}), bf16[8,192,768]{2,1,0:T(8,128)(2,1)S(1)}, u32[]{:S(2)}, u32[]{:S(2)}) async-start(bf16[8,192,768]{2,1,0:T(8,128)(2,1)} %bitcast.314), calls=%async_computation.3 | async-start | bytes 4718592 | tf_op jit(solution)/shard_map/while/body/eval_jaxpr/all_to_all | solution.py:293
  360.9 23.6 %reduce-scatter.12.cloned.1.call-start = ((), (), s32[]{:S(2)}) async-start(), calls=%async_computation.13 | async-start | bytes 245760 | tf_op jit(solution)/shard_map/while
  363.5 201.0 %reduce-scatter.10.cloned.1.call-start = ((), (), s32[]{:S(2)}) async-start(), calls=%async_computation.12 | async-start | bytes 1474560 | tf_op jit(solution)/shard_map/while/body/eval_jaxpr/reduce_scatter | solution.py:356
  385.4 34.2 %copy-start.42 = (f32[192,8]{0,1:T(8,128)}, f32[192,8]{0,1:T(8,128)S(1)}, u32[]{:S(2)}) copy-start(f32[192,8]{0,1:T(8,128)S(1)} %select_add_fusion.19) | copy-start | bytes 18436 | tf_op jit(solution)/shard_map/while
  438.5 127.1 %reduce-scatter.8.cloned.1.call-start = ((), (), s32[]{:S(2)}) async-start(), calls=%async_computation.11 | async-start | bytes 4423680 | tf_op jit(solution)/shard_map/while/body/eval_jaxpr/reduce_scatter | solution.py:353
  568.7 51.3 %all-gather.7.cloned.1.call-start = ((), (), s32[]{:S(2)}) async-start(), calls=%async_computation.9 | async-start | bytes 4423680 | tf_op jit(solution)/shard_map/while/body/eval_jaxpr/all_gather | solution.py:218
  569.3 74.7 %all-gather.9.cloned.1.call-start = ((), (), s32[]{:S(2)}) async-start(), calls=%async_computation.10 | async-start | bytes 1474560 | tf_op jit(solution)/shard_map/while/body/eval_jaxpr/all_gather | solution.py:219
  579.5 40.5 %copy-start.44 = (f32[512]{0:T(512)}, f32[512]{0:T(512)S(1)}, u32[]{:S(2)}) copy-start(f32[512]{0:T(512)S(1)} %fusion.229) | copy-start | bytes 6148 | tf_op jit(solution)/shard_map/while
  653.1 71.6 %slice-start.3 = ((s8[4718592]{0:T(1024)(128)(4,1)}), s8[4194304]{0:T(1024)(128)(4,1)S(1)}, s32[]{:S(2)}) async-start(s8[4718592]{0:T(1024)(128)(4,1)} %bitcast.334), calls=%async_computation.17 | async-start | bytes 8388608 | tf_op jit(solution)/shard_map/while
  740.6 58.0 %all-to-all-start.1 = ((bf16[8,192,768]{2,1,0:T(8,128)(2,1)}), bf16[8,192,768]{2,1,0:T(8,128)(2,1)}, u32[]{:S(2)}, u32[]{:S(2)}) async-start(bf16[8,192,768]{2,1,0:T(8,128)(2,1)} %bitcast.282), calls=%async_computation.1 | async-start | bytes 4718592 | tf_op jit(solution)/shard_map/while/body/eval_jaxpr/all_to_all | solution.py:204
  820.9 82.8 %slice-start.5 = ((s8[4718592]{0:T(1024)(128)(4,1)}), s8[4194304]{0:T(1024)(128)(4,1)S(1)}, s32[]{:S(2)}) async-start(s8[4718592]{0:T(1024)(128)(4,1)} %bitcast.337), calls=%async_computation.19 | async-start | bytes 8388608 | tf_op jit(solution)/shard_map/while
  912.5 57.1 %all-to-all-start.3 = ((bf16[8,192,768]{2,1,0:T(8,128)(2,1)}), bf16[8,192,768]{2,1,0:T(8,128)(2,1)S(1)}, u32[]{:S(2)}, u32[]{:S(2)}) async-start(bf16[8,192,768]{2,1,0:T(8,128)(2,1)} %bitcast.314), calls=%async_computation.3 | async-start | bytes 4718592 | tf_op jit(solution)/shard_map/while/body/eval_jaxpr/all_to_all | solution.py:293
  916.2 24.5 %reduce-scatter.12.cloned.1.call-start = ((), (), s32[]{:S(2)}) async-start(), calls=%async_computation.13 | async-start | bytes 245760 | tf_op jit(solution)/shard_map/while
  918.7 203.1 %reduce-scatter.10.cloned.1.call-start = ((), (), s32[]{:S(2)}) async-start(), calls=%async_computation.12 | async-start | bytes 1474560 | tf_op jit(solution)/shard_map/while/body/eval_jaxpr/reduce_scatter | solution.py:356
  941.6 33.3 %copy-start.42 = (f32[192,8]{0,1:T(8,128)}, f32[192,8]{0,1:T(8,128)S(1)}, u32[]{:S(2)}) copy-start(f32[192,8]{0,1:T(8,128)S(1)} %select_add_fusion.19) | copy-start | bytes 18436 | tf_op jit(solution)/shard_map/while
  993.8 129.2 %reduce-scatter.8.cloned.1.call-start = ((), (), s32[]{:S(2)}) async-start(), calls=%async_computation.11 | async-start | bytes 4423680 | tf_op jit(solution)/shard_map/while/body/eval_jaxpr/reduce_scatter | solution.py:353
  1129.4 83.9 %all-reduce.19.cloned.1.call-start = ((), (), s32[]{:S(2)}) async-start(), calls=%async_computation.7 | async-start | bytes 2359296 | tf_op jit(solution)/shard_map/psum | solution.py:387
  1133.8 251.8 %all-reduce.21.cloned.1.call-start = ((), (), s32[]{:S(2)}) async-start(), calls=%async_computation.8 | async-start | bytes 18874368 | tf_op jit(solution)/shard_map/psum | solution.py:390
  (122 other events, 1316.2 us)
Sparse Core Ops, SparseCore 0:
  10.9 33.6 all-gather.6
  46.2 17.4 all-gather.8
  364.3 20.1 reduce-scatter.11
  438.7 23.8 reduce-scatter.9
  473.9 38.2 reduce-scatter.7
  570.9 29.7 all-gather.6
  602.4 17.4 all-gather.8
  919.6 21.0 reduce-scatter.11
  993.9 24.6 reduce-scatter.9
  1028.8 39.3 reduce-scatter.7
Sparse Core Ops, SparseCore 1:
  1133.9 79.3 all-reduce.18
  1216.5 169.1 all-reduce.20
where the time goes:
time: 1410 us
  waiting for transfers between devices  382 us (27%)
  matrix products  350 us (25%)
  blocking collectives  310 us (22%)
  local copies, waits for them, and re-layouts  215 us (15%)
  other arithmetic  104 us (7%)
  starting transfers between devices  18.1 us (1%)
  between operations  15.8 us (1%)
    psum x1, waiting for transfers between devices, body(): lax.psum(first_acc.astype(jnp.bfloat16), 'dp').astype(jnp.float32)  168 us
    all_to_all x2, blocking collectives, micro_step(): lax.all_to_all(send_rows, 'expert', split_axis=0, concat_axis=0, tiled=True)  118 us
    all_to_all x2, blocking collectives, micro_step(): lax.all_to_all(grad_send, 'expert', split_axis=0, concat_axis=0, tiled=True)  115 us
    all_to_all x2, waiting for transfers between devices, expert_forward(): lax.all_to_all(produced.reshape(source_count, slot_count, model_width), '...  81.1 us
    all_to_all x2, waiting for transfers between devices, micro_step(): lax.all_to_all(grad_expert_rows.reshape(grad_recv.shape), 'expert', split...  57 us
    psum x1, waiting for transfers between devices, body(): lax.psum(shortened(dense_acc), 'expert')  44.8 us
    dot_general x2, matrix products, micro_step(): jnp.einsum('rd,fd->rf', grad_flat, last_out, preferred_element_type=jnp.f...  44.5 us
    mul x2, local copies, waits for them, and re-layouts, backward_block(): attention_score_gradient = probabilities * (grad_probs - inner_sum)  37.2 us
  transfers between devices with their start and end apart: 16, of which 8 were waited for; matrix products, arithmetic and copies ran while one was open for 27% of the time, Pallas kernels for 0%

commit v1 on v0

v1 whole, which is shorter than its diff:
```python
import functools

import jax
import jax.numpy as jnp
import numpy as np
from jax import lax
from jax.experimental import pallas as pl
from jax.experimental.pallas import tpu as pltpu
from jax.sharding import PartitionSpec as P

HEAD = 64
PAIR = 2 * HEAD
STRIP = 128
LANES = 128
VMEM_BYTES = 60 * 1024 * 1024

epsilon = 1e-06
bucket_edges = (12, 16, 23, 32, 46, 64, 91)
masked_score = -1e30
gelu_a = float(np.sqrt(2.0 / np.pi))
gelu_b = 0.044715

F32 = jnp.float32
BF16 = jnp.bfloat16


def dot(a, b):
    return jnp.dot(a, b, preferred_element_type=F32)


def dot_nt(a, b):
    return lax.dot_general(a, b, (((1,), (1,)), ((), ())), preferred_element_type=F32)


def dot_tn(a, b):
    return lax.dot_general(a, b, (((0,), (0,)), ((), ())), preferred_element_type=F32)


def iota(shape, dim):
    return lax.broadcasted_iota(jnp.int32, shape, dim)


def hot(mask):
    return jnp.where(mask, 1.0, 0.0).astype(BF16)


def params(**extra):
    return pltpu.CompilerParams(vmem_limit_bytes=VMEM_BYTES, **extra)


def bucket_table(length, buckets):
    offset = np.arange(2 * length) - (length - 1)
    distance = np.abs(offset)
    far = 8 + sum((distance >= edge).astype(np.int32) for edge in bucket_edges)
    bucket = np.where(distance < 8, distance, far) + 16 * (offset > 0)
    table = (bucket[None, :] == np.arange(buckets)[:, None]) & (offset < length)[None, :]
    return table.astype(np.float32)


def strip_kernel(base_ref, out_ref):
    heads, width = base_ref.shape
    for h in range(heads):
        row = jnp.broadcast_to(base_ref[h : h + 1, :], (STRIP, width))
        rolled = pltpu.roll(row, width - (STRIP - 1), 1, stride=1, stride_axis=0)
        out_ref[h] = rolled[:, : width - STRIP].astype(BF16)


def dispatch_kernel(experts, capacity, ids_row_ref, ids_col_ref, cot_ref, row_ref, col_ref, send_ref):
    length = cot_ref.shape[0]
    padded = max(16, experts)
    before = hot(iota((length, length), 0) < iota((length, length), 1))
    level = iota((padded, length), 0)
    first, second = ids_row_ref[0:1, :], ids_row_ref[1:2, :]
    place = dot(hot((level == first) | (level == second)), before).astype(jnp.int32)
    slot = place + level * capacity
    row_first = jnp.sum(jnp.where(level == first, slot, 0), axis=0, keepdims=True)
    row_second = jnp.sum(jnp.where(level == second, slot, 0), axis=0, keepdims=True)
    row_ref[0:1, :] = row_first
    row_ref[1:2, :] = row_second

    after = hot(iota((length, length), 1) < iota((length, length), 0))
    level = iota((length, LANES), 1)
    first, second = ids_col_ref[:, 0:1], ids_col_ref[:, 1:2]
    place = dot(after, hot((level == first) | (level == second)))
    slot = place + (level * capacity).astype(F32)
    col_ref[:, 0:1] = jnp.sum(jnp.where(level == first, slot, 0.0), axis=1, keepdims=True).astype(jnp.int32)
    col_ref[:, 1:2] = jnp.sum(jnp.where(level == second, slot, 0.0), axis=1, keepdims=True).astype(jnp.int32)
    scatter_rows(row_first, row_second, cot_ref[...], send_ref)


def scatter_rows(row_first, row_second, values, send_ref):
    total, length = send_ref.shape[0], values.shape[0]
    step = 256
    for start in range(0, total, step):
        slots = iota((step, length), 0) + start
        pick = hot((slots == row_first) | (slots == row_second))
        send_ref[start : start + step, :] = dot(pick, values).astype(BF16)


def fill_pick(col_ref, pick_ref):
    length, total = pick_ref.shape
    first, second = col_ref[:, 0:1], col_ref[:, 1:2]
    step = 256
    for start in range(0, total, step):
        slots = iota((length, step), 1) + start
        pick_ref[:, start : start + step] = hot((slots == first) | (slots == second))


def head_mask(length):
    return iota((length, PAIR), 1) < HEAD


def forward_kernel(
    x_ref, gains_ref, weight_ref, strip_ref, block_row_ref, block_col_ref, row_ref,
    proj_ref, mixed_ref, total_ref, hidden_ref, send_ref,
):
    length, width = x_ref.shape
    scale = HEAD ** (-0.5)
    x = x_ref[...].astype(F32)
    r1 = lax.rsqrt(jnp.mean(x * x, axis=1, keepdims=True) + epsilon)
    normed = (x * r1 * gains_ref[0:1, :]).astype(BF16)
    proj_ref[...] = dot(normed, weight_ref[:, : 3 * width]).astype(BF16)

    def pair(p, carry):
        lanes = pl.multiple_of(p * PAIR, PAIR)
        q = proj_ref[:, pl.ds(lanes, PAIR)]
        k = proj_ref[:, pl.ds(width + lanes, PAIR)]
        v = proj_ref[:, pl.ds(2 * width + lanes, PAIR)]
        left = head_mask(length)
        zero = jnp.zeros_like(k)
        outs = [None] * (length // STRIP)
        for h in range(2):
            keep = left if h == 0 else jnp.logical_not(left)
            kh = jnp.where(keep, k, zero)
            vh = jnp.where(keep, v, zero)
            strip = strip_ref[2 * p + h].astype(F32)
            for i in range(length // STRIP):
                rows = slice(i * STRIP, (i + 1) * STRIP)
                start = length - STRIP - i * STRIP
                s = dot_nt(q[rows], kh) * scale + strip[:, start : start + length]
                s = jnp.where(block_row_ref[...] <= block_col_ref[rows, :], s, masked_score)
                top = jnp.max(s, axis=1, keepdims=True)
                e = jnp.exp(s - top)
                total = jnp.sum(e, axis=1, keepdims=True)
                weights = (e * (1.0 / total)).astype(BF16)
                total_ref[2 * p + h, rows, :] = top + jnp.log(total)
                part = dot(weights, vh)
                outs[i] = part if outs[i] is None else outs[i] + part
        for i, part in enumerate(outs):
            mixed_ref[i * STRIP : (i + 1) * STRIP, pl.ds(lanes, PAIR)] = part.astype(BF16)
        return carry

    lax.fori_loop(0, width // PAIR, pair, 0)
    hidden = x + dot(mixed_ref[...], weight_ref[:, 3 * width : 4 * width])
    hidden_ref[...] = hidden
    r2 = lax.rsqrt(jnp.mean(hidden * hidden, axis=1, keepdims=True) + epsilon)
    second = (hidden * r2 * gains_ref[1:2, :]).astype(BF16)
    scatter_rows(row_ref[0:1, :], row_ref[1:2, :], second, send_ref)


def backward_kernel(
    back_ref, col_ref, cot_ref, hidden_ref, gains_ref, weight_ref, proj_ref, total_ref, strip_ref,
    block_row_ref, block_col_ref, x_ref,
    grad_x_ref, branch_ref, grad_proj_ref, normed_ref, grad_gain_ref, diagonal_ref,
    pick_ref, grad_mixed_ref, low_ref, prob_ref, strip_sum_ref,
):
    length, width = cot_ref.shape
    scale = HEAD ** (-0.5)
    fill_pick(col_ref, pick_ref)
    grad_second = dot(pick_ref[...], back_ref[...])
    hidden = hidden_ref[...]
    r2 = lax.rsqrt(jnp.mean(hidden * hidden, axis=1, keepdims=True) + epsilon)
    scaled = grad_second * gains_ref[1:2, :]
    inner = jnp.mean(hidden * scaled, axis=1, keepdims=True)
    grad_hidden = cot_ref[...].astype(F32) + r2 * scaled - hidden * (r2 * r2 * r2 * inner)
    grad_gain_ref[1:2, :] = jnp.sum(grad_second * hidden * r2, axis=0, keepdims=True)
    branch = grad_hidden.astype(BF16)
    branch_ref[...] = branch
    grad_mixed_ref[...] = dot_nt(branch, weight_ref[:, 3 * width : 4 * width]).astype(BF16)

    def pair(p, carry):
        lanes = pl.multiple_of(p * PAIR, PAIR)
        q = proj_ref[:, pl.ds(lanes, PAIR)]
        k = proj_ref[:, pl.ds(width + lanes, PAIR)]
        v = proj_ref[:, pl.ds(2 * width + lanes, PAIR)]
        g = grad_mixed_ref[:, pl.ds(lanes, PAIR)]
        q_turned = q.astype(F32).T.astype(BF16)
        g_turned = g.astype(F32).T.astype(BF16)
        left = head_mask(length)
        zero = jnp.zeros_like(k)
        outs = [None] * (length // STRIP)
        keys, values = [], []
        for h in range(2):
            keep = left if h == 0 else jnp.logical_not(left)
            kh = jnp.where(keep, k, zero)
            vh = jnp.where(keep, v, zero)
            strip = strip_ref[2 * p + h].astype(F32)
            strip_sum_ref[...] = jnp.zeros_like(strip_sum_ref)
            for i in range(length // STRIP):
                rows = slice(i * STRIP, (i + 1) * STRIP)
                start = length - STRIP - i * STRIP
                s = dot_nt(q[rows], kh) * scale + strip[:, start : start + length]
                s = jnp.where(block_row_ref[...] <= block_col_ref[rows, :], s, masked_score)
                prob = jnp.exp(s - total_ref[2 * p + h, rows, :])
                grad_prob = dot_nt(g[rows], vh)
                row_inner = jnp.sum(prob * grad_prob, axis=1, keepdims=True)
                grad_score = prob * (grad_prob - row_inner)
                strip_sum_ref[:, start : start + length] += grad_score
                low = grad_score.astype(BF16)
                low_ref[rows, :] = low
                prob_ref[rows, :] = prob.astype(BF16)
                part = dot(low, kh)
                outs[i] = part if outs[i] is None else outs[i] + part
            half = slice(h * HEAD, (h + 1) * HEAD)
            keys.append(dot(q_turned[half], low_ref[...]))
            values.append(dot(g_turned[half], prob_ref[...]))
            gathered = jnp.zeros((8, 2 * length), F32)
            for a in range(STRIP // 8):
                piece = strip_sum_ref[8 * a : 8 * a + 8, :]
                gathered += pltpu.roll(piece, STRIP - 8 - 8 * a, 1) if a < STRIP // 8 - 1 else piece
            line = gathered[7:8]
            for b in range(7):
                line += pltpu.roll(gathered[b : b + 1], 7 - b, 1)
            diagonal_ref[pl.ds(2 * p + h, 1), :] = line
        for i, part in enumerate(outs):
            grad_proj_ref[i * STRIP : (i + 1) * STRIP, pl.ds(lanes, PAIR)] = (part * scale).astype(BF16)
        grad_key = jnp.concatenate(keys, axis=0).T
        grad_value = jnp.concatenate(values, axis=0).T
        grad_proj_ref[:, pl.ds(width + lanes, PAIR)] = (grad_key * scale).astype(BF16)
        grad_proj_ref[:, pl.ds(2 * width + lanes, PAIR)] = grad_value.astype(BF16)
        return carry

    lax.fori_loop(0, width // PAIR, pair, 0)
    x = x_ref[...].astype(F32)
    r1 = lax.rsqrt(jnp.mean(x * x, axis=1, keepdims=True) + epsilon)
    normed_ref[...] = (x * r1 * gains_ref[0:1, :]).astype(BF16)
    grad_normed = dot_nt(grad_proj_ref[...], weight_ref[:, : 3 * width])
    scaled = grad_normed * gains_ref[0:1, :]
    inner = jnp.mean(x * scaled, axis=1, keepdims=True)
    grad_gain_ref[0:1, :] = jnp.sum(grad_normed * x * r1, axis=0, keepdims=True)
    grad_x_ref[...] = (grad_hidden + r1 * scaled - x * (r1 * r1 * r1 * inner)).astype(BF16)


def expert_kernel(
    rows_ref, cot_ref, ids_ref, mine_ref, router_ref, router_turned_ref, first_ref, last_ref,
    out_ref, back_ref, act_ref, grad_up_ref, scaled_ref, grad_router_ref,
    gate_ref, other_ref, out_acc, back_acc,
):
    step = pl.program_id(0)
    total = rows_ref.shape[0]
    sources, length = ids_ref.shape[1], ids_ref.shape[2]
    capacity = total // sources
    mine = mine_ref[0, 0]
    tile = 512

    @pl.when(step == 0)
    def _():
        first, second = ids_ref[0], ids_ref[1]
        named = (first == mine) | (second == mine)
        before = hot(iota((length, length), 0) < iota((length, length), 1))
        place = dot(hot(named), before).astype(jnp.int32)
        slot = jnp.where(named, place, -1)
        partner = jnp.where(first == mine, second, first).astype(F32)
        for s in range(sources):
            here = iota((capacity, length), 0) == slot[s : s + 1, :]
            other_ref[s * capacity : (s + 1) * capacity, :] = jnp.sum(
                jnp.where(here, partner[s : s + 1, :], 0.0), axis=1, keepdims=True
            ).astype(jnp.int32)
        lane = iota((total, LANES), 1)
        logits = dot(rows_ref[...], router_ref[...])
        gap = jnp.sum(
            jnp.where(lane == mine, logits, 0.0) - jnp.where(lane == other_ref[...], logits, 0.0),
            axis=1, keepdims=True,
        )
        small = jnp.exp(-jnp.abs(gap))
        gate = jnp.where(gap >= 0, 1.0, small) / (1.0 + small)
        gate_ref[...] = gate
        scaled_ref[...] = (gate * cot_ref[...].astype(F32)).astype(BF16)

    first_weight, last_weight = first_ref[...], last_ref[...]

    def row_tile(t, carry):
        at = pl.ds(pl.multiple_of(t * tile, tile), tile)
        rows = rows_ref[at, :]
        scaled = scaled_ref[at, :]
        up = dot(rows, first_weight)
        grad_act = dot_nt(scaled, last_weight)
        square = up * up
        half = 0.5 * jnp.tanh(up * (gelu_a + (gelu_a * gelu_b) * square)) + 0.5
        act = up * half
        slope = half + (act * (1.0 - half)) * (2 * gelu_a + (6 * gelu_a * gelu_b) * square)
        act_low = act.astype(BF16)
        grad_up = (grad_act * slope).astype(BF16)
        act_ref[at, :] = act_low
        grad_up_ref[at, :] = grad_up
        out_part = dot(act_low, last_weight)
        back_part = dot_nt(grad_up, first_weight)

        @pl.when(step == 0)
        def _():
            out_acc[at, :] = out_part
            back_acc[at, :] = back_part

        @pl.when(step > 0)
        def _():
            out_acc[at, :] += out_part
            back_acc[at, :] += back_part

        return carry

    lax.fori_loop(0, total // tile, row_tile, 0)

    @pl.when(step == pl.num_programs(0) - 1)
    def _():
        grad_router = jnp.zeros(grad_router_ref.shape, F32)
        for t in range(total // tile):
            at = slice(t * tile, (t + 1) * tile)
            produced = out_acc[at, :].astype(BF16).astype(F32)
            gate = gate_ref[at, :]
            out_ref[at, :] = (gate * produced).astype(BF16)
            grad_gate = jnp.sum(cot_ref[at, :].astype(F32) * produced, axis=1, keepdims=True)
            share = gate * (1.0 - gate) * grad_gate
            lane = iota((tile, LANES), 1)
            signed = jnp.where(lane == mine, share, 0.0) - jnp.where(lane == other_ref[at, :], share, 0.0)
            high = signed.astype(BF16)
            rest = (signed - high.astype(F32)).astype(BF16)
            routed = dot(high, router_turned_ref[...]) + dot(rest, router_turned_ref[...])
            back_ref[at, :] = (back_acc[at, :] + routed).astype(BF16)
            rows = rows_ref[at, :]
            grad_router = grad_router + dot_tn(rows, high) + dot_tn(rows, rest)
        grad_router_ref[...] = grad_router


def pair_grad_kernel(a0_ref, a1_ref, b0_ref, b1_ref, out_ref):
    out_ref[...] = (dot_tn(a0_ref[...], b0_ref[...]) + dot_tn(a1_ref[...], b1_ref[...])).astype(BF16)


def dense_grad_kernel(n0, n1, g0, g1, m0, m1, b0, b1, small, out_ref):
    width = n0.shape[1]
    for start in range(0, 3 * width, width):
        cols = slice(start, start + width)
        out_ref[:, cols] = (dot_tn(n0[...], g0[:, cols]) + dot_tn(n1[...], g1[:, cols])).astype(BF16)
    out_ref[:, 3 * width : 4 * width] = (dot_tn(m0[...], b0[...]) + dot_tn(m1[...], b1[...])).astype(BF16)
    out_ref[:, 4 * width :] = small[...]


def combine_kernel(out_ref, col_ref, hidden_ref, result_ref, pick_ref):
    fill_pick(col_ref, pick_ref)
    result_ref[...] = (hidden_ref[...] + dot(pick_ref[...], out_ref[...])).astype(BF16)


def cost(flops, byte_count, transcendentals=0):
    return pl.CostEstimate(flops=int(flops), bytes_accessed=int(byte_count), transcendentals=int(transcendentals))


def shaped(shape, dtype):
    return jax.ShapeDtypeStruct(shape, dtype)


def make_strip(base):
    heads, width = base.shape
    return pl.pallas_call(
        strip_kernel,
        out_shape=shaped((heads, STRIP, width - STRIP), BF16),
        compiler_params=params(),
        cost_estimate=cost(1e8, 4e6),
    )(base)


def dispatch(ids, cot, experts, capacity):
    length, width = cot.shape
    total = experts * capacity
    return pl.pallas_call(
        functools.partial(dispatch_kernel, experts, capacity),
        out_shape=(
            shaped((2, length), jnp.int32),
            shaped((length, 2), jnp.int32),
            shaped((total, width), BF16),
        ),
        compiler_params=params(),
        cost_estimate=cost(2 * total * length * width, 4e6),
    )(ids.T, ids, cot)


def forward(x, gains, weight, strip, block_row, block_col, row_slots, total):
    length, width = x.shape
    heads = width // HEAD
    return pl.pallas_call(
        forward_kernel,
        out_shape=(
            shaped((length, 3 * width), BF16),
            shaped((length, width), BF16),
            shaped((heads, length, 1), F32),
            shaped((length, width), F32),
            shaped((total, width), BF16),
        ),
        compiler_params=params(),
        cost_estimate=cost(
            2 * length * width * 4 * width + 8 * heads * length * length * HEAD + 2 * total * length * width,
            24e6, heads * length * length,
        ),
    )(x, gains, weight, strip, block_row, block_col, row_slots)


def backward(back, col, cot, hidden, gains, weight, proj, totals, strip, block_row, block_col, x):
    length, width = x.shape
    heads = width // HEAD
    total = back.shape[0]
    return pl.pallas_call(
        backward_kernel,
        out_shape=(
            shaped((length, width), BF16),
            shaped((length, width), BF16),
            shaped((length, 3 * width), BF16),
            shaped((length, width), BF16),
            shaped((2, width), F32),
            shaped((heads, 2 * length), F32),
        ),
        scratch_shapes=[
            pltpu.VMEM((length, total), BF16),
            pltpu.VMEM((length, width), BF16),
            pltpu.VMEM((length, length), BF16),
            pltpu.VMEM((length, length), BF16),
            pltpu.VMEM((STRIP, 2 * length), F32),
        ],
        compiler_params=params(),
        cost_estimate=cost(
            2 * length * width * 4 * width + 20 * heads * length * length * HEAD + 2 * total * length * width,
            30e6, heads * length * length,
        ),
    )(back, col, cot, hidden, gains, weight, proj, totals, strip, block_row, block_col, x)


def expert(rows, cot, ids, mine, router, router_turned, first, last):
    total, width = rows.shape
    inner = first.shape[1]
    step = 512
    whole = lambda shape: pl.BlockSpec(shape, lambda f: (0,) * len(shape))
    return pl.pallas_call(
        expert_kernel,
        grid=(inner // step,),
        in_specs=[
            whole(rows.shape), whole(cot.shape), whole(ids.shape),
            pl.BlockSpec(memory_space=pltpu.SMEM),
            whole(router.shape), whole(router_turned.shape),
            pl.BlockSpec((width, step), lambda f: (0, f)),
            pl.BlockSpec((step, width), lambda f: (f, 0)),
        ],
        out_specs=(
            whole((total, width)), whole((total, width)),
            pl.BlockSpec((total, step), lambda f: (0, f)),
            pl.BlockSpec((total, step), lambda f: (0, f)),
            whole((total, width)), whole((width, LANES)),
        ),
        out_shape=(
            shaped((total, width), BF16), shaped((total, width), BF16),
            shaped((total, inner), BF16), shaped((total, inner), BF16),
            shaped((total, width), BF16), shaped((width, LANES), F32),
        ),
        scratch_shapes=[
            pltpu.VMEM((total, 1), F32),
            pltpu.VMEM((total, 1), jnp.int32),
            pltpu.VMEM((total, width), F32),
            pltpu.VMEM((total, width), F32),
        ],
        compiler_params=params(dimension_semantics=("arbitrary",)),
        cost_estimate=cost(8 * total * width * inner, 40e6, total * inner),
    )(rows, cot, ids, mine, router, router_turned, first, last)


def pair_grad(a0, a1, b0, b1, split_left):
    total, left = a0.shape
    right = b0.shape[1]
    step = 512
    if split_left:
        grid, a_spec = (left // step,), pl.BlockSpec((total, step), lambda f: (0, f))
        b_spec = pl.BlockSpec((total, right), lambda f: (0, 0))
        out_spec = pl.BlockSpec((step, right), lambda f: (f, 0))
    else:
        grid, a_spec = (right // step,), pl.BlockSpec((total, left), lambda f: (0, 0))
        b_spec = pl.BlockSpec((total, step), lambda f: (0, f))
        out_spec = pl.BlockSpec((left, step), lambda f: (0, f))
    return pl.pallas_call(
        pair_grad_kernel,
        grid=grid,
        in_specs=[a_spec, a_spec, b_spec, b_spec],
        out_specs=out_spec,
        out_shape=shaped((left, right), BF16),
        compiler_params=params(dimension_semantics=("arbitrary",)),
        cost_estimate=cost(4 * total * left * right, 30e6),
    )(a0, a1, b0, b1)


def dense_grad(*arrays):
    small = arrays[-1]
    width = arrays[0].shape[1]
    length = arrays[0].shape[0]
    return pl.pallas_call(
        dense_grad_kernel,
        out_shape=shaped((width, 4 * width + small.shape[1]), BF16),
        compiler_params=params(),
        cost_estimate=cost(4 * length * width * 4 * width, 20e6),
    )(*arrays)


def combine(out_rows, col, hidden):
    length, width = hidden.shape
    total = out_rows.shape[0]
    return pl.pallas_call(
        combine_kernel,
        out_shape=shaped((length, width), BF16),
        scratch_shapes=[pltpu.VMEM((length, total), BF16)],
        compiler_params=params(),
        cost_estimate=cost(2 * total * length * width, 6e6),
    )(out_rows, col, hidden)


def body(
    dp, inputs, gain_one, w_qkv, w_out, rel_table, second_norm_gain, w_router, w_in, w_back,
    expert_ids, block_ids, cotangent,
):
    micro, length, width = inputs.shape
    experts = w_router.shape[1]
    capacity = 3 * length // experts
    total = experts * capacity
    buckets, heads = rel_table.shape[0] * dp, rel_table.shape[1]
    shard = gain_one.shape[0]
    first_in, last_out = w_in[0], w_back[0]
    mine = lax.axis_index("expert").astype(jnp.int32).reshape(1, 1)

    def exchange(rows):
        return lax.all_to_all(
            rows.reshape(experts, capacity, width), "expert", split_axis=0, concat_axis=0, tiled=True
        ).reshape(total, width)

    table_column = jnp.pad(rel_table.reshape(-1), (0, shard - rel_table.size))
    small = jnp.concatenate([gain_one[:, None], second_norm_gain[:, None], table_column[:, None], w_router], axis=1)
    small = jnp.pad(small, ((0, 0), (0, LANES - small.shape[1])))
    packed = lax.all_gather(jnp.concatenate([w_qkv, w_out, small], axis=1), "dp", axis=0, tiled=True)
    extra = packed[:, 4 * width :]
    gains = extra[:, :2].astype(F32).T
    table = extra[:, 2].reshape(dp, shard)[:, : rel_table.size].reshape(buckets, heads)
    router = jnp.pad(extra[:, 3 : 3 + experts], ((0, 0), (0, LANES - experts)))
    router_turned = router.T
    levels = bucket_table(length, buckets)
    base = lax.dot_general(
        table, jnp.asarray(levels, BF16), (((0,), (0,)), ((), ())), preferred_element_type=F32
    )
    ids_row = jnp.transpose(expert_ids, (0, 2, 1))
    ids_all = lax.all_gather(ids_row, "expert", axis=0, tiled=False)
    ids_all = jnp.transpose(ids_all, (1, 2, 0, 3))
    strip = make_strip(base)

    slots, cot_rows = [], []
    for m in range(micro):
        row, col, send = dispatch(expert_ids[m], cotangent[m], experts, capacity)
        slots.append((row, col))
        cot_rows.append(exchange(send))

    kept, rows = [], []
    for m in range(micro):
        block_row, block_col = block_ids[m], block_ids[m].reshape(length, 1)
        proj, mixed, totals, hidden, send = forward(
            inputs[m], gains, packed, strip, block_row, block_col, slots[m][0], total
        )
        kept.append((proj, mixed, totals, hidden, block_row, block_col))
        rows.append(exchange(send))

    expert_outs = []
    for m in range(micro):
        expert_outs.append(
            expert(rows[m], cot_rows[m], ids_all[m], mine, router, router_turned, first_in, last_out)
        )
    backs = [exchange(expert_outs[m][1]) for m in range(micro)]
    weighted = [exchange(expert_outs[m][0]) for m in range(micro)]

    grad_last = pair_grad(
        expert_outs[0][2], expert_outs[1][2], expert_outs[0][4], expert_outs[1][4], True
    )
    grad_first = pair_grad(rows[0], rows[1], expert_outs[0][3], expert_outs[1][3], False)
    grad_last = lax.psum(grad_last, "dp").astype(F32)
    grad_first = lax.psum(grad_first, "dp").astype(F32)
    grad_router = lax.psum(expert_outs[0][5][:, :experts] + expert_outs[1][5][:, :experts], ("dp", "expert"))
    grad_router = lax.dynamic_slice_in_dim(grad_router, lax.axis_index("dp") * shard, shard, 0)

    back_outs = []
    for m in range(micro):
        proj, mixed, totals, hidden, block_row, block_col = kept[m]
        back_outs.append(
            backward(
                backs[m], slots[m][1], cotangent[m], hidden, gains, packed, proj, totals, strip,
                block_row, block_col, inputs[m],
            )
        )
    results = [combine(weighted[m], slots[m][1], kept[m][3]) for m in range(micro)]

    gain_grads = back_outs[0][4] + back_outs[1][4]
    diagonals = back_outs[0][5] + back_outs[1][5]
    table_grad = lax.dot_general(
        jnp.asarray(levels, F32), diagonals, (((1,), (1,)), ((), ())),
        precision=lax.Precision.HIGHEST, preferred_element_type=F32,
    )
    table_grad = jnp.pad(table_grad.reshape(dp, rel_table.size), ((0, 0), (0, shard - rel_table.size)))
    small_grad = jnp.concatenate([gain_grads.T, table_grad.reshape(width, 1)], axis=1).astype(BF16)
    small_grad = jnp.pad(small_grad, ((0, 0), (0, LANES - small_grad.shape[1])))
    dense = dense_grad(
        back_outs[0][3], back_outs[1][3], back_outs[0][2], back_outs[1][2],
        kept[0][1], kept[1][1], back_outs[0][1], back_outs[1][1], small_grad,
    )
    dense = lax.psum_scatter(dense, "dp", scatter_dimension=0, tiled=True)
    dense = lax.psum(dense, "expert").astype(F32)
    tail = dense[:, 4 * width :]
    return (
        jnp.stack(results),
        jnp.stack([out[0] for out in back_outs]),
        tail[:, 0],
        dense[:, : 3 * width],
        dense[:, 3 * width : 4 * width],
        tail[: rel_table.size, 2].reshape(rel_table.shape),
        tail[:, 1],
        grad_router,
        grad_first[None],
        grad_last[None],
    )


def solution(mesh):
    split = P(None, ("dp", "expert"), None)
    in_specs = (
        split, P("dp"), P("dp", None), P("dp", None), P("dp", None), P("dp"), P("dp", None),
        P("expert", None, None), P("expert", None, None), split, split, split,
    )
    out_specs = (
        split, split, P("dp"), P("dp", None), P("dp", None), P("dp", None), P("dp"), P("dp", None),
        P("expert", None, None), P("expert", None, None),
    )
    return jax.shard_map(
        functools.partial(body, mesh.shape["dp"]), mesh=mesh, in_specs=in_specs, out_specs=out_specs, check_vma=False
    )
```

time: 1410 us -> 827 us (0.59)
  matrix products: 350 us -> 1.83 us
  Pallas kernels: 0 us -> 288 us
  local copies, waits for them, and re-layouts: 215 us -> 25.6 us
  blocking collectives: 310 us -> 151 us
  waiting for transfers between devices: 382 us -> 277 us
  other arithmetic: 104 us -> 20.9 us
  starting transfers between devices: 18.1 us -> 38.3 us
    dot_general x46 -> x2, matrix products: 350 us -> 1.83 us  [the longest x1 1.02 us: body(): lax.dot_general(jnp.asarray(levels, F32), diagonals, (((1,), (1,)), ((),...]
    pallas_call x0 -> x14, Pallas kernels: none -> 288 us  [the longest x2 109 us: expert(): pl.pallas_call(expert_kernel, grid=(inner // step,), in_specs=[whole(rows...]
    all_to_all x4 -> x0, blocking collectives: 234 us -> none  [the longest x2 118 us: micro_step(): lax.all_to_all(send_rows, 'expert', split_axis=0, concat_axis=0, tiled=True)]
    psum x2, waiting for transfers between devices: 213 us -> 144 us  [the longest x1 73.1 us: body(): dense = lax.psum(dense, 'expert').astype(F32)]
    gather x10 -> x0, local copies, waits for them, and re-layouts: 59.1 us -> none  [the longest x2 15.1 us: micro_step(): returned.reshape(-1, model_width)[target].astype(jnp.float32)]
    psum x1, blocking collectives: 20.5 us -> 77.8 us  [body(): lax.psum(expert_outs[0][5][:, :experts] + expert_outs[1][5][:, :experts],...]
    all_gather x4 -> x1, blocking collectives: 20.7 us -> 73.4 us  [body(): ids_all = lax.all_gather(ids_row, 'expert', axis=0, tiled=False)]
    mul x8 -> x0, local copies, waits for them, and re-layouts: 38 us -> none  [the longest x2 37.2 us: backward_block(): attention_score_gradient = probabilities * (grad_probs - inner_sum)]
  transfers between devices with their start and end apart: 16 -> 12, of which waited for: 8 -> 7; matrix products, arithmetic and copies ran while one was open for 27% -> 3% of each run, Pallas kernels for 0% -> 30%
where the time goes in v1:
time: 827 us; the launch traced here: 817 us
  Pallas kernels  288 us (35%)
  waiting for transfers between devices  277 us (33%)
  blocking collectives  151 us (18%)
  starting transfers between devices  38.3 us (5%)
  local copies, waits for them, and re-layouts  25.6 us (3%)
  other arithmetic  20.9 us (3%)
  between operations  14.5 us (2%)
    all_to_all x8, waiting for transfers between devices, exchange(): lax.all_to_all(rows.reshape(experts, capacity, width), 'expert', split_ax...  132 us
    pallas_call x2, Pallas kernels, expert(): pl.pallas_call(expert_kernel, grid=(inner // step,), in_specs=[whole(rows...  109 us
    psum x1, blocking collectives, body(): lax.psum(expert_outs[0][5][:, :experts] + expert_outs[1][5][:, :experts],...  77.8 us
    all_gather x1, blocking collectives, body(): ids_all = lax.all_gather(ids_row, 'expert', axis=0, tiled=False)  73.4 us
    psum x1, waiting for transfers between devices, body(): dense = lax.psum(dense, 'expert').astype(F32)  73.1 us
    psum x1, waiting for transfers between devices, body(): grad_first = lax.psum(grad_first, 'dp').astype(F32)  70.9 us
    pallas_call x2, Pallas kernels, backward(): pl.pallas_call(backward_kernel, out_shape=(shaped((length, width), BF16),...  59.9 us
    pallas_call x2, Pallas kernels, forward(): pl.pallas_call(forward_kernel, out_shape=(shaped((length, 3 * width), BF1...  44.6 us
  transfers between devices with their start and end apart: 12, of which 7 were waited for; matrix products, arithmetic and copies ran while one was open for 3% of the time, Pallas kernels for 30%

profile of v1, /device:TPU:0, one launch (start us, length us, event | category | flops | bytes accessed | tf_op | source)
XLA Modules:
  0.0 817.4 jit_solution(9403341682120884300)
XLA Ops:
  19.7 7.3 all-to-all-start.1
  32.2 48.6 %all-to-all-done.1 = bf16[8,192,768]{2,1,0:T(8,128)(2,1)S(1)} async-done(((bf16[8,192,768]{2,1,0:T(8,128)(2,1)}), bf16[8,192,768]{2,1,0:T(8,128)(2,1)S(1)}, u32[]{:S(2)}, u32[]{:S(2)}) %all-to-all-start.1) | async-done | bytes 2359328 | tf_op jit(solution)/shard_map/all_to_all | solution.py:532
  95.2 22.3 %shard_map.215 = (bf16[512,2304]{1,0:T(8,128)(2,1)}, bf16[512,768]{1,0:T(8,128)(2,1)}, f32[12,512,1]{2,1,0:T(8,128)}, f32[512,768]{1,0:T(8,128)}, bf16[1536,768]{1,0:T(8,128)(2,1)}) custom-call(bf16[512,768]{1,0:T(8,128)(2,1)} %get-tuple-element.139.x_ref, f32[2,768]{1,0:T(2,128)} %copy.65.gains_ref, ...), custom_call_target="tpu_custom_call" | custom-call | flops 5234491392 | bytes 24000000 | tf_op jit(solution)/shard_map/pallas_call | solution.py:388
  117.5 22.6 %all-to-all-done.4 = bf16[8,192,768]{2,1,0:T(8,128)(2,1)} async-done(((bf16[8,192,768]{2,1,0:T(8,128)(2,1)}), bf16[8,192,768]{2,1,0:T(8,128)(2,1)}, u32[]{:S(2)}, u32[]{:S(2)}) %all-to-all-start.4) | async-done | bytes 2359328 | tf_op jit(solution)/shard_map/all_to_all | solution.py:532
  144.8 22.3 %shard_map.219 = (bf16[512,2304]{1,0:T(8,128)(2,1)}, bf16[512,768]{1,0:T(8,128)(2,1)}, f32[12,512,1]{2,1,0:T(8,128)}, f32[512,768]{1,0:T(8,128)}, bf16[1536,768]{1,0:T(8,128)(2,1)}) custom-call(bf16[512,768]{1,0:T(8,128)(2,1)} %get-tuple-element.138.x_ref, f32[2,768]{1,0:T(2,128)} %copy.65.gains_ref, ...), custom_call_target="tpu_custom_call" | custom-call | flops 5234491392 | bytes 24000000 | tf_op jit(solution)/shard_map/pallas_call | solution.py:388
  167.1 30.9 %all-to-all-done = bf16[8,192,768]{2,1,0:T(8,128)(2,1)S(1)} async-done(((bf16[8,192,768]{2,1,0:T(8,128)(2,1)}), bf16[8,192,768]{2,1,0:T(8,128)(2,1)S(1)}, u32[]{:S(2)}, u32[]{:S(2)}) %all-to-all-start) | async-done | bytes 2359328 | tf_op jit(solution)/shard_map/all_to_all | solution.py:532
  203.7 73.4 %all-gather = s32[16,2,512]{2,1,0:T(2,128)S(1)} all-gather(s32[2,2,512]{2,1,0:T(2,128)S(1)} %bitcast.92), channel_id=2, replica_groups=mesh['dp'=4,'expert'=8] {'expert'}, dimensions={0}, use_global_device_ids=true | all-gather | bytes 73728 | tf_op jit(solution)/shard_map/all_gather | solution.py:550
  280.4 54.6 %shard_map.216 = (bf16[1536,768]{1,0:T(8,128)(2,1)}, bf16[1536,768]{1,0:T(8,128)(2,1)}, bf16[1536,3072]{1,0:T(8,128)(2,1)}, bf16[1536,3072]{1,0:T(8,128)(2,1)}, ...) custom-call(bf16[1536,768]{1,0:T(8,128)(2,1)} %bitcast.73, bf16[1536,768]{1,0:T(8,128)(2,1)} %bitcast.76, ...), custom_call_target="tpu_custom_call" | custom-call | flops 28991029248 | bytes 40000000 | tf_op jit(solution)/shard_map/pallas_call | solution.py:439
  339.1 54.7 %shard_map.220 = (bf16[1536,768]{1,0:T(8,128)(2,1)}, bf16[1536,768]{1,0:T(8,128)(2,1)}, bf16[1536,3072]{1,0:T(8,128)(2,1)}, bf16[1536,3072]{1,0:T(8,128)(2,1)}, ...) custom-call(bf16[1536,768]{1,0:T(8,128)(2,1)} %bitcast.29.rows_ref.a1_ref, bf16[1536,768]{1,0:T(8,128)(2,1)} %bitcast.31.cot_ref, ...), custom_call_target="tpu_custom_call" | custom-call | flops 28991029248 | bytes 40000000 | tf_op jit(solution)/shard_map/pallas_call | solution.py:439
  395.2 6.0 all-to-all-start.7
  401.5 29.8 %shard_map.222 = (bf16[512,768]{1,0:T(8,128)(2,1)}, bf16[512,768]{1,0:T(8,128)(2,1)}, bf16[512,2304]{1,0:T(8,128)(2,1)}, bf16[512,768]{1,0:T(8,128)(2,1)}, f32[2,768]{1,0:T(2,128)}, /*index=5*/f32[12,1024]{1,0:T(8,128)}) custom-call(bf16[1536,768]{1,0:T(8,128)(2,1)} %bitcast.79, s32[512,2]{1,0:T(8,128)} %get-tuple-element.54.col_ref, ...), custom_call_target="tpu_custom_call" | custom-call | flops 7650410496 | bytes 30000000 | tf_op jit(solution)/shard_map/pallas_call | solution.py:409
  431.2 18.5 %all-to-all-done.7 = bf16[8,192,768]{2,1,0:T(8,128)(2,1)} async-done(((bf16[8,192,768]{2,1,0:T(8,128)(2,1)}), bf16[8,192,768]{2,1,0:T(8,128)(2,1)}, u32[]{:S(2)}, u32[]{:S(2)}) %all-to-all-start.7) | async-done | bytes 2359328 | tf_op jit(solution)/shard_map/all_to_all | solution.py:532
  449.8 30.1 %shard_map.223 = (bf16[512,768]{1,0:T(8,128)(2,1)}, bf16[512,768]{1,0:T(8,128)(2,1)}, bf16[512,2304]{1,0:T(8,128)(2,1)}, bf16[512,768]{1,0:T(8,128)(2,1)}, f32[2,768]{1,0:T(2,128)}, /*index=5*/f32[12,1024]{1,0:T(8,128)}) custom-call(bf16[1536,768]{1,0:T(8,128)(2,1)} %bitcast.40.back_ref, s32[512,2]{1,0:T(8,128)} %get-tuple-element.60.col_ref, ...), custom_call_target="tpu_custom_call" | custom-call | flops 7650410496 | bytes 30000000 | tf_op jit(solution)/shard_map/pallas_call | solution.py:409
  482.9 11.0 %shard_map.224 = bf16[768,3200]{1,0:T(8,128)(2,1)} custom-call(bf16[512,768]{1,0:T(8,128)(2,1)} %get-tuple-element.70.n0, bf16[512,768]{1,0:T(8,128)(2,1)} %get-tuple-element.71.n1, bf16[512,2304]{1,0:T(8,128)(2,1)} %get-tuple-element.72.g0, bf16[512,2304]{1,0:T(8,128)(2,1)} %get-tuple-element.73.g1, bf16[512,768]{1,0:T(8,128)(2,1)} %get-tuple-element.74.m0, ...), custom_call_target="tpu_custom_call" | custom-call | flops 4831838208 | bytes 20000000 | tf_op jit(solution)/shard_map/pallas_call | solution.py:498
  497.6 21.4 %shard_map.225 = bf16[768,3072]{1,0:T(8,128)(2,1)} custom-call(bf16[1536,768]{1,0:T(8,128)(2,1)} %bitcast.74, bf16[1536,768]{1,0:T(8,128)(2,1)} %bitcast.29.rows_ref.a1_ref, bf16[1536,3072]{1,0:T(8,128)(2,1)} %get-tuple-element.84.b0_ref, bf16[1536,3072]{1,0:T(8,128)(2,1)} %get-tuple-element.85.b1_ref), custom_call_target="tpu_custom_call" | custom-call | flops 14495514624 | bytes 30000000 | tf_op jit(solution)/shard_map/pallas_call | solution.py:483
  519.0 20.2 %shard_map.226 = bf16[3072,768]{1,0:T(8,128)(2,1)} custom-call(bf16[1536,3072]{1,0:T(8,128)(2,1)} %get-tuple-element.86.a0_ref, bf16[1536,3072]{1,0:T(8,128)(2,1)} %get-tuple-element.87.a1_ref, bf16[1536,768]{1,0:T(8,128)(2,1)} %get-tuple-element.88.b0_ref, bf16[1536,768]{1,0:T(8,128)(2,1)} %get-tuple-element.89.b1_ref), custom_call_target="tpu_custom_call" | custom-call | flops 14495514624 | bytes 30000000 | tf_op jit(solution)/shard_map/pallas_call | solution.py:483
  539.2 11.5 %all-to-all-done.2 = bf16[8,192,768]{2,1,0:T(8,128)(2,1)S(1)} async-done(((bf16[8,192,768]{2,1,0:T(8,128)(2,1)}), bf16[8,192,768]{2,1,0:T(8,128)(2,1)S(1)}, u32[]{:S(2)}, u32[]{:S(2)}) %all-to-all-start.2) | async-done | bytes 2359328 | tf_op jit(solution)/shard_map/all_to_all | solution.py:532
  557.2 77.8 %psum.29 = f32[768,8]{1,0:T(8,128)S(1)} all-reduce(f32[768,8]{1,0:T(8,128)S(1)} %slice_add_fusion), channel_id=1, replica_groups=mesh['dp'=4,'expert'=8] {'dp','expert'}, use_global_device_ids=true, to_apply=%region_2.3 | all-reduce | flops 6144 | bytes 49152 | tf_op jit(solution)/shard_map/psum | solution.py:583
  635.7 4.7 shard_map.217
  640.5 5.4 shard_map.221
  649.1 70.9 %all-reduce.11.cloned.1.call-done = (bf16[1,768,3072]{2,1,0:T(8,128)(2,1)}, bf16[1,3072,768]{2,1,0:T(8,128)(2,1)}) async-done(((bf16[1,768,3072]{2,1,0:T(8,128)(2,1)}, bf16[1,3072,768]{2,1,0:T(8,128)(2,1)}), (bf16[1,768,3072]{2,1,0:T(8,128)(2,1)}, bf16[1,3072,768]{2,1,0:T(8,128)(2,1)})) %all-reduce.11.cloned.1.call-update) | async-done | bytes 9437200 | tf_op jit(solution)/shard_map/psum | solution.py:582
  719.9 7.5 broadcast_in_dim.25
  727.4 4.5 broadcast_in_dim.27
  731.9 73.1 %all-reduce.9.cloned.1.call-done = bf16[192,3200]{1,0:T(8,128)(2,1)} async-done(((bf16[192,3200]{1,0:T(8,128)(2,1)}), bf16[192,3200]{1,0:T(8,128)(2,1)}) %all-reduce.9.cloned.1.call-update) | async-done | bytes 1228816 | tf_op jit(solution)/shard_map/psum | solution.py:611
  (115 shorter events, 73.8 us)
Async XLA Ops:
  7.2 5.6 copy-start.8
  7.2 5.6 copy-start.9
  7.2 80.9 %all-gather.3.cloned.1.call-start = ((), (), s32[]{:S(2)}) async-start(), calls=%async_computation.9 | async-start | bytes 6144000 | tf_op jit(solution)/shard_map/all_gather | solution.py:539
  19.7 61.1 %all-to-all-start.1 = ((bf16[8,192,768]{2,1,0:T(8,128)(2,1)}), bf16[8,192,768]{2,1,0:T(8,128)(2,1)S(1)}, u32[]{:S(2)}, u32[]{:S(2)}) async-start(bf16[8,192,768]{2,1,0:T(8,128)(2,1)} %bitcast.83), calls=%async_computation.1 | async-start | bytes 4718592 | tf_op jit(solution)/shard_map/all_to_all | solution.py:532
  80.8 5.8 copy-start.21
  80.8 10.3 %copy-start.17 = (bf16[32,1024]{1,0:T(8,128)(2,1)S(1)}, bf16[32,1024]{1,0:T(8,128)(2,1)}, u32[]{:S(2)}) copy-start(bf16[32,1024]{1,0:T(8,128)(2,1)} %constant.22.clone) | copy-start | bytes 196612
  82.3 57.8 %all-to-all-start.4 = ((bf16[8,192,768]{2,1,0:T(8,128)(2,1)}), bf16[8,192,768]{2,1,0:T(8,128)(2,1)}, u32[]{:S(2)}, u32[]{:S(2)}) async-start(bf16[8,192,768]{2,1,0:T(8,128)(2,1)} %bitcast.77), calls=%async_computation.4 | async-start | bytes 4718592 | tf_op jit(solution)/shard_map/all_to_all | solution.py:532
  140.1 57.9 %all-to-all-start = ((bf16[8,192,768]{2,1,0:T(8,128)(2,1)}), bf16[8,192,768]{2,1,0:T(8,128)(2,1)S(1)}, u32[]{:S(2)}, u32[]{:S(2)}) async-start(bf16[8,192,768]{2,1,0:T(8,128)(2,1)} %bitcast.82), calls=%async_computation | async-start | bytes 4718592 | tf_op jit(solution)/shard_map/all_to_all | solution.py:532
  199.3 135.7 %all-to-all-start.3 = ((bf16[8,192,768]{2,1,0:T(8,128)(2,1)}), bf16[8,192,768]{2,1,0:T(8,128)(2,1)}, u32[]{:S(2)}, u32[]{:S(2)}) async-start(bf16[8,192,768]{2,1,0:T(8,128)(2,1)} %bitcast.78), calls=%async_computation.3 | async-start | bytes 4718592 | tf_op jit(solution)/shard_map/all_to_all | solution.py:532
  335.0 58.8 %all-to-all-start.6 = ((bf16[8,192,768]{2,1,0:T(8,128)(2,1)}), bf16[8,192,768]{2,1,0:T(8,128)(2,1)S(1)}, u32[]{:S(2)}, u32[]{:S(2)}) async-start(bf16[8,192,768]{2,1,0:T(8,128)(2,1)} %bitcast.81), calls=%async_computation.6 | async-start | bytes 4718592 | tf_op jit(solution)/shard_map/all_to_all | solution.py:532
  395.2 54.5 %all-to-all-start.7 = ((bf16[8,192,768]{2,1,0:T(8,128)(2,1)}), bf16[8,192,768]{2,1,0:T(8,128)(2,1)}, u32[]{:S(2)}, u32[]{:S(2)}) async-start(bf16[8,192,768]{2,1,0:T(8,128)(2,1)} %bitcast.80), calls=%async_computation.7 | async-start | bytes 4718592 | tf_op jit(solution)/shard_map/all_to_all | solution.py:532
  401.2 155.4 %reduce-scatter.2.cloned.1.call-start = ((), (), s32[]{:S(2)}) async-start(), calls=%async_computation.10 | async-start | bytes 6144000 | tf_op jit(solution)/shard_map/reduce_scatter | solution.py:610
  449.8 30.1 %copy-start.16 = (f32[32,1024]{1,0:T(8,128)S(1)}, f32[32,1024]{1,0:T(8,128)}, u32[]{:S(2)}) copy-start(f32[32,1024]{1,0:T(8,128)} %constant.23.clone) | copy-start | bytes 393220
  449.8 30.1 %copy-start.18 = (f32[12,1024]{1,0:T(8,128)S(1)}, f32[12,1024]{1,0:T(8,128)}, u32[]{:S(2)}) copy-start(f32[12,1024]{1,0:T(8,128)} %get-tuple-element.80) | copy-start | bytes 147460
  449.8 31.5 %copy-start.20 = (f32[2,768]{1,0:T(2,128)S(1)}, f32[2,768]{1,0:T(2,128)}, u32[]{:S(2)}) copy-start(f32[2,768]{1,0:T(2,128)} %get-tuple-element.78) | copy-start | bytes 18436
  494.0 56.8 %all-to-all-start.2 = ((bf16[8,192,768]{2,1,0:T(8,128)(2,1)}), bf16[8,192,768]{2,1,0:T(8,128)(2,1)S(1)}, u32[]{:S(2)}, u32[]{:S(2)}) async-start(bf16[8,192,768]{2,1,0:T(8,128)(2,1)} %bitcast.75), calls=%async_computation.2 | async-start | bytes 4718592 | tf_op jit(solution)/shard_map/all_to_all | solution.py:532
  497.6 222.3 %all-reduce.11.cloned.1.call-start = ((), (), s32[]{:S(2)}) async-start(), calls=%async_computation.12 | async-start | bytes 18874368 | tf_op jit(solution)/shard_map/psum | solution.py:582
  550.7 6.4 copy-start.14
  550.7 6.4 copy-start.15
  552.1 88.3 %all-to-all-start.5 = ((bf16[8,192,768]{2,1,0:T(8,128)(2,1)}), bf16[8,192,768]{2,1,0:T(8,128)(2,1)}, u32[]{:S(2)}, u32[]{:S(2)}) async-start(bf16[8,192,768]{2,1,0:T(8,128)(2,1)} %bitcast.72), calls=%async_computation.5 | async-start | bytes 4718592 | tf_op jit(solution)/shard_map/all_to_all | solution.py:532
  556.5 248.5 %all-reduce.9.cloned.1.call-start = ((), (), s32[]{:S(2)}) async-start(), calls=%async_computation.11 | async-start | bytes 2457600 | tf_op jit(solution)/shard_map/psum | solution.py:611
  640.4 5.4 copy-start.12
  640.4 5.4 copy-start.13
  719.9 7.5 copy-start.2
  (10 other events, 15.3 us)
Sparse Core Ops, SparseCore 0:
  12.9 41.2 all-gather.2
  494.1 48.0 reduce-scatter.1
  545.5 174.3 all-reduce.10
  723.7 81.2 all-reduce.8

commit v2 on v1

v2 whole, which is shorter than its diff:
```python
import functools

import jax
import jax.numpy as jnp
import numpy as np
from jax import lax
from jax.experimental import pallas as pl
from jax.experimental.pallas import tpu as pltpu
from jax.sharding import PartitionSpec as P

HEAD = 64
PAIR = 2 * HEAD
STRIP = 128
LANES = 128
VMEM_BYTES = 60 * 1024 * 1024
SCALE = 5
VECTOR = pl.BlockSpec(memory_space=pltpu.VMEM)
SCALAR = pl.BlockSpec(memory_space=pltpu.SMEM)
ANYWHERE = pl.BlockSpec(memory_space=pl.ANY)

epsilon = 1e-06
bucket_edges = (12, 16, 23, 32, 46, 64, 91)
masked_score = -1e30
gelu_a = float(np.sqrt(2.0 / np.pi))
gelu_b = 0.044715

F32 = jnp.float32
BF16 = jnp.bfloat16


def dot(a, b):
    return jnp.dot(a, b, preferred_element_type=F32)


def dot_nt(a, b):
    return lax.dot_general(a, b, (((1,), (1,)), ((), ())), preferred_element_type=F32)


def dot_tn(a, b):
    return lax.dot_general(a, b, (((0,), (0,)), ((), ())), preferred_element_type=F32)


def iota(shape, dim):
    return lax.broadcasted_iota(jnp.int32, shape, dim)


def hot(mask):
    return jnp.where(mask, 1.0, 0.0).astype(BF16)


def params(**extra):
    return pltpu.CompilerParams(vmem_limit_bytes=VMEM_BYTES, **extra)


def bucket_table(length, buckets):
    offset = np.arange(2 * length) - (length - 1)
    distance = np.abs(offset)
    far = 8 + sum((distance >= edge).astype(np.int32) for edge in bucket_edges)
    bucket = np.where(distance < 8, distance, far) + 16 * (offset > 0)
    table = (bucket[None, :] == np.arange(buckets)[:, None]) & (offset < length)[None, :]
    return table.astype(np.float32)


def strip_kernel(base_ref, out_ref):
    heads, width = base_ref.shape
    for h in range(heads):
        row = jnp.broadcast_to(base_ref[h : h + 1, :], (STRIP, width))
        rolled = pltpu.roll(row, width - (STRIP - 1), 1, stride=1, stride_axis=0)
        out_ref[h] = rolled[:, : width - STRIP].astype(BF16)


def slots_kernel(experts, near, capacity, ids_row_ref, ids_col_ref, far_row_ref, far_col_ref, mine_ref, row_ref, row_far_ref, col_ref, col_far_ref):
    length = ids_row_ref.shape[1]
    base = mine_ref[0, 0] // near * near
    padded = max(16, experts)
    before = hot(iota((length, length), 0) < iota((length, length), 1))
    for ids_row, row_out in ((ids_row_ref, row_ref), (far_row_ref, row_far_ref)):
        level = iota((padded, length), 0)
        first, second = ids_row[0:1, :], ids_row[1:2, :]
        place = dot(hot((level == first) | (level == second)), before).astype(jnp.int32)
        block = level - base
        slot = jnp.where((block >= 0) & (block < near), place + block * capacity, -1)
        row_out[0:1, :] = jnp.sum(jnp.where(level == first, slot, 0), axis=0, keepdims=True)
        row_out[1:2, :] = jnp.sum(jnp.where(level == second, slot, 0), axis=0, keepdims=True)

    after = hot(iota((length, length), 1) < iota((length, length), 0))
    for ids_col, col_out in ((ids_col_ref, col_ref), (far_col_ref, col_far_ref)):
        level = iota((length, LANES), 1)
        first, second = ids_col[:, 0:1], ids_col[:, 1:2]
        slot = dot(after, hot((level == first) | (level == second))) + (level * capacity).astype(F32)
        col_out[:, 0:1] = jnp.sum(jnp.where(level == first, slot, 0.0), axis=1, keepdims=True).astype(jnp.int32)
        col_out[:, 1:2] = jnp.sum(jnp.where(level == second, slot, 0.0), axis=1, keepdims=True).astype(jnp.int32)


def scatter_kernel(picks, *refs):
    count = len(picks)
    slots, refs, send_ref = refs[:count], refs[count:-1], refs[-1]
    values = []
    for part in picks:
        values.append([ref if pick is None else ref.at[pick] for pick, ref in zip(part, refs)])
        refs = refs[len(part) :]
    scatter_parts(slots, values, send_ref)


def scatter_parts(slot_refs, value_refs, send_ref):
    near, length = send_ref.shape[0], slot_refs[0].shape[1]
    count = len(slot_refs)
    capacity = send_ref.shape[1] // count
    for n in range(count):
        first, second = slot_refs[n][0:1, :], slot_refs[n][1:2, :]
        values = [ref[...] for ref in value_refs[n]]
        for d in range(near):
            slots = iota((capacity, length), 0) + d * capacity
            pick = hot((slots == first) | (slots == second))
            total, start = None, 0
            for value in values:
                part = dot(pick[:, start : start + value.shape[0]], value)
                total = part if total is None else total + part
                start += value.shape[0]
            send_ref[d, n * capacity : (n + 1) * capacity, :] = total.astype(BF16)


def fill_pick(col_ref, pick_ref, offset=0):
    length, total = pick_ref.shape
    first, second = col_ref[:, 0:1] - offset, col_ref[:, 1:2] - offset
    step = 256
    for start in range(0, total, step):
        slots = iota((length, step), 1) + start
        pick_ref[:, start : start + step] = hot((slots == first) | (slots == second))


def gather_kernel(first_ref, second_ref, mine_ref, blocks_ref, first_sum_ref, second_sum_ref, pick_ref, near_ref):
    near, pair_rows, _ = blocks_ref.shape
    capacity = pair_rows // 2
    offset = mine_ref[0, 0] // near * near * capacity
    for part, (col_ref, sum_ref) in enumerate(((first_ref, first_sum_ref), (second_ref, second_sum_ref))):
        fill_pick(col_ref, pick_ref, offset)
        for d in range(near):
            near_ref[d * capacity : (d + 1) * capacity, :] = blocks_ref[d, part * capacity : (part + 1) * capacity, :]
        sum_ref[...] = dot(pick_ref[...], near_ref[...]).astype(BF16)


def head_mask(length):
    return iota((length, PAIR), 1) < HEAD


def forward_kernel(
    m, x_ref, gains_ref, weight_ref, strip_ref, block_row_ref, block_col_ref, row_ref,
    proj_ref, mixed_ref, total_ref, hidden_ref, second_ref, send_ref,
):
    _, length, width = x_ref.shape
    scale = HEAD ** (-0.5)
    x = x_ref[m].astype(F32)
    r1 = lax.rsqrt(jnp.mean(x * x, axis=1, keepdims=True) + epsilon)
    normed = (x * r1 * gains_ref[0:1, :]).astype(BF16)
    proj_ref[...] = dot(normed, weight_ref[:, : 3 * width]).astype(BF16)

    def pair(p, carry):
        lanes = pl.multiple_of(p * PAIR, PAIR)
        q = proj_ref[:, pl.ds(lanes, PAIR)]
        k = proj_ref[:, pl.ds(width + lanes, PAIR)]
        v = proj_ref[:, pl.ds(2 * width + lanes, PAIR)]
        left = head_mask(length)
        zero = jnp.zeros_like(k)
        outs = [None] * (length // STRIP)
        for h in range(2):
            keep = left if h == 0 else jnp.logical_not(left)
            kh = jnp.where(keep, k, zero)
            vh = jnp.where(keep, v, zero)
            strip = strip_ref[2 * p + h].astype(F32)
            for i in range(length // STRIP):
                rows = slice(i * STRIP, (i + 1) * STRIP)
                start = length - STRIP - i * STRIP
                s = dot_nt(q[rows], kh) * scale + strip[:, start : start + length]
                s = jnp.where(block_row_ref[m] <= block_col_ref[rows, m : m + 1], s, masked_score)
                top = jnp.max(s, axis=1, keepdims=True)
                e = jnp.exp(s - top)
                total = jnp.sum(e, axis=1, keepdims=True)
                weights = (e * (1.0 / total)).astype(BF16)
                total_ref[2 * p + h, rows, :] = top + jnp.log(total)
                part = dot(weights, vh)
                outs[i] = part if outs[i] is None else outs[i] + part
        for i, part in enumerate(outs):
            mixed_ref[i * STRIP : (i + 1) * STRIP, pl.ds(lanes, PAIR)] = part.astype(BF16)
        return carry

    lax.fori_loop(0, width // PAIR, pair, 0)
    hidden = x + dot(mixed_ref[...], weight_ref[:, 3 * width : 4 * width])
    hidden_ref[...] = hidden
    r2 = lax.rsqrt(jnp.mean(hidden * hidden, axis=1, keepdims=True) + epsilon)
    second_ref[...] = (hidden * r2 * gains_ref[1:2, :]).astype(BF16)
    scatter_parts([row_ref], [[second_ref]], send_ref)


def backward_kernel(near, part, *refs):
    backward_main(part, refs[:near], *refs[near:])


def backward_main(
    part, far_refs, own_ref, mine_ref, col_ref, cot_ref, hidden_ref, gains_ref, weight_ref, proj_ref, total_ref, strip_ref,
    block_row_ref, block_col_ref, x_ref,
    grad_x_ref, branch_ref, grad_proj_ref, normed_ref, grad_gain_ref, diagonal_ref,
    pick_ref, back_ref, grad_mixed_ref, low_ref, prob_ref, strip_sum_ref,
):
    _, length, width = cot_ref.shape
    scale = HEAD ** (-0.5)
    near, capacity = own_ref.shape[0], own_ref.shape[1] // 2
    mine = mine_ref[0, 0]
    base = mine // near * near
    for d in range(near):
        own = own_ref[d, part * capacity : (part + 1) * capacity, :]
        back_ref[pl.ds(pl.multiple_of((base + d) * capacity, 16), capacity), :] = own
        back_ref[pl.ds(pl.multiple_of((mine ^ (near | d)) * capacity, 16), capacity), :] = far_refs[d][...]
    fill_pick(col_ref, pick_ref)
    grad_second = dot(pick_ref[...], back_ref[...])
    hidden = hidden_ref[...]
    r2 = lax.rsqrt(jnp.mean(hidden * hidden, axis=1, keepdims=True) + epsilon)
    scaled = grad_second * gains_ref[1:2, :]
    inner = jnp.mean(hidden * scaled, axis=1, keepdims=True)
    grad_hidden = cot_ref[part].astype(F32) + r2 * scaled - hidden * (r2 * r2 * r2 * inner)
    grad_gain_ref[1:2, :] = jnp.sum(grad_second * hidden * r2, axis=0, keepdims=True)
    branch = grad_hidden.astype(BF16)
    branch_ref[...] = branch
    grad_mixed_ref[...] = dot_nt(branch, weight_ref[:, 3 * width : 4 * width]).astype(BF16)

    m = part

    def pair(p, carry):
        lanes = pl.multiple_of(p * PAIR, PAIR)
        q = proj_ref[:, pl.ds(lanes, PAIR)]
        k = proj_ref[:, pl.ds(width + lanes, PAIR)]
        v = proj_ref[:, pl.ds(2 * width + lanes, PAIR)]
        g = grad_mixed_ref[:, pl.ds(lanes, PAIR)]
        q_turned = q.astype(F32).T.astype(BF16)
        g_turned = g.astype(F32).T.astype(BF16)
        left = head_mask(length)
        zero = jnp.zeros_like(k)
        outs = [None] * (length // STRIP)
        keys, values = [], []
        for h in range(2):
            keep = left if h == 0 else jnp.logical_not(left)
            kh = jnp.where(keep, k, zero)
            vh = jnp.where(keep, v, zero)
            strip = strip_ref[2 * p + h].astype(F32)
            strip_sum_ref[...] = jnp.zeros_like(strip_sum_ref)
            for i in range(length // STRIP):
                rows = slice(i * STRIP, (i + 1) * STRIP)
                start = length - STRIP - i * STRIP
                s = dot_nt(q[rows], kh) * scale + strip[:, start : start + length]
                s = jnp.where(block_row_ref[m] <= block_col_ref[rows, m : m + 1], s, masked_score)
                prob = jnp.exp(s - total_ref[2 * p + h, rows, :])
                grad_prob = dot_nt(g[rows], vh)
                row_inner = jnp.sum(prob * grad_prob, axis=1, keepdims=True)
                grad_score = prob * (grad_prob - row_inner)
                strip_sum_ref[:, start : start + length] += grad_score
                low = grad_score.astype(BF16)
                low_ref[rows, :] = low
                prob_ref[rows, :] = prob.astype(BF16)
                part = dot(low, kh)
                outs[i] = part if outs[i] is None else outs[i] + part
            half = slice(h * HEAD, (h + 1) * HEAD)
            keys.append(dot(q_turned[half], low_ref[...]))
            values.append(dot(g_turned[half], prob_ref[...]))
            gathered = jnp.zeros((8, 2 * length), F32)
            for a in range(STRIP // 8):
                piece = strip_sum_ref[8 * a : 8 * a + 8, :]
                gathered += pltpu.roll(piece, STRIP - 8 - 8 * a, 1) if a < STRIP // 8 - 1 else piece
            line = gathered[7:8]
            for b in range(7):
                line += pltpu.roll(gathered[b : b + 1], 7 - b, 1)
            diagonal_ref[pl.ds(2 * p + h, 1), :] = line
        for i, part in enumerate(outs):
            grad_proj_ref[i * STRIP : (i + 1) * STRIP, pl.ds(lanes, PAIR)] = (part * scale).astype(BF16)
        grad_key = jnp.concatenate(keys, axis=0).T
        grad_value = jnp.concatenate(values, axis=0).T
        grad_proj_ref[:, pl.ds(width + lanes, PAIR)] = (grad_key * scale).astype(BF16)
        grad_proj_ref[:, pl.ds(2 * width + lanes, PAIR)] = grad_value.astype(BF16)
        return carry

    lax.fori_loop(0, width // PAIR, pair, 0)
    x = x_ref[part].astype(F32)
    r1 = lax.rsqrt(jnp.mean(x * x, axis=1, keepdims=True) + epsilon)
    normed_ref[...] = (x * r1 * gains_ref[0:1, :]).astype(BF16)
    grad_normed = dot_nt(grad_proj_ref[...], weight_ref[:, : 3 * width])
    scaled = grad_normed * gains_ref[0:1, :]
    inner = jnp.mean(x * scaled, axis=1, keepdims=True)
    grad_gain_ref[0:1, :] = jnp.sum(grad_normed * x * r1, axis=0, keepdims=True)
    grad_x_ref[...] = (grad_hidden + r1 * scaled - x * (r1 * r1 * r1 * inner)).astype(BF16)


def expert_kernel(
    kind, near, alias, part, *refs,
):
    sent_ref, cots_ref, ids_ref, mine_ref, router_ref, router_turned_ref, first_ref, last_ref = refs[:8]
    refs = refs[8 + alias :]
    back_refs, refs = refs[: near if kind else 1], refs[near if kind else 1 :]
    all_ref, act_ref, grad_up_ref, scaled_ref, grad_router_ref = refs[:5]
    gate_ref, other_ref, out_acc, back_acc, slot_ref, partner_ref, out_ref, back_ref, sem = refs[5:]
    step = pl.program_id(0)
    total = scaled_ref.shape[0]
    _, sources, length = ids_ref.shape
    capacity = total // near
    mine = mine_ref[0, 0]
    base = mine // near * near
    tile = total

    @pl.when(step == 0)
    def _():
        first, second = ids_ref[0], ids_ref[1]
        named = (first == mine) | (second == mine)
        before = hot(iota((length, length), 0) < iota((length, length), 1))
        place = dot(hot(named), before).astype(jnp.int32)
        slot_ref[...] = jnp.where(named, place, -1)
        partner_ref[...] = jnp.where(first == mine, second, first).astype(F32)
        for d in range(near):
            at = slice(d * capacity, (d + 1) * capacity)
            source = pl.ds((base + d) ^ (kind * near), 1)
            here = iota((capacity, length), 0) == slot_ref[source, :]
            other_ref[at, :] = jnp.sum(
                jnp.where(here, partner_ref[source, :], 0.0), axis=1, keepdims=True
            ).astype(jnp.int32)
        lane = iota((total, LANES), 1)
        logits = dot(sent_ref[...].reshape(total, -1), router_ref[...])
        gap = jnp.sum(
            jnp.where(lane == mine, logits, 0.0) - jnp.where(lane == other_ref[...], logits, 0.0),
            axis=1, keepdims=True,
        )
        small = jnp.exp(-jnp.abs(gap))
        gate = jnp.where(gap >= 0, 1.0, small) / (1.0 + small)
        gate_ref[...] = gate
        scaled_ref[...] = (gate * cots_ref[...].reshape(total, -1).astype(F32)).astype(BF16)

    first_weight, last_weight = first_ref[...], last_ref[...]
    rows = sent_ref[...].reshape(total, -1)
    scaled = scaled_ref[...]
    up = dot(rows, first_weight)
    grad_act = dot_nt(scaled, last_weight)
    square = up * up
    half = 0.5 * jnp.tanh(up * (gelu_a + (gelu_a * gelu_b) * square)) + 0.5
    act = up * half
    slope = half + (act * (1.0 - half)) * (2 * gelu_a + (6 * gelu_a * gelu_b) * square)
    act_low = act.astype(BF16)
    grad_up = (grad_act * slope).astype(BF16)
    act_ref[...] = act_low
    grad_up_ref[...] = grad_up
    out_part = dot(act_low, last_weight)
    back_part = dot_nt(grad_up, first_weight)

    @pl.when(step == 0)
    def _():
        out_acc[...] = out_part
        back_acc[...] = back_part

    @pl.when(step > 0)
    def _():
        out_acc[...] += out_part
        back_acc[...] += back_part

    @pl.when(step == pl.num_programs(0) - 1)
    def _():
        grad_router = jnp.zeros(grad_router_ref.shape, F32)
        copies = []
        for d in range(near):
            at = slice(d * capacity, (d + 1) * capacity)
            produced = out_acc[at, :].astype(BF16).astype(F32)
            gate = gate_ref[at, :]
            here = pl.ds(part * capacity, capacity)
            out_ref[at, :] = (gate * produced).astype(BF16)
            copies.append(pltpu.make_async_copy(out_ref.at[at, :], all_ref.at[d, here, :], sem.at[0, d]))
            copies[-1].start()
            grad_gate = jnp.sum(cots_ref[d].astype(F32) * produced, axis=1, keepdims=True)
            share = gate * (1.0 - gate) * grad_gate
            lane = iota((capacity, LANES), 1)
            signed = jnp.where(lane == mine, share, 0.0) - jnp.where(lane == other_ref[at, :], share, 0.0)
            high = signed.astype(BF16)
            rest = (signed - high.astype(F32)).astype(BF16)
            routed = dot(high, router_turned_ref[...]) + dot(rest, router_turned_ref[...])
            back = (back_acc[at, :] + routed).astype(BF16)
            if kind:
                for e in range(near):
                    @pl.when((mine % near) ^ d == e)
                    def _():
                        back_refs[e][...] = back
            else:
                back_ref[at, :] = back
                copies.append(pltpu.make_async_copy(back_ref.at[at, :], back_refs[0].at[d, here, :], sem.at[1, d]))
                copies[-1].start()
            rows = sent_ref[d]
            grad_router = grad_router + dot_tn(rows, high) + dot_tn(rows, rest)
        grad_router_ref[...] = grad_router
        for copy in copies:
            copy.wait()


def expert_grad_kernel(parts, flat, half_ref, *refs):
    total = None
    for a_ref, b_ref in zip(refs[:parts], refs[parts : 2 * parts]):
        a, b = a_ref[...], b_ref[...]
        product = dot_tn(a.reshape(-1, a.shape[-1]), b)
        total = product if total is None else total + product
    if len(refs) > 2 * parts + 1:
        total = total + refs[2 * parts][...].astype(F32)
    refs[-1][...] = total.astype(BF16)


def join_kernel(odd_ref, mine_ref, other_ref, out_ref):
    own = pl.program_id(0) == odd_ref[0]
    out_ref[...] = jnp.where(own, mine_ref[...], other_ref[...]).astype(F32)


def dense_grad_kernel(n0, n1, g0, g1, m0, m1, b0, b1, small, left_ref, right_ref):
    width = n0.shape[1]
    left_ref[...] = (dot_tn(n0[...], g0[:, : 2 * width]) + dot_tn(n1[...], g1[:, : 2 * width])).astype(BF16)
    right_ref[:, :width] = (dot_tn(n0[...], g0[:, 2 * width :]) + dot_tn(n1[...], g1[:, 2 * width :])).astype(BF16)
    right_ref[:, width : 2 * width] = (dot_tn(m0[...], b0[...]) + dot_tn(m1[...], b1[...])).astype(BF16)
    right_ref[:, 2 * width :] = small[...]


def combine_kernel(out_ref, far_ref, mine_ref, col_ref, hidden_ref, result_ref, pick_ref):
    near, capacity, _ = out_ref.shape
    fill_pick(col_ref, pick_ref, mine_ref[0, 0] // near * near * capacity)
    rows = out_ref[...].reshape(near * capacity, -1)
    summed = dot(pick_ref[...], rows) + far_ref[...].astype(F32)
    result_ref[...] = (hidden_ref[...] + summed).astype(BF16)


def cost(flops, byte_count, transcendentals=0):
    return pl.CostEstimate(flops=int(SCALE * flops), bytes_accessed=int(byte_count), transcendentals=int(transcendentals))


def shaped(shape, dtype):
    return jax.ShapeDtypeStruct(shape, dtype)


def later(kernel, count, ties):
    if not ties:
        return kernel
    return lambda *refs: kernel(*refs[:count], *refs[count + ties :])


def make_strip(base, after):
    heads, width = base.shape
    return pl.pallas_call(
        later(strip_kernel, 1, len(after)),
        in_specs=[VECTOR] + [ANYWHERE] * len(after),
        out_shape=shaped((heads, STRIP, width - STRIP), BF16),
        compiler_params=params(),
        cost_estimate=cost(0, 0),
    )(base, *after)


def place(ids, far_ids, mine, experts, near, capacity):
    length = ids.shape[0]
    row, col = shaped((2, length), jnp.int32), shaped((length, 2), jnp.int32)
    return pl.pallas_call(
        functools.partial(slots_kernel, experts, near, capacity),
        out_shape=(row, row, col, col),
        in_specs=[VECTOR] * 4 + [SCALAR],
        compiler_params=params(),
        cost_estimate=cost(0, 0),
    )(ids.T, ids, far_ids, far_ids.T, mine)


def scatter(near, capacity, *parts, after=()):
    slots = [part[0] for part in parts]
    values = [value for part in parts for value, _ in part[1]]
    picks = [[pick for _, pick in part[1]] for part in parts]
    length, width = slots[0].shape[1], values[0].shape[-1]
    total = near * capacity * len(parts)
    return pl.pallas_call(
        later(functools.partial(scatter_kernel, picks), len(slots) + len(values), len(after)),
        in_specs=[VECTOR] * (len(slots) + len(values)) + [ANYWHERE] * len(after),
        out_shape=shaped((near, capacity * len(parts), width), BF16),
        compiler_params=params(),
        cost_estimate=cost(2 * total * length * width, 6e6),
    )(*slots, *values, *after)


def gather(col, base, blocks, after):
    length, width = col[0].shape[0], blocks.shape[2]
    near, capacity = blocks.shape[0], blocks.shape[1] // 2
    total = near * capacity
    return pl.pallas_call(
        later(gather_kernel, 4, len(after)),
        out_shape=(shaped((length, width), BF16), shaped((length, width), BF16)),
        in_specs=[VECTOR] * 2 + [SCALAR, VECTOR] + [ANYWHERE] * len(after),
        scratch_shapes=[pltpu.VMEM((length, total), BF16), pltpu.VMEM((total, width), BF16)],
        compiler_params=params(),
        cost_estimate=cost(4 * total * length * width, 6e6),
    )(*col, base, blocks, *after)


def forward(m, x, gains, weight, strip, block_row, block_col, row_slots, near, capacity, after):
    _, length, width = x.shape
    heads = width // HEAD
    return pl.pallas_call(
        later(functools.partial(forward_kernel, m), 7, len(after)),
        in_specs=[VECTOR] * 7 + [ANYWHERE] * len(after),
        out_shape=(
            shaped((length, 3 * width), BF16),
            shaped((length, width), BF16),
            shaped((heads, length, 1), F32),
            shaped((length, width), F32),
            shaped((length, width), BF16),
            shaped((near, capacity, width), BF16),
        ),
        compiler_params=params(),
        cost_estimate=cost(
            2 * length * width * 4 * width + 8 * heads * length * length * HEAD,
            24e6, heads * length * length,
        ),
    )(x, gains, weight, strip, block_row, block_col, row_slots, *after)


def backward(
    part, own, far, mine, col, cot, hidden, gains, weight, proj, totals, strip, block_row, block_col, x, after
):
    _, length, width = x.shape
    heads = width // HEAD
    near, capacity = own.shape[0], own.shape[1] // 2
    total = 2 * near * capacity
    return pl.pallas_call(
        later(functools.partial(backward_kernel, near, part), near + 13, len(after)),
        in_specs=[VECTOR] * (near + 1) + [SCALAR] + [VECTOR] * 11 + [ANYWHERE] * len(after),
        out_shape=(
            shaped((length, width), BF16),
            shaped((length, width), BF16),
            shaped((length, 3 * width), BF16),
            shaped((length, width), BF16),
            shaped((2, width), F32),
            shaped((heads, 2 * length), F32),
        ),
        scratch_shapes=[
            pltpu.VMEM((length, total), BF16),
            pltpu.VMEM((total, width), BF16),
            pltpu.VMEM((length, width), BF16),
            pltpu.VMEM((length, length), BF16),
            pltpu.VMEM((length, length), BF16),
            pltpu.VMEM((STRIP, 2 * length), F32),
        ],
        compiler_params=params(),
        cost_estimate=cost(
            2 * length * width * 4 * width + 20 * heads * length * length * HEAD + 2 * total * length * width,
            30e6, heads * length * length,
        ),
    )(*far, own, mine, col, cot, hidden, gains, weight, proj, totals, strip, block_row, block_col, x, *after)


def block_of(count, near, capacity, width, index):
    return pl.BlockSpec((near, capacity, width), lambda f: (0, index, 0), pipeline_mode=pl.Buffered(1))


def expert(kind, part, sent, cots, ids, mine, router, router_turned, first, last, earlier, after):
    (sent, sent_block), (cots, cot_block) = sent, cots
    near, _, width = sent.shape
    experts = ids.shape[1]
    capacity = 3 * ids.shape[2] // experts
    total = near * capacity
    inner = first.shape[1]
    step = 768

    def whole(shape):
        return pl.BlockSpec(shape, lambda f: (0,) * len(shape), pipeline_mode=pl.Buffered(1))

    anywhere = pl.BlockSpec(memory_space=pl.ANY)
    shared = shaped((near, 2 * capacity, width), BF16)
    if kind:
        back_specs = tuple(whole((capacity, width)) for _ in range(near))
        back_shapes = tuple(shaped((capacity, width), BF16) for _ in range(near))
    else:
        back_specs, back_shapes = (anywhere,), (shared,)
    count = len(back_specs)
    alias = len(earlier)
    targets = (count,) if kind else (0, 1)
    outs = pl.pallas_call(
        later(functools.partial(expert_kernel, kind, near, alias, part), 8 + alias, len(after)),
        grid=(inner // step,),
        in_specs=[
            block_of(0, near, capacity, width, sent_block), block_of(0, near, capacity, width, cot_block),
            whole(ids.shape), SCALAR, whole(router.shape), whole(router_turned.shape),
            pl.BlockSpec((width, step), lambda f: (0, f)),
            pl.BlockSpec((step, width), lambda f: (f, 0)),
        ] + [anywhere] * (alias + len(after)),
        out_specs=back_specs + (
            anywhere,
            pl.BlockSpec((total, step), lambda f: (0, f)),
            pl.BlockSpec((total, step), lambda f: (0, f)),
            whole((total, width)), whole((width, LANES)),
        ),
        out_shape=back_shapes + (
            shared,
            shaped((total, inner), BF16), shaped((total, inner), BF16),
            shaped((total, width), BF16), shaped((width, LANES), F32),
        ),
        scratch_shapes=[
            pltpu.VMEM((total, 1), F32),
            pltpu.VMEM((total, 1), jnp.int32),
            pltpu.VMEM((total, width), F32),
            pltpu.VMEM((total, width), F32),
            pltpu.VMEM(ids.shape[1:], jnp.int32),
            pltpu.VMEM(ids.shape[1:], F32),
            pltpu.VMEM((total, width), BF16),
            pltpu.VMEM((total, width), BF16),
            pltpu.SemaphoreType.DMA((2, near)),
        ],
        input_output_aliases={8 + n: target for n, target in enumerate(targets)} if alias else {},
        compiler_params=params(dimension_semantics=("arbitrary",)),
        cost_estimate=cost(8 * total * width * inner, 30e6, total * inner),
    )(sent, cots, ids, mine, router, router_turned, first, last, *earlier, *after)
    backs = list(outs[:count])
    return (backs if kind else backs[0]), outs[count], outs[count + 1 :]


def last_grad(half, acts, scaled, received, after):
    total, inner = acts[0].shape
    width = scaled[0].shape[1]
    step = 512
    count = inner // 2 // step
    out_spec = pl.BlockSpec((step, width), lambda f, half: (f, 0))
    specs = [pl.BlockSpec((total, step), lambda f, half: (0, half[0] * count + f))] * len(acts)
    specs += [pl.BlockSpec((total, width), lambda f, half: (0, 0))] * len(acts)
    extra = [] if received is None else [received]
    return pl.pallas_call(
        later(functools.partial(expert_grad_kernel, len(acts), True), 1 + 2 * len(acts) + len(extra), len(after)),
        grid_spec=pltpu.PrefetchScalarGridSpec(
            num_scalar_prefetch=1, grid=(count,), in_specs=specs + [out_spec] * len(extra) + [ANYWHERE] * len(after),
            out_specs=out_spec
        ),
        out_shape=shaped((inner // 2, width), BF16),
        compiler_params=params(dimension_semantics=("arbitrary",)),
        cost_estimate=cost(len(acts) * total * inner * width, 15e6),
    )(half, *acts, *scaled, *extra, *after)


def first_grad(half, rows, ups, received, after):
    total, inner = ups[0].shape
    near, _, width = rows[0][0].shape
    capacity = total // near
    step = 768
    out_spec = pl.BlockSpec((width // 2, step), lambda f, half: (0, f))

    def row_spec(block):
        return pl.BlockSpec((near, capacity, width // 2), lambda f, half: (0, block, half[0]))

    specs = [row_spec(block) for _, block in rows]
    specs += [pl.BlockSpec((total, step), lambda f, half: (0, f))] * len(ups)
    extra = [] if received is None else [received]
    return pl.pallas_call(
        later(functools.partial(expert_grad_kernel, len(ups), False), 1 + 2 * len(ups) + len(extra), len(after)),
        grid_spec=pltpu.PrefetchScalarGridSpec(
            num_scalar_prefetch=1, grid=(inner // step,), in_specs=specs + [out_spec] * len(extra) + [ANYWHERE] * len(after),
            out_specs=out_spec
        ),
        out_shape=shaped((width // 2, inner), BF16),
        compiler_params=params(dimension_semantics=("arbitrary",)),
        cost_estimate=cost(len(ups) * total * inner * width, 25e6),
    )(half, *[array for array, _ in rows], *ups, *extra, *after)


def join(odd, mine, other):
    rows, columns = mine.shape
    step = rows // 3
    spec = pl.BlockSpec((step, columns), lambda h, i, odd: (i, 0))
    return pl.pallas_call(
        join_kernel,
        grid_spec=pltpu.PrefetchScalarGridSpec(
            num_scalar_prefetch=1, grid=(2, 3), in_specs=[spec, spec],
            out_specs=pl.BlockSpec((step, columns), lambda h, i, odd: (h * 3 + i, 0)),
        ),
        out_shape=shaped((2 * rows, columns), F32),
        compiler_params=params(dimension_semantics=("arbitrary", "arbitrary")),
        cost_estimate=cost(rows * columns, 20e6),
    )(odd, mine, other)


def dense_grad(*arrays, after):
    small = arrays[-1]
    width = arrays[0].shape[1]
    length = arrays[0].shape[0]
    return pl.pallas_call(
        later(dense_grad_kernel, len(arrays), len(after)),
        in_specs=[VECTOR] * len(arrays) + [ANYWHERE] * len(after),
        out_shape=(shaped((width, 2 * width), BF16), shaped((width, 2 * width + small.shape[1]), BF16)),
        compiler_params=params(),
        cost_estimate=cost(4 * length * width * 4 * width, 20e6),
    )(*arrays, *after)


def combine(out_rows, part, far, mine, col, hidden):
    length, width = hidden.shape
    near, capacity = out_rows.shape[0], out_rows.shape[1] // 2
    total = near * capacity
    plain = pl.BlockSpec((length, width), lambda f: (0, 0))
    return pl.pallas_call(
        combine_kernel,
        grid=(1,),
        in_specs=[
            block_of(0, near, capacity, width, part), plain, SCALAR, pl.BlockSpec(col.shape, lambda f: (0, 0)), plain,
        ],
        out_specs=plain,
        out_shape=shaped((length, width), BF16),
        scratch_shapes=[pltpu.VMEM((length, total), BF16)],
        compiler_params=params(),
        cost_estimate=cost(2 * total * length * width, 6e6),
    )(out_rows, far, mine, col, hidden)


def swap(value, axis, size, bit):
    return lax.ppermute(value, axis, [(i, i ^ bit) for i in range(size)])


def pair_sum(a, b):
    return (a.astype(F32) + b.astype(F32)).astype(BF16)


def halve(value, axis, name, size, bit):
    odd = (lax.axis_index(name) & bit) > 0
    count = value.shape[axis] // 2
    low = lax.slice_in_dim(value, 0, count, axis=axis)
    high = lax.slice_in_dim(value, count, 2 * count, axis=axis)
    kept, sent = jnp.where(odd, high, low), jnp.where(odd, low, high)
    return pair_sum(kept, swap(sent, name, size, bit))


def unite(value, name, size, bit):
    odd = (lax.axis_index(name) & bit) > 0
    other = swap(value, name, size, bit)
    return jnp.concatenate([jnp.where(odd, other, value), jnp.where(odd, value, other)], axis=0)


def dense_sum(left, right, dp, experts, after):
    def split(value):
        return halve(value.reshape(dp // 2, 2, value.shape[0] // dp, value.shape[1]), 1, "dp", dp, 1)[:, 0]

    def along_dp(value):
        bit = 2
        while bit < dp:
            shape = value.shape
            value = halve(value.reshape(shape[0] // 2, 2, *shape[1:]), 1, "dp", dp, bit)[:, 0]
            bit *= 2
        return value

    left, right = split(left), split(right)
    left = after(0, along_dp(left))
    right = halve(right, 1, "expert", experts, 1)
    left = halve(left, 1, "expert", experts, 1)
    right = along_dp(right)
    rows = after(1, jnp.concatenate([left[0], right[0]], axis=1))
    step, bit = 2, 2
    while bit < experts:
        rows = after(step, halve(rows, 0, "expert", experts, bit))
        step, bit = step + 1, bit * 2
    while bit > 1:
        bit //= 2
        rows = unite(rows, "expert", experts, bit)
        if bit == 2:
            rows = after(9, rows)
    return rows.astype(F32)


def body(
    dp, experts, inputs, gain_one, w_qkv, w_out, rel_table, second_norm_gain, w_router, w_in, w_back,
    expert_ids, block_ids, cotangent,
):
    micro, length, width = inputs.shape
    capacity = 3 * length // experts
    near = experts // 2
    buckets, heads = rel_table.shape[0] * dp, rel_table.shape[1]
    shard = gain_one.shape[0]
    first_in, last_out = w_in[0], w_back[0]
    mine = lax.axis_index("expert").astype(jnp.int32).reshape(1, 1)

    groups = [list(range(near)), list(range(near, experts))]
    odd = (lax.axis_index("dp") & 1).astype(jnp.int32).reshape(1)

    def cross(value, bit):
        return swap(value, "expert", experts, bit)

    def around(blocks):
        return lax.all_to_all(
            blocks, "expert", split_axis=0, concat_axis=0, axis_index_groups=groups, tiled=True
        )

    def order(*values):
        return lax.optimization_barrier(values)

    middle = length // 2
    cot0_top, cot0_end = cross(cotangent[0, :middle], near), cross(cotangent[0, middle:], near)

    ids_row = jnp.transpose(expert_ids, (0, 2, 1))
    ids_all = lax.all_to_all(
        jnp.broadcast_to(ids_row[None], (experts,) + ids_row.shape), "expert", split_axis=0, concat_axis=0, tiled=True
    )
    ids_all = jnp.transpose(ids_all, (1, 2, 0, 3))
    ids_far = lax.dynamic_index_in_dim(ids_all, lax.axis_index("expert") ^ near, 2, keepdims=False)

    table_column = jnp.pad(rel_table.reshape(-1), (0, shard - rel_table.size))
    small = jnp.concatenate([gain_one[:, None], second_norm_gain[:, None], table_column[:, None], w_router], axis=1)
    extra = jnp.pad(small, ((0, 0), (0, LANES - small.shape[1])))
    bit = 1
    while bit < dp:
        other = swap(extra, "dp", dp, bit)
        high = (lax.axis_index("dp") & bit) > 0
        extra = jnp.concatenate([jnp.where(high, other, extra), jnp.where(high, extra, other)], axis=0)
        bit *= 2
    packed = lax.all_gather(jnp.concatenate([w_qkv, w_out], axis=1), "dp", axis=0, tiled=True)
    gains = extra[:, :2].astype(F32).T
    table = extra[:, 2].reshape(dp, shard)[:, : rel_table.size].reshape(buckets, heads)
    router = jnp.pad(extra[:, 3 : 3 + experts], ((0, 0), (0, LANES - experts)))
    router_turned = router.T
    levels = bucket_table(length, buckets)
    base = lax.dot_general(
        table, jnp.asarray(levels, BF16), (((0,), (0,)), ((), ())), preferred_element_type=F32
    )
    strip = make_strip(base, [])
    places = [place(expert_ids[m], ids_far[m], mine, experts, near, capacity) for m in range(micro)]

    kept = []
    block_cols = block_ids[:, 0, :].T

    def layer_front(m, after):
        block_row, block_col = block_ids, block_cols
        proj, mixed, totals, hidden, second, send = forward(
            m, inputs, gains, packed, strip, block_row, block_col, places[m][0], near, capacity, after
        )
        kept.append((proj, mixed, totals, hidden, block_row, block_col))
        return second, send

    cot_own = around(
        scatter(near, capacity, (places[0][0], [(cotangent, 0)]), (places[1][0], [(cotangent, 1)]), after=[cot0_top, strip])
    )
    second0, send0 = layer_front(0, [])
    second0_far = cross(second0, near)
    own0 = around(send0)
    second1, send1 = layer_front(1, [send0, cot0_end])
    own1 = around(send1)

    common = (mine, router, router_turned, first_in, last_out)
    cot1_far = cross(order(cotangent[1], second0_far, send1)[0], near)
    back_own, out_own, kept0_own = expert(
        0, 0, (own0, 0), (cot_own, 0), ids_all[0], *common, (), [second0_far, send1]
    )
    second1_far = cross(order(second1, second0_far)[0], near)
    far0_send = scatter(
        near, capacity, (places[0][1], [(cot0_top, None), (cot0_end, None)]), (places[0][1], [(second0_far, None)]),
        after=[out_own],
    )
    far0 = around(far0_send)
    back_own, out_own, kept1_own = expert(
        0, 1, (own1, 0), (cot_own, 1), ids_all[1], *common, (back_own, out_own), [far0_send]
    )
    far1_send = scatter(
        near, capacity, (places[1][1], [(cot1_far, None)]), (places[1][1], [(second1_far, None)]), after=[out_own],
    )
    far1 = around(far1_send)
    back0_far, out_far, kept0_far = expert(1, 0, (far0, 1), (far0, 0), ids_all[0], *common, (), [far1_send])
    back1_far, out_far, kept1_far = expert(1, 1, (far1, 1), (far1, 0), ids_all[1], *common, (out_far,), [])
    back_own, out_own, _ = order(back_own, out_own, back0_far[0])
    back_own, out_own, out_far = around(back_own), around(out_own), around(out_far)
    home = [
        [cross(block, near | d) for d, block in enumerate(back0_far)],
        [cross(block, near | d) for d, block in enumerate(back1_far)],
    ]
    quarter = max(1, near // 4)

    parts = (kept0_own, kept1_own, kept0_far, kept1_far)
    acts, ups, scaled, routers = zip(*parts)
    rows = ((own0, 0), (own1, 0), (far0, 1), (far1, 1))
    grad_router = sum(routers)[:, :experts]

    home0, home1 = home
    other = 1 - odd
    last_part = last_grad(other, acts, scaled, None, home0[: 2 * quarter] + [back_own])
    last_got = swap(last_part, "dp", dp, 1)
    first_part = first_grad(other, rows, ups, None, [last_part] + home0[2 * quarter : 3 * quarter])
    first_got = swap(first_part, "dp", dp, 1)
    last_sum = last_grad(odd, acts, scaled, last_got, [first_part] + home0[3 * quarter :])
    first_sum = first_grad(odd, rows, ups, first_got, [last_sum] + home1[:quarter])
    first_whole = first_sum

    def over_dp(value):
        bit = 2
        while bit < dp:
            other = swap(value, "dp", dp, bit)
            value = pair_sum(value, other)
            bit *= 2
        return value, other

    def pieces(value):
        count = value.shape[0] // 4
        return [value[n * count : (n + 1) * count] for n in range(4)]

    last_sum, last_came = zip(*[over_dp(piece) for piece in pieces(last_sum)])
    first_sum = pieces(first_sum)
    first_sum[0], first_came = over_dp(first_sum[0])

    def layer_back(m, after):
        proj, mixed, totals, hidden, block_row, block_col = kept[m]
        return backward(
            m, back_own, home[m], mine, places[m][2], cotangent, hidden, gains, packed, proj, totals, strip,
            block_row, block_col, inputs, after,
        )

    back_outs = [layer_back(0, [first_whole, last_came[0]] + home1[quarter : 2 * quarter])]
    out_sums = gather((places[0][3], places[1][3]), mine, out_far, [back_outs[0][1]])
    out0_far, out1_far = cross(out_sums[0], near), cross(out_sums[1], near)
    back_outs.append(layer_back(1, [last_came[1], last_came[2], out_sums[0]]))

    gain_grads = back_outs[0][4] + back_outs[1][4]
    diagonals = back_outs[0][5] + back_outs[1][5]
    table_grad = lax.dot_general(
        jnp.asarray(levels, F32), diagonals, (((1,), (1,)), ((), ())),
        precision=lax.Precision.HIGHEST, preferred_element_type=F32,
    )
    table_grad = jnp.pad(table_grad.reshape(dp, rel_table.size), ((0, 0), (0, shard - rel_table.size)))
    small_grad = jnp.concatenate([gain_grads.T, table_grad.reshape(width, 1), grad_router], axis=1).astype(BF16)
    small_grad = jnp.pad(small_grad, ((0, 0), (0, LANES - small_grad.shape[1])))
    left, right = dense_grad(
        back_outs[0][3], back_outs[1][3], back_outs[0][2], back_outs[1][2],
        kept[0][1], kept[1][1], back_outs[0][1], back_outs[1][1], small_grad,
        after=[last_came[3], first_came, out0_far, out_own],
    )
    results = [combine(out_own, 0, out0_far, mine, places[0][2], kept[0][3])]
    last_sum = jnp.concatenate(last_sum, axis=0)
    grad_last = join(odd, last_sum, swap(last_sum, "dp", dp, 1))
    grad_first = None

    def after(step, value):
        nonlocal grad_first, grad_last, first_sum, out1_far
        if step == 0:
            value, results[0] = order(value, results[0])
        if step == 1:
            value, grad_last, out1_far, *rest = order(value, grad_last, out1_far, *first_sum[1:])
            results.append(combine(out_own, 1, out1_far, mine, places[1][2], kept[1][3]))
            both = jnp.concatenate(first_sum[:1] + [over_dp(piece)[0] for piece in rest], axis=0)
            grad_first = join(odd, both, swap(both, "dp", dp, 1))
        if step == 3:
            value, results[1] = order(value, results[1])
        if step == 9:
            value, grad_first = order(value, grad_first)
        return value

    dense = dense_sum(left, right, dp, experts, after)
    tail = dense[:, 4 * width :]
    return (
        jnp.stack(results),
        jnp.stack([out[0] for out in back_outs]),
        tail[:, 0],
        dense[:, : 3 * width],
        dense[:, 3 * width : 4 * width],
        tail[: rel_table.size, 2].reshape(rel_table.shape),
        tail[:, 1],
        tail[:, 3 : 3 + experts],
        grad_first[None],
        grad_last[None],
    )


def solution(mesh):
    split = P(None, ("dp", "expert"), None)
    in_specs = (
        split, P("dp"), P("dp", None), P("dp", None), P("dp", None), P("dp"), P("dp", None),
        P("expert", None, None), P("expert", None, None), split, split, split,
    )
    out_specs = (
        split, split, P("dp"), P("dp", None), P("dp", None), P("dp", None), P("dp"), P("dp", None),
        P("expert", None, None), P("expert", None, None),
    )
    return jax.shard_map(
        functools.partial(body, mesh.shape["dp"], mesh.shape["expert"]), mesh=mesh, in_specs=in_specs, out_specs=out_specs, check_vma=False
    )
```

time: 827 us -> 621 us (0.75)
  waiting for transfers between devices: 277 us -> 116 us
  blocking collectives: 151 us -> 0 us
  starting transfers between devices: 38.3 us -> 91.2 us
  Pallas kernels: 288 us -> 329 us
  other arithmetic: 20.9 us -> 31.2 us
    psum x2 -> x0, waiting for transfers between devices: 144 us -> none  [the longest x1 73.1 us: body(): dense = lax.psum(dense, 'expert').astype(F32)]
    all_to_all x8 -> x9, waiting for transfers between devices: 132 us -> 47.1 us  [the longest x8 47 us: around(): lax.all_to_all(blocks, 'expert', split_axis=0, concat_axis=0, axis_index_...]
    psum x1 -> x0, blocking collectives: 77.8 us -> none  [body(): lax.psum(expert_outs[0][5][:, :experts] + expert_outs[1][5][:, :experts],...]
    all_gather x1 -> x0, blocking collectives: 73.4 us -> none  [body(): ids_all = lax.all_gather(ids_row, 'expert', axis=0, tiled=False)]
    ppermute x0 -> x40, waiting for transfers between devices: none -> 69.1 us  [swap(): return lax.ppermute(value, axis, [(i, i ^ bit) for i in range(size)])]
    ppermute x0 -> x40, starting transfers between devices: none -> 50.4 us  [swap(): return lax.ppermute(value, axis, [(i, i ^ bit) for i in range(size)])]
    pallas_call x14 -> x24, Pallas kernels: 288 us -> 329 us  [the longest x4 109 us: expert(): pl.pallas_call(later(functools.partial(expert_kernel, kind, near, alias,...]
    broadcast_in_dim x2 -> x0, other arithmetic: 12 us -> none  [the longest x1 7.52 us: body(): grad_first[None]]
  transfers between devices with their start and end apart: 12 -> 50, of which waited for: 7 -> 19; matrix products, arithmetic and copies ran while one was open for 3% -> 7% of each run, Pallas kernels for 30% -> 51%
where the time goes in v2:
time: 621 us; the launch traced here: 611 us
  Pallas kernels  329 us (53%)
  waiting for transfers between devices  116 us (19%)
  starting transfers between devices  91.2 us (15%)
  other arithmetic  31.2 us (5%)
  local copies, waits for them, and re-layouts  25.9 us (4%)
  between operations  15.3 us (2%)
    pallas_call x4, Pallas kernels, expert(): pl.pallas_call(later(functools.partial(expert_kernel, kind, near, alias,...  109 us
    ppermute x40, waiting for transfers between devices, swap(): return lax.ppermute(value, axis, [(i, i ^ bit) for i in range(size)])  69.1 us
    pallas_call x2, Pallas kernels, backward(): pl.pallas_call(later(functools.partial(backward_kernel, near, part), near...  62.9 us
    ppermute x40, starting transfers between devices, swap(): return lax.ppermute(value, axis, [(i, i ^ bit) for i in range(size)])  50.4 us
    all_to_all x8, waiting for transfers between devices, around(): lax.all_to_all(blocks, 'expert', split_axis=0, concat_axis=0, axis_index_...  47 us
    pallas_call x2, Pallas kernels, forward(): pl.pallas_call(later(functools.partial(forward_kernel, m), 7, len(after))...  43.9 us
    all_to_all x8, starting transfers between devices, around(): lax.all_to_all(blocks, 'expert', split_axis=0, concat_axis=0, axis_index_...  33.9 us
    pallas_call x2, Pallas kernels, first_grad(): pl.pallas_call(later(functools.partial(expert_grad_kernel, len(ups), Fals...  26 us
  transfers between devices with their start and end apart: 50, of which 19 were waited for; matrix products, arithmetic and copies ran while one was open for 7% of the time, Pallas kernels for 51%

profile of v2, /device:TPU:0, one launch (start us, length us, event | category | flops | bytes accessed | tf_op | source)
XLA Modules:
  0.0 610.8 jit_solution(4446695499661379667)
XLA Ops:
  11.2 6.8 %all-to-all-start = ((s32[8,2,2,512]{3,2,1,0:T(2,128)}), s32[8,2,2,512]{3,2,1,0:T(2,128)S(1)}, u32[]{:S(2)}, u32[]{:S(2)}) async-start(s32[8,2,2,512]{3,2,1,0:T(2,128)} %broadcast_in_dim.21), calls=%async_computation | async-start | bytes 131072 | tf_op jit(solution)/shard_map/all_to_all | solution.py:791
  57.0 21.9 %shard_map.215 = (bf16[512,2304]{1,0:T(8,128)(2,1)}, bf16[512,768]{1,0:T(8,128)(2,1)}, f32[12,512,1]{2,1,0:T(8,128)}, f32[512,768]{1,0:T(8,128)}, bf16[512,768]{...) custom-call(bf16[2,512,768]{2,1,0:T(8,128)(2,1)} %refs_16_.3, f32[2,768]{1,0:T(2,128)} %convert_bitcast_fusion.gains_ref.refs_1_.refs_9_, ...), custom_call_target="tpu_custom_call" | custom-call | flops 20132659200 | bytes 24000000 | tf_op jit(solution)/shard_map/pallas_call | solution.py:496
  89.7 22.0 %shard_map.218 = (bf16[512,2304]{1,0:T(8,128)(2,1)}, bf16[512,768]{1,0:T(8,128)(2,1)}, f32[12,512,1]{2,1,0:T(8,128)}, f32[512,768]{1,0:T(8,128)}, bf16[512,768]{...) custom-call(bf16[2,512,768]{2,1,0:T(8,128)(2,1)} %refs_16_.3, f32[2,768]{1,0:T(2,128)} %convert_bitcast_fusion.gains_ref.refs_1_.refs_9_, ...), custom_call_target="tpu_custom_call" | custom-call | flops 20132659200 | bytes 24000000 | tf_op jit(solution)/shard_map/pallas_call | solution.py:496
  111.7 9.2 %collective-permute-done.4.refs_8_.refs_4_ = bf16[512,768]{1,0:T(8,128)(2,1)} collective-permute-done((bf16[512,768]{1,0:T(8,128)(2,1)}, bf16[512,768]{1,0:T(8,128)(2,1)}, u32[]{:S(2)}, u32[]{:S(2)}) %collective-permute-start.4) | collective-permute-done | bytes 786464 | tf_op jit(solution)/shard_map/ppermute | solution.py:709
  127.4 26.7 %shard_map.219 = (bf16[4,384,768]{2,1,0:T(8,128)(2,1)}, bf16[4,384,768]{2,1,0:T(8,128)(2,1)}, bf16[768,3072]{1,0:T(8,128)(2,1)}, bf16[768,3072]{1,0:T(8,128)(2,1...) custom-call(bf16[4,192,768]{2,1,0:T(8,128)(2,1)} %copy-done.14, bf16[4,384,768]{2,1,0:T(8,128)(2,1)} %copy-done.12, ...), custom_call_target="tpu_custom_call" | custom-call | flops 72477573120 | bytes 30000000 | tf_op jit(solution)/shard_map/pallas_call | solution.py:575
  158.3 9.7 %all-to-all-done.4.refs_0_.refs_2_ = bf16[4,192,768]{2,1,0:T(8,128)(2,1)S(1)} async-done(((bf16[4,192,768]{2,1,0:T(8,128)(2,1)}), bf16[4,192,768]{2,1,0:T(8,128)(2,1)S(1)}, u32[]{:S(2)}, u32[]{:S(2)}) %all-to-all-start.4) | async-done | bytes 1179680 | tf_op jit(solution)/shard_map/all_to_all | solution.py:780
  173.9 26.7 %shard_map.221 = (bf16[4,384,768]{2,1,0:T(8,128)(2,1)}, bf16[4,384,768]{2,1,0:T(8,128)(2,1)}, bf16[768,3072]{1,0:T(8,128)(2,1)}, bf16[768,3072]{1,0:T(8,128)(2,1...) custom-call(bf16[4,192,768]{2,1,0:T(8,128)(2,1)} %copy-done.15, ...), custom_call_target="tpu_custom_call", output_to_operand_aliasing={{0}: (8, {}), {1}: (9, {})} | custom-call | flops 72477573120 | bytes 30000000 | tf_op jit(solution)/shard_map/pallas_call | solution.py:575
  204.9 10.6 %all-to-all-done.3.refs_0_.refs_1_.refs_3_ = bf16[4,384,768]{2,1,0:T(8,128)(2,1)S(1)} async-done(((bf16[4,384,768]{2,1,0:T(8,128)(2,1)}), bf16[4,384,768]{2,1,0:T(8,128)(2,1)S(1)}, u32[]{:S(2)}, u32[]{:S(2)}) %all-to-all-start.3) | async-done | bytes 2359328 | tf_op jit(solution)/shard_map/all_to_all | solution.py:780
  220.2 28.0 %shard_map.223 = (bf16[192,768]{1,0:T(8,128)(2,1)}, bf16[192,768]{1,0:T(8,128)(2,1)}, bf16[192,768]{1,0:T(8,128)(2,1)}, bf16[192,768]{1,0:T(8,128)(2,1)}, bf16[4...) custom-call(bf16[4,384,768]{2,1,0:T(8,128)(2,1)} %copy-done.11, ...), custom_call_target="tpu_custom_call" | custom-call | flops 72477573120 | bytes 30000000 | tf_op jit(solution)/shard_map/pallas_call | solution.py:575
  259.8 28.0 %shard_map.224 = (bf16[192,768]{1,0:T(8,128)(2,1)}, bf16[192,768]{1,0:T(8,128)(2,1)}, bf16[192,768]{1,0:T(8,128)(2,1)}, bf16[192,768]{1,0:T(8,128)(2,1)}, bf16[4...) custom-call(bf16[4,384,768]{2,1,0:T(8,128)(2,1)} %all-to-all-done.6., ...), custom_call_target="tpu_custom_call", output_to_operand_aliasing={{4}: (8, {})} | custom-call | flops 72477573120 | bytes 30000000 | tf_op jit(solution)/shard_map/pallas_call | solution.py:575
  293.9 18.2 %all-to-all-done.5.refs_11_.refs_4_ = bf16[4,384,768]{2,1,0:T(8,128)(2,1)S(1)} async-done(((bf16[4,384,768]{2,1,0:T(8,128)(2,1)}), bf16[4,384,768]{2,1,0:T(8,128)(2,1)S(1)}, u32[]{:S(2)}, u32[]{:S(2)}) %all-to-all-start.5) | async-done | bytes 2359328 | tf_op jit(solution)/shard_map/all_to_all | solution.py:780
  320.0 12.6 %shard_map.225.refs_9_ = bf16[1536,768]{1,0:T(8,128)(2,1)} custom-call(s32[1]{0:T(128)S(6)} %sub.3.refs_0_, bf16[768,3072]{1,0:T(8,128)(2,1)} %get-tuple-element.120.refs_1_, bf16[768,3072]{1,0:T(8,128)(2,1)} %get-tuple-element.121.refs_2_, bf16[768,3072]{1,0:T(8,128)(2,1)} %get-tuple-element.122.refs_3_, bf16[768,3072]{1,0:T(8,128)(2,1)} %get-tuple-element.123.refs_4_, ...), custom_call_target="tpu_custom_call" | custom-call | flops 36238786560 | bytes 15000000 | tf_op jit(solution)/shard_map/pallas_call | solution.py:623
  332.7 12.9 %shard_map.226.refs_10_ = bf16[384,3072]{1,0:T(8,128)(2,1)} custom-call(s32[1]{0:T(128)S(6)} %sub.3.refs_0_, bf16[4,192,768]{2,1,0:T(8,128)(2,1)} %copy-done.14, bf16[4,192,768]{2,1,0:T(8,128)(2,1)} %copy-done.15, bf16[4,384,768]{2,1,0:T(8,128)(2,1)} %copy-done.11, bf16[4,384,768]{2,1,0:T(8,128)(2,1)} %all-to-all-done.6.refs_0_.refs_1_.refs_4_, ...), custom_call_target="tpu_custom_call" | custom-call | flops 36238786560 | bytes 25000000 | tf_op jit(solution)/shard_map/pallas_call | solution.py:648
  349.5 13.0 %shard_map.227.refs_10_ = bf16[1536,768]{1,0:T(8,128)(2,1)} custom-call(s32[1]{0:T(128)} %bitcast.23.refs_0_.odd_ref, bf16[768,3072]{1,0:T(8,128)(2,1)} %get-tuple-element.120.refs_1_, bf16[768,3072]{1,0:T(8,128)(2,1)} %get-tuple-element.121.refs_2_, bf16[768,3072]{1,0:T(8,128)(2,1)} %get-tuple-element.122.refs_3_, ...), custom_call_target="tpu_custom_call" | custom-call | flops 36238786560 | bytes 15000000 | tf_op jit(solution)/shard_map/pallas_call | solution.py:623
  368.3 13.1 %shard_map.228.refs_17_ = bf16[384,3072]{1,0:T(8,128)(2,1)} custom-call(s32[1]{0:T(128)} %bitcast.23.refs_0_.odd_ref, bf16[4,192,768]{2,1,0:T(8,128)(2,1)} %copy-done.14, bf16[4,192,768]{2,1,0:T(8,128)(2,1)} %copy-done.15, bf16[4,384,768]{2,1,0:T(8,128)(2,1)} %copy-done.11, bf16[4,384,768]{2,1,0:T(8,128)(2,1)} %all-to-all-done.6.refs_0_.refs_1_.refs_4_, ...), custom_call_target="tpu_custom_call" | custom-call | flops 36238786560 | bytes 25000000 | tf_op jit(solution)/shard_map/pallas_call | solution.py:648
  387.1 31.0 %shard_map.229 = (bf16[512,768]{1,0:T(8,128)(2,1)}, bf16[512,768]{1,0:T(8,128)(2,1)}, bf16[512,2304]{1,0:T(8,128)(2,1)}, bf16[512,768]{1,0:T(8,128)(2,1)}, f32[2,768]{1,0:T(2,128)}, /*index=5*/f32[12,1024]{1,0:T(8,128)}) custom-call(bf16[192,768]{1,0:T(8,128)(2,1)} %copy-done.35, bf16[192,768]{1,0:T(8,128)(2,1)} %collective-permute-done.8.refs_10_.refs_1_, ...), custom_call_target="tpu_custom_call" | custom-call | flops 38252052480 | bytes 30000000 | tf_op jit(solution)/shard_map/pallas_call | solution.py:522
  428.9 31.9 %shard_map.231 = (bf16[512,768]{1,0:T(8,128)(2,1)}, bf16[512,768]{1,0:T(8,128)(2,1)}, bf16[512,2304]{1,0:T(8,128)(2,1)}, bf16[512,768]{1,0:T(8,128)(2,1)}, f32[2,768]{1,0:T(2,128)}, /*index=5*/f32[12,1024]{1,0:T(8,128)}) custom-call(bf16[192,768]{1,0:T(8,128)(2,1)} %collective-permute-done.13.refs_11_.refs_0_, ...), custom_call_target="tpu_custom_call" | custom-call | flops 38252052480 | bytes 30000000 | tf_op jit(solution)/shard_map/pallas_call | solution.py:522
  467.2 10.3 %shard_map.232 = (bf16[768,1536]{1,0:T(8,128)(2,1)}, bf16[768,1664]{1,0:T(8,128)(2,1)}) custom-call(bf16[512,768]{1,0:T(8,128)(2,1)} %get-tuple-element.130.refs_0_, bf16[512,768]{1,0:T(8,128)(2,1)} %get-tuple-element.142.refs_1_, bf16[512,2304]{1,0:T(8,128)(2,1)} %get-tuple-element.143.refs_2_, bf16[512,2304]{1,0:T(8,128)(2,1)} %get-tuple-element.144.refs_3_, ...), custom_call_target="tpu_custom_call" | custom-call | flops 24159191040 | bytes 20000000 | tf_op jit(solution)/shard_map/pallas_call | solution.py:680
  498.0 8.8 %shard_map.234 = f32[3072,768]{1,0:T(8,128)} custom-call(s32[1]{0:T(128)} %bitcast.23.refs_0_.odd_ref, bf16[1536,768]{1,0:T(8,128)(2,1)} %pad_maximum_fusion.mine_ref, bf16[1536,768]{1,0:T(8,128)(2,1)} %collective-permute-done.29.other_ref), custom_call_target="tpu_custom_call" | custom-call | flops 5898240 | bytes 20000000 | tf_op jit(solution)/shard_map/pallas_call | solution.py:664
  543.7 11.3 %collective-permute-done.36 = bf16[96,3072]{1,0:T(8,128)(2,1)S(1)} collective-permute-done((bf16[96,3072]{1,0:T(8,128)(2,1)S(1)}, bf16[96,3072]{1,0:T(8,128)(2,1)S(1)}, u32[]{:S(2)}, u32[]{:S(2)}) %collective-permute-start.36) | collective-permute-done | bytes 589856 | tf_op jit(solution)/shard_map/ppermute | solution.py:709
  555.2 8.9 %collective-permute-done.37 = bf16[96,3072]{1,0:T(8,128)(2,1)S(1)} collective-permute-done((bf16[96,3072]{1,0:T(8,128)(2,1)S(1)}, bf16[96,3072]{1,0:T(8,128)(2,1)S(1)}, u32[]{:S(2)}, u32[]{:S(2)}) %collective-permute-start.37) | collective-permute-done | bytes 589856 | tf_op jit(solution)/shard_map/ppermute | solution.py:709
  566.4 7.9 %collective-permute-done.34 = bf16[48,3200]{1,0:T(8,128)(2,1)S(1)} collective-permute-done((bf16[48,3200]{1,0:T(8,128)(2,1)S(1)}, bf16[48,3200]{1,0:T(8,128)(2,1)S(1)}, u32[]{:S(2)}, u32[]{:S(2)}) %collective-permute-start.34) | collective-permute-done | bytes 307232 | tf_op jit(solution)/shard_map/ppermute | solution.py:709
  574.5 8.7 %shard_map.236 = f32[768,3072]{1,0:T(8,128)} custom-call(s32[1]{0:T(128)} %bitcast.23.refs_0_.odd_ref, bf16[384,3072]{1,0:T(8,128)(2,1)} %copy-done.3, bf16[384,3072]{1,0:T(8,128)(2,1)} %collective-permute-done.38.other_ref), custom_call_target="tpu_custom_call" | custom-call | flops 5898240 | bytes 20000000 | tf_op jit(solution)/shard_map/pallas_call | solution.py:664
  588.0 10.6 %collective-permute-done.39 = bf16[96,3200]{1,0:T(8,128)(2,1)S(1)} collective-permute-done((bf16[96,3200]{1,0:T(8,128)(2,1)S(1)}, bf16[96,3200]{1,0:T(8,128)(2,1)S(1)}, u32[]{:S(2)}, u32[]{:S(2)}) %collective-permute-start.39) | collective-permute-done | bytes 614432 | tf_op jit(solution)/shard_map/ppermute | solution.py:709
  (262 shorter events, 206.7 us)
Async XLA Ops:
  7.2 49.8 %all-gather.2.cloned.1.call-start = ((), (), s32[]{:S(2)}) async-start(), calls=%async_computation.9 | async-start | bytes 5898240 | tf_op jit(solution)/shard_map/all_gather | solution.py:806
  45.9 40.0 %all-to-all-start.2 = ((bf16[4,384,768]{2,1,0:T(8,128)(2,1)}), bf16[4,384,768]{2,1,0:T(8,128)(2,1)S(1)}, u32[]{:S(2)}, u32[]{:S(2)}) async-start(bf16[4,384,768]{2,1,0:T(8,128)(2,1)} %shard_map.217), calls=%async_computation.2 | async-start | bytes 4718592 | tf_op jit(solution)/shard_map/all_to_all | solution.py:780
  49.7 40.0 %collective-permute-start.1 = (bf16[256,768]{1,0:T(8,128)(2,1)}, bf16[256,768]{1,0:T(8,128)(2,1)}, u32[]{:S(2)}, u32[]{:S(2)}) collective-permute-start(bf16[256,768]{1,0:T(8,128)(2,1)} %get-tuple-element.248), channel_id=1, source_target_pairs={{0,4},{1,5},{2,6},{3,7},{4,0},{5,1},{6,2},{7,3},{8,12},{9,13},{10,... | collective-permute-start | bytes 1179656 | tf_op jit(solution)/shard_map/ppermute | solution.py:709
  78.9 42.0 %collective-permute-start.4 = (bf16[512,768]{1,0:T(8,128)(2,1)}, bf16[512,768]{1,0:T(8,128)(2,1)}, u32[]{:S(2)}, u32[]{:S(2)}) collective-permute-start(bf16[512,768]{1,0:T(8,128)(2,1)} %get-tuple-element.94), channel_id=1, source_target_pairs={{0,4},{1,5},{2,6},{3,7},{4,0},{5,1},{6,2},{7,3},{8,12},{9,13},{10,... | collective-permute-start | bytes 2359304 | tf_op jit(solution)/shard_map/ppermute | solution.py:709
  120.9 79.8 %collective-permute-start.5 = (bf16[512,768]{1,0:T(8,128)(2,1)}, bf16[512,768]{1,0:T(8,128)(2,1)}, u32[]{:S(2)}, u32[]{:S(2)}) collective-permute-start(bf16[512,768]{1,0:T(8,128)(2,1)} %slice_bitcast_fusion), channel_id=1, source_target_pairs={{0,4},{1,5},{2,6},{3,7},{4,0},{5,1},{6,2},{7,3},{8,12},{9,13},{10,... | collective-permute-start | bytes 2359304 | tf_op jit(solution)/shard_map/ppermute | solution.py:709
  120.9 79.8 %collective-permute-start.6 = (bf16[512,768]{1,0:T(8,128)(2,1)}, bf16[512,768]{1,0:T(8,128)(2,1)}, u32[]{:S(2)}, u32[]{:S(2)}) collective-permute-start(bf16[512,768]{1,0:T(8,128)(2,1)} %get-tuple-element.102), channel_id=1, source_target_pairs={{0,4},{1,5},{2,6},{3,7},{4,0},{5,1},{6,2},{7,3},{8,12},{9,13},{10,... | collective-permute-start | bytes 2359304 | tf_op jit(solution)/shard_map/ppermute | solution.py:709
  123.9 44.1 %all-to-all-start.4 = ((bf16[4,192,768]{2,1,0:T(8,128)(2,1)}), bf16[4,192,768]{2,1,0:T(8,128)(2,1)S(1)}, u32[]{:S(2)}, u32[]{:S(2)}) async-start(bf16[4,192,768]{2,1,0:T(8,128)(2,1)} %get-tuple-element.97.refs_9_), calls=%async_computation.4 | async-start | bytes 2359296 | tf_op jit(solution)/shard_map/all_to_all | solution.py:780
  169.0 46.5 %all-to-all-start.3 = ((bf16[4,384,768]{2,1,0:T(8,128)(2,1)}), bf16[4,384,768]{2,1,0:T(8,128)(2,1)S(1)}, u32[]{:S(2)}, u32[]{:S(2)}) async-start(bf16[4,384,768]{2,1,0:T(8,128)(2,1)} %shard_map.220.refs_10_), calls=%async_computation.3 | async-start | bytes 4718592 | tf_op jit(solution)/shard_map/all_to_all | solution.py:780
  215.5 40.4 %all-to-all-start.6 = ((bf16[4,384,768]{2,1,0:T(8,128)(2,1)}), bf16[4,384,768]{2,1,0:T(8,128)(2,1)}, u32[]{:S(2)}, u32[]{:S(2)}) async-start(bf16[4,384,768]{2,1,0:T(8,128)(2,1)} %shard_map.222.refs_8_), calls=%async_computation.6 | async-start | bytes 4718592 | tf_op jit(solution)/shard_map/all_to_all | solution.py:780
  248.2 43.5 %collective-permute-start.7 = (bf16[192,768]{1,0:T(8,128)(2,1)}, bf16[192,768]{1,0:T(8,128)(2,1)S(1)}, u32[]{:S(2)}, u32[]{:S(2)}) collective-permute-start(bf16[192,768]{1,0:T(8,128)(2,1)} %get-tuple-element.105), channel_id=1, source_target_pairs={{0,4},{1,5},{2,6},{3,7},{4,0},{5,1},{6,2},{7,3},{8,12},{9,13},{10,... | collective-permute-start | bytes 884744 | tf_op jit(solution)/shard_map/ppermute | solution.py:709
  249.4 69.0 %collective-permute-start.8 = (bf16[192,768]{1,0:T(8,128)(2,1)}, bf16[192,768]{1,0:T(8,128)(2,1)}, u32[]{:S(2)}, u32[]{:S(2)}) collective-permute-start(bf16[192,768]{1,0:T(8,128)(2,1)} %get-tuple-element.106), channel_id=1, source_target_pairs={{0,5},{1,4},{2,7},{3,6},{4,1},{5,0},{6,3},{7,2},{8,13},{9,12},{10,... | collective-permute-start | bytes 884744 | tf_op jit(solution)/shard_map/ppermute | solution.py:709
  252.6 80.0 %collective-permute-start.9 = (bf16[192,768]{1,0:T(8,128)(2,1)}, bf16[192,768]{1,0:T(8,128)(2,1)}, u32[]{:S(2)}, u32[]{:S(2)}) collective-permute-start(bf16[192,768]{1,0:T(8,128)(2,1)} %get-tuple-element.107), channel_id=1, source_target_pairs={{0,6},{1,7},{2,4},{3,5},{4,2},{5,3},{6,0},{7,1},{8,14},{9,15},{10,... | collective-permute-start | bytes 884744 | tf_op jit(solution)/shard_map/ppermute | solution.py:709
  255.0 90.5 %collective-permute-start.10 = (bf16[192,768]{1,0:T(8,128)(2,1)}, bf16[192,768]{1,0:T(8,128)(2,1)}, u32[]{:S(2)}, u32[]{:S(2)}) collective-permute-start(bf16[192,768]{1,0:T(8,128)(2,1)} %get-tuple-element.108), channel_id=1, source_target_pairs={{0,7},{1,6},{2,5},{3,4},{4,3},{5,2},{6,1},{7,0},{8,15},{9,14},{10,... | collective-permute-start | bytes 884744 | tf_op jit(solution)/shard_map/ppermute | solution.py:709
  255.9 56.2 %all-to-all-start.5 = ((bf16[4,384,768]{2,1,0:T(8,128)(2,1)}), bf16[4,384,768]{2,1,0:T(8,128)(2,1)S(1)}, u32[]{:S(2)}, u32[]{:S(2)}) async-start(bf16[4,384,768]{2,1,0:T(8,128)(2,1)} %get-tuple-element.110), calls=%async_computation.5 | async-start | bytes 4718592 | tf_op jit(solution)/shard_map/all_to_all | solution.py:780
  287.7 77.7 %collective-permute-start.13 = (bf16[192,768]{1,0:T(8,128)(2,1)}, bf16[192,768]{1,0:T(8,128)(2,1)}, u32[]{:S(2)}, u32[]{:S(2)}) collective-permute-start(bf16[192,768]{1,0:T(8,128)(2,1)} %get-tuple-element.128), channel_id=1, source_target_pairs={{0,4},{1,5},{2,6},{3,7},{4,0},{5,1},{6,2},{7,3},{8,12},{9,13},{10,... | collective-permute-start | bytes 884744 | tf_op jit(solution)/shard_map/ppermute | solution.py:709
  291.6 93.2 %collective-permute-start.15 = (bf16[192,768]{1,0:T(8,128)(2,1)}, bf16[192,768]{1,0:T(8,128)(2,1)}, u32[]{:S(2)}, u32[]{:S(2)}) collective-permute-start(bf16[192,768]{1,0:T(8,128)(2,1)} %get-tuple-element.129), channel_id=1, source_target_pairs={{0,5},{1,4},{2,7},{3,6},{4,1},{5,0},{6,3},{7,2},{8,13},{9,12},{10,... | collective-permute-start | bytes 884744 | tf_op jit(solution)/shard_map/ppermute | solution.py:709
  313.5 104.6 %all-to-all-start.7 = ((bf16[4,384,768]{2,1,0:T(8,128)(2,1)}), bf16[4,384,768]{2,1,0:T(8,128)(2,1)}, u32[]{:S(2)}, u32[]{:S(2)}) async-start(bf16[4,384,768]{2,1,0:T(8,128)(2,1)} %get-tuple-element.139), calls=%async_computation.7 | async-start | bytes 4718592 | tf_op jit(solution)/shard_map/all_to_all | solution.py:780
  318.4 108.4 %collective-permute-start.16 = (bf16[192,768]{1,0:T(8,128)(2,1)}, bf16[192,768]{1,0:T(8,128)(2,1)}, u32[]{:S(2)}, u32[]{:S(2)}) collective-permute-start(bf16[192,768]{1,0:T(8,128)(2,1)} %get-tuple-element.131), channel_id=1, source_target_pairs={{0,6},{1,7},{2,4},{3,5},{4,2},{5,3},{6,0},{7,1},{8,14},{9,15},{10,... | collective-permute-start | bytes 884744 | tf_op jit(solution)/shard_map/ppermute | solution.py:709
  345.5 82.5 %collective-permute-start.17 = (bf16[192,768]{1,0:T(8,128)(2,1)S(1)}, bf16[192,768]{1,0:T(8,128)(2,1)}, u32[]{:S(2)}, u32[]{:S(2)}) collective-permute-start(bf16[192,768]{1,0:T(8,128)(2,1)S(1)} %copy-done.36), channel_id=1, source_target_pairs={{0,7},{1,6},{2,5},{3,4},{4,3},{5,2},{6,1},{7,0},{8,15},{9,14},{10,... | collective-permute-start | bytes 884744 | tf_op jit(solution)/shard_map/ppermute | solution.py:709
  384.2 82.9 %collective-permute-start.21 = (bf16[96,3072]{1,0:T(8,128)(2,1)}, bf16[96,3072]{1,0:T(8,128)(2,1)}, u32[]{:S(2)}, u32[]{:S(2)}) collective-permute-start(bf16[96,3072]{1,0:T(8,128)(2,1)} %get-tuple-element.239), channel_id=1, source_target_pairs={{0,16},{8,24},{16,0},{24,8},{1,17},{9,25},{17,1},{25,9},{2,18},{10... | collective-permute-start | bytes 1769480 | tf_op jit(solution)/shard_map/ppermute | solution.py:709
  384.8 43.3 %collective-permute-start.18 = (bf16[384,768]{1,0:T(8,128)(2,1)}, bf16[384,768]{1,0:T(8,128)(2,1)S(1)}, u32[]{:S(2)}, u32[]{:S(2)}) collective-permute-start(bf16[384,768]{1,0:T(8,128)(2,1)} %get-tuple-element.246), channel_id=1, source_target_pairs={{0,16},{8,24},{16,0},{24,8},{1,17},{9,25},{17,1},{25,9},{2,18},{10... | collective-permute-start | bytes 1769480 | tf_op jit(solution)/shard_map/ppermute | solution.py:709
  386.3 41.8 %collective-permute-start.19 = (bf16[384,768]{1,0:T(8,128)(2,1)}, bf16[384,768]{1,0:T(8,128)(2,1)}, u32[]{:S(2)}, u32[]{:S(2)}) collective-permute-start(bf16[384,768]{1,0:T(8,128)(2,1)} %get-tuple-element.245), channel_id=1, source_target_pairs={{0,16},{8,24},{16,0},{24,8},{1,17},{9,25},{17,1},{25,9},{2,18},{10... | collective-permute-start | bytes 1769480 | tf_op jit(solution)/shard_map/ppermute | solution.py:709
  418.1 49.1 %all-to-all-start.8 = ((bf16[4,384,768]{2,1,0:T(8,128)(2,1)}), bf16[4,384,768]{2,1,0:T(8,128)(2,1)}, u32[]{:S(2)}, u32[]{:S(2)}) async-start(bf16[4,384,768]{2,1,0:T(8,128)(2,1)} %get-tuple-element.156.refs_4_), calls=%async_computation.8 | async-start | bytes 4718592 | tf_op jit(solution)/shard_map/all_to_all | solution.py:780
  426.8 40.3 %collective-permute-start.20 = (bf16[384,768]{1,0:T(8,128)(2,1)S(1)}, bf16[384,768]{1,0:T(8,128)(2,1)}, u32[]{:S(2)}, u32[]{:S(2)}) collective-permute-start(bf16[384,768]{1,0:T(8,128)(2,1)S(1)} %get-tuple-element.244), channel_id=1, source_target_pairs={{0,16},{8,24},{16,0},{24,8},{1,17},{9,25},{17,1},{25,9},{2,18},{10... | collective-permute-start | bytes 1769480 | tf_op jit(solution)/shard_map/ppermute | solution.py:709
  (65 other events, 891.3 us)
Sparse Core Ops, SparseCore 0:
  10.2 42.2 all-gather.1

commit v3 on v2

--- a/solution.py
+++ b/solution.py
@@ -147,6 +147,7 @@
 def forward_kernel(
     m, x_ref, gains_ref, weight_ref, strip_ref, block_row_ref, block_col_ref, row_ref,
     proj_ref, mixed_ref, total_ref, hidden_ref, second_ref, send_ref,
+    score_ref, weight_part_ref, mask_ref,
 ):
     _, length, width = x_ref.shape
     scale = HEAD ** (-0.5)
@@ -154,34 +155,34 @@
     r1 = lax.rsqrt(jnp.mean(x * x, axis=1, keepdims=True) + epsilon)
     normed = (x * r1 * gains_ref[0:1, :]).astype(BF16)
     proj_ref[...] = dot(normed, weight_ref[:, : 3 * width]).astype(BF16)
+    total_ref[...] = jnp.zeros_like(total_ref)
+
+    mask_ref[...] = jnp.where(block_row_ref[m] <= block_col_ref[:, m : m + 1], 0.0, masked_score)
+    lane = iota((STRIP, LANES), 1)
 
     def pair(p, carry):
         lanes = pl.multiple_of(p * PAIR, PAIR)
-        q = proj_ref[:, pl.ds(lanes, PAIR)]
+        q = proj_ref[:, pl.ds(lanes, PAIR)] * scale
         k = proj_ref[:, pl.ds(width + lanes, PAIR)]
         v = proj_ref[:, pl.ds(2 * width + lanes, PAIR)]
         left = head_mask(length)
         zero = jnp.zeros_like(k)
-        outs = [None] * (length // STRIP)
+        keeps = (left, jnp.logical_not(left))
         for h in range(2):
-            keep = left if h == 0 else jnp.logical_not(left)
-            kh = jnp.where(keep, k, zero)
-            vh = jnp.where(keep, v, zero)
+            score_ref[h] = dot_nt(q, jnp.where(keeps[h], k, zero))
+        for h in range(2):
             strip = strip_ref[2 * p + h].astype(F32)
             for i in range(length // STRIP):
                 rows = slice(i * STRIP, (i + 1) * STRIP)
                 start = length - STRIP - i * STRIP
-                s = dot_nt(q[rows], kh) * scale + strip[:, start : start + length]
-                s = jnp.where(block_row_ref[m] <= block_col_ref[rows, m : m + 1], s, masked_score)
+                s = (score_ref[h, rows, :] + strip[:, start : start + length]) + mask_ref[rows, :]
                 top = jnp.max(s, axis=1, keepdims=True)
                 e = jnp.exp(s - top)
                 total = jnp.sum(e, axis=1, keepdims=True)
-                weights = (e * (1.0 / total)).astype(BF16)
-                total_ref[2 * p + h, rows, :] = top + jnp.log(total)
-                part = dot(weights, vh)
-                outs[i] = part if outs[i] is None else outs[i] + part
-        for i, part in enumerate(outs):
-            mixed_ref[i * STRIP : (i + 1) * STRIP, pl.ds(lanes, PAIR)] = part.astype(BF16)
+                weight_part_ref[h, rows, :] = (e * (1.0 / total)).astype(BF16)
+                total_ref[rows, :] = jnp.where(lane == 2 * p + h, top + jnp.log(total), total_ref[rows, :])
+        out = dot(weight_part_ref[0], jnp.where(keeps[0], v, zero)) + dot(weight_part_ref[1], jnp.where(keeps[1], v, zero))
+        mixed_ref[:, pl.ds(lanes, PAIR)] = out.astype(BF16)
         return carry
 
     lax.fori_loop(0, width // PAIR, pair, 0)
@@ -200,7 +201,7 @@
     part, far_refs, own_ref, mine_ref, col_ref, cot_ref, hidden_ref, gains_ref, weight_ref, proj_ref, total_ref, strip_ref,
     block_row_ref, block_col_ref, x_ref,
     grad_x_ref, branch_ref, grad_proj_ref, normed_ref, grad_gain_ref, diagonal_ref,
-    pick_ref, back_ref, grad_mixed_ref, low_ref, prob_ref, strip_sum_ref,
+    pick_ref, back_ref, grad_mixed_ref, low_ref, prob_ref, strip_sum_ref, score_ref, grad_prob_ref, mask_ref,
 ):
     _, length, width = cot_ref.shape
     scale = HEAD ** (-0.5)
@@ -223,7 +224,8 @@
     branch_ref[...] = branch
     grad_mixed_ref[...] = dot_nt(branch, weight_ref[:, 3 * width : 4 * width]).astype(BF16)
 
-    m = part
+    mask_ref[...] = jnp.where(block_row_ref[part] <= block_col_ref[:, part : part + 1], 0.0, masked_score)
+    lane = iota((STRIP, LANES), 1)
 
     def pair(p, carry):
         lanes = pl.multiple_of(p * PAIR, PAIR)
@@ -235,32 +237,30 @@
         g_turned = g.astype(F32).T.astype(BF16)
         left = head_mask(length)
         zero = jnp.zeros_like(k)
-        outs = [None] * (length // STRIP)
+        keeps = (left, jnp.logical_not(left))
+        scaled_q = q * scale
+        for h in range(2):
+            score_ref[h] = dot_nt(scaled_q, jnp.where(keeps[h], k, zero))
+            grad_prob_ref[h] = dot_nt(g, jnp.where(keeps[h], v, zero))
         keys, values = [], []
         for h in range(2):
-            keep = left if h == 0 else jnp.logical_not(left)
-            kh = jnp.where(keep, k, zero)
-            vh = jnp.where(keep, v, zero)
             strip = strip_ref[2 * p + h].astype(F32)
             strip_sum_ref[...] = jnp.zeros_like(strip_sum_ref)
             for i in range(length // STRIP):
                 rows = slice(i * STRIP, (i + 1) * STRIP)
                 start = length - STRIP - i * STRIP
-                s = dot_nt(q[rows], kh) * scale + strip[:, start : start + length]
-                s = jnp.where(block_row_ref[m] <= block_col_ref[rows, m : m + 1], s, masked_score)
-                prob = jnp.exp(s - total_ref[2 * p + h, rows, :])
-                grad_prob = dot_nt(g[rows], vh)
+                s = (score_ref[h, rows, :] + strip[:, start : start + length]) + mask_ref[rows, :]
+                row_total = jnp.sum(jnp.where(lane == 2 * p + h, total_ref[rows, :], 0.0), axis=1, keepdims=True)
+                prob = jnp.exp(s - row_total)
+                grad_prob = grad_prob_ref[h, rows, :]
                 row_inner = jnp.sum(prob * grad_prob, axis=1, keepdims=True)
                 grad_score = prob * (grad_prob - row_inner)
                 strip_sum_ref[:, start : start + length] += grad_score
-                low = grad_score.astype(BF16)
-                low_ref[rows, :] = low
-                prob_ref[rows, :] = prob.astype(BF16)
-                part = dot(low, kh)
-                outs[i] = part if outs[i] is None else outs[i] + part
+                low_ref[h, rows, :] = grad_score.astype(BF16)
+                prob_ref[h, rows, :] = prob.astype(BF16)
             half = slice(h * HEAD, (h + 1) * HEAD)
-            keys.append(dot(q_turned[half], low_ref[...]))
-            values.append(dot(g_turned[half], prob_ref[...]))
+            keys.append(dot(q_turned[half], low_ref[h]))
+            values.append(dot(g_turned[half], prob_ref[h]))
             gathered = jnp.zeros((8, 2 * length), F32)
             for a in range(STRIP // 8):
                 piece = strip_sum_ref[8 * a : 8 * a + 8, :]
@@ -269,8 +269,8 @@
             for b in range(7):
                 line += pltpu.roll(gathered[b : b + 1], 7 - b, 1)
             diagonal_ref[pl.ds(2 * p + h, 1), :] = line
-        for i, part in enumerate(outs):
-            grad_proj_ref[i * STRIP : (i + 1) * STRIP, pl.ds(lanes, PAIR)] = (part * scale).astype(BF16)
+        grad_query = dot(low_ref[0], jnp.where(keeps[0], k, zero)) + dot(low_ref[1], jnp.where(keeps[1], k, zero))
+        grad_proj_ref[:, pl.ds(lanes, PAIR)] = (grad_query * scale).astype(BF16)
         grad_key = jnp.concatenate(keys, axis=0).T
         grad_value = jnp.concatenate(values, axis=0).T
         grad_proj_ref[:, pl.ds(width + lanes, PAIR)] = (grad_key * scale).astype(BF16)
@@ -358,23 +358,23 @@
 
     @pl.when(step == pl.num_programs(0) - 1)
     def _():
-        grad_router = jnp.zeros(grad_router_ref.shape, F32)
-        copies = []
+        copies, parts = [], []
+        lane = iota((capacity, LANES), 1)
+        here = pl.ds(part * capacity, capacity)
         for d in range(near):
             at = slice(d * capacity, (d + 1) * capacity)
             produced = out_acc[at, :].astype(BF16).astype(F32)
             gate = gate_ref[at, :]
-            here = pl.ds(part * capacity, capacity)
             out_ref[at, :] = (gate * produced).astype(BF16)
             copies.append(pltpu.make_async_copy(out_ref.at[at, :], all_ref.at[d, here, :], sem.at[0, d]))
             copies[-1].start()
             grad_gate = jnp.sum(cots_ref[d].astype(F32) * produced, axis=1, keepdims=True)
             share = gate * (1.0 - gate) * grad_gate
-            lane = iota((capacity, LANES), 1)
             signed = jnp.where(lane == mine, share, 0.0) - jnp.where(lane == other_ref[at, :], share, 0.0)
             high = signed.astype(BF16)
             rest = (signed - high.astype(F32)).astype(BF16)
-            routed = dot(high, router_turned_ref[...]) + dot(rest, router_turned_ref[...])
+            parts.append(jnp.concatenate([high, rest], axis=1))
+            routed = dot(parts[-1], router_turned_ref[...])
             back = (back_acc[at, :] + routed).astype(BF16)
             if kind:
                 for e in range(near):
@@ -385,9 +385,8 @@
                 back_ref[at, :] = back
                 copies.append(pltpu.make_async_copy(back_ref.at[at, :], back_refs[0].at[d, here, :], sem.at[1, d]))
                 copies[-1].start()
-            rows = sent_ref[d]
-            grad_router = grad_router + dot_tn(rows, high) + dot_tn(rows, rest)
-        grad_router_ref[...] = grad_router
+        both = dot_tn(jnp.concatenate(parts, axis=0), rows)
+        grad_router_ref[...] = both[:LANES] + both[LANES:]
         for copy in copies:
             copy.wait()
 
@@ -499,11 +498,14 @@
         out_shape=(
             shaped((length, 3 * width), BF16),
             shaped((length, width), BF16),
-            shaped((heads, length, 1), F32),
+            shaped((length, LANES), F32),
             shaped((length, width), F32),
             shaped((length, width), BF16),
             shaped((near, capacity, width), BF16),
         ),
+        scratch_shapes=[
+            pltpu.VMEM((2, length, length), F32), pltpu.VMEM((2, length, length), BF16), pltpu.VMEM((length, length), F32),
+        ],
         compiler_params=params(),
         cost_estimate=cost(
             2 * length * width * 4 * width + 8 * heads * length * length * HEAD,
@@ -534,9 +536,12 @@
             pltpu.VMEM((length, total), BF16),
             pltpu.VMEM((total, width), BF16),
             pltpu.VMEM((length, width), BF16),
-            pltpu.VMEM((length, length), BF16),
-            pltpu.VMEM((length, length), BF16),
+            pltpu.VMEM((2, length, length), BF16),
+            pltpu.VMEM((2, length, length), BF16),
             pltpu.VMEM((STRIP, 2 * length), F32),
+            pltpu.VMEM((2, length, length), F32),
+            pltpu.VMEM((2, length, length), F32),
+            pltpu.VMEM((length, length), F32),
         ],
         compiler_params=params(),
         cost_estimate=cost(
@@ -585,12 +590,12 @@
             anywhere,
             pl.BlockSpec((total, step), lambda f: (0, f)),
             pl.BlockSpec((total, step), lambda f: (0, f)),
-            whole((total, width)), whole((width, LANES)),
+            whole((total, width)), whole((LANES, width)),
         ),
         out_shape=back_shapes + (
             shared,
             shaped((total, inner), BF16), shaped((total, inner), BF16),
-            shaped((total, width), BF16), shaped((width, LANES), F32),
+            shaped((total, width), BF16), shaped((LANES, width), F32),
         ),
         scratch_shapes=[
             pltpu.VMEM((total, 1), F32),
@@ -657,20 +662,21 @@
     )(half, *[array for array, _ in rows], *ups, *extra, *after)
 
 
-def join(odd, mine, other):
+def join(odd, mine, other, after):
     rows, columns = mine.shape
     step = rows // 3
-    spec = pl.BlockSpec((step, columns), lambda h, i, odd: (i, 0))
-    return pl.pallas_call(
-        join_kernel,
+    own = pl.BlockSpec((step, columns), lambda h, i, odd: (jnp.where(h == odd[0], i, 2 * (1 - h)), 0))
+    far = pl.BlockSpec((step, columns), lambda h, i, odd: (jnp.where(h == odd[0], 2 * (1 - h), i), 0))
+    return pl.pallas_call(
+        later(join_kernel, 3, len(after)),
         grid_spec=pltpu.PrefetchScalarGridSpec(
-            num_scalar_prefetch=1, grid=(2, 3), in_specs=[spec, spec],
+            num_scalar_prefetch=1, grid=(2, 3), in_specs=[own, far] + [ANYWHERE] * len(after),
             out_specs=pl.BlockSpec((step, columns), lambda h, i, odd: (h * 3 + i, 0)),
         ),
         out_shape=shaped((2 * rows, columns), F32),
         compiler_params=params(dimension_semantics=("arbitrary", "arbitrary")),
         cost_estimate=cost(rows * columns, 20e6),
-    )(odd, mine, other)
+    )(odd, mine, other, *after)
 
 
 def dense_grad(*arrays, after):
@@ -686,23 +692,23 @@
     )(*arrays, *after)
 
 
-def combine(out_rows, part, far, mine, col, hidden):
+def combine(out_rows, part, far, mine, col, hidden, after):
     length, width = hidden.shape
     near, capacity = out_rows.shape[0], out_rows.shape[1] // 2
     total = near * capacity
     plain = pl.BlockSpec((length, width), lambda f: (0, 0))
     return pl.pallas_call(
-        combine_kernel,
+        later(combine_kernel, 5, len(after)),
         grid=(1,),
         in_specs=[
             block_of(0, near, capacity, width, part), plain, SCALAR, pl.BlockSpec(col.shape, lambda f: (0, 0)), plain,
-        ],
+        ] + [ANYWHERE] * len(after),
         out_specs=plain,
         out_shape=shaped((length, width), BF16),
         scratch_shapes=[pltpu.VMEM((length, total), BF16)],
         compiler_params=params(),
         cost_estimate=cost(2 * total * length * width, 6e6),
-    )(out_rows, far, mine, col, hidden)
+    )(out_rows, far, mine, col, hidden, *after)
 
 
 def swap(value, axis, size, bit):
@@ -753,8 +759,7 @@
     while bit > 1:
         bit //= 2
         rows = unite(rows, "expert", experts, bit)
-        if bit == 2:
-            rows = after(9, rows)
+        rows = after({4: 8, 2: 9}.get(bit), rows)
     return rows.astype(F32)
 
 
@@ -807,7 +812,7 @@
     gains = extra[:, :2].astype(F32).T
     table = extra[:, 2].reshape(dp, shard)[:, : rel_table.size].reshape(buckets, heads)
     router = jnp.pad(extra[:, 3 : 3 + experts], ((0, 0), (0, LANES - experts)))
-    router_turned = router.T
+    router_turned = jnp.concatenate([router.T, router.T], axis=0)
     levels = bucket_table(length, buckets)
     base = lax.dot_general(
         table, jnp.asarray(levels, BF16), (((0,), (0,)), ((), ())), preferred_element_type=F32
@@ -837,17 +842,17 @@
 
     common = (mine, router, router_turned, first_in, last_out)
     cot1_far = cross(order(cotangent[1], second0_far, send1)[0], near)
-    back_own, out_own, kept0_own = expert(
-        0, 0, (own0, 0), (cot_own, 0), ids_all[0], *common, (), [second0_far, send1]
-    )
     second1_far = cross(order(second1, second0_far)[0], near)
     far0_send = scatter(
         near, capacity, (places[0][1], [(cot0_top, None), (cot0_end, None)]), (places[0][1], [(second0_far, None)]),
-        after=[out_own],
-    )
-    far0 = around(far0_send)
+        after=[send1],
+    )
+    back_own, out_own, kept0_own = expert(
+        0, 0, (own0, 0), (cot_own, 0), ids_all[0], *common, (), [far0_send]
+    )
+    far0 = around(order(far0_send, out_own)[0])
     back_own, out_own, kept1_own = expert(
-        0, 1, (own1, 0), (cot_own, 1), ids_all[1], *common, (back_own, out_own), [far0_send]
+        0, 1, (own1, 0), (cot_own, 1), ids_all[1], *common, (back_own, out_own), []
     )
     far1_send = scatter(
         near, capacity, (places[1][1], [(cot1_far, None)]), (places[1][1], [(second1_far, None)]), after=[out_own],
@@ -866,7 +871,7 @@
     parts = (kept0_own, kept1_own, kept0_far, kept1_far)
     acts, ups, scaled, routers = zip(*parts)
     rows = ((own0, 0), (own1, 0), (far0, 1), (far1, 1))
-    grad_router = sum(routers)[:, :experts]
+    grad_router = sum(routers)[:experts].T
 
     home0, home1 = home
     other = 1 - odd
@@ -892,7 +897,7 @@
 
     last_sum, last_came = zip(*[over_dp(piece) for piece in pieces(last_sum)])
     first_sum = pieces(first_sum)
-    first_sum[0], first_came = over_dp(first_sum[0])
+    first_sum[:3], first_came = map(list, zip(*[over_dp(piece) for piece in first_sum[:3]]))
 
     def layer_back(m, after):
         proj, mixed, totals, hidden, block_row, block_col = kept[m]
@@ -918,29 +923,31 @@
     left, right = dense_grad(
         back_outs[0][3], back_outs[1][3], back_outs[0][2], back_outs[1][2],
         kept[0][1], kept[1][1], back_outs[0][1], back_outs[1][1], small_grad,
-        after=[last_came[3], first_came, out0_far, out_own],
-    )
-    results = [combine(out_own, 0, out0_far, mine, places[0][2], kept[0][3])]
+        after=[last_came[3], *first_came, out0_far, out_own],
+    )
+    results = [combine(out_own, 0, out0_far, mine, places[0][2], kept[0][3], [left])]
     last_sum = jnp.concatenate(last_sum, axis=0)
-    grad_last = join(odd, last_sum, swap(last_sum, "dp", dp, 1))
-    grad_first = None
+    grad_last = join(odd, last_sum, swap(last_sum, "dp", dp, 1), [left])
 
     def after(step, value):
-        nonlocal grad_first, grad_last, first_sum, out1_far
-        if step == 0:
+        nonlocal grad_last, out1_far
+        if step == 1:
+            value, grad_last, out1_far, *rest = order(value, grad_last, out1_far, *first_sum[3:])
+            results.append(combine(out_own, 1, out1_far, mine, places[1][2], kept[1][3], [results[0], grad_last]))
+            rest, came = zip(*[over_dp(piece) for piece in rest])
+            first_sum[3:] = rest
+            first_came.extend(came)
+        if step == 2:
             value, results[0] = order(value, results[0])
-        if step == 1:
-            value, grad_last, out1_far, *rest = order(value, grad_last, out1_far, *first_sum[1:])
-            results.append(combine(out_own, 1, out1_far, mine, places[1][2], kept[1][3]))
-            both = jnp.concatenate(first_sum[:1] + [over_dp(piece)[0] for piece in rest], axis=0)
-            grad_first = join(odd, both, swap(both, "dp", dp, 1))
         if step == 3:
             value, results[1] = order(value, results[1])
-        if step == 9:
-            value, grad_first = order(value, grad_first)
+        if step == 8:
+            value, first_came[3] = order(value, first_came[3])
         return value
 
     dense = dense_sum(left, right, dp, experts, after)
+    first_sum = jnp.concatenate(first_sum, axis=0)
+    grad_first = join(odd, first_sum, swap(first_sum, "dp", dp, 1), [results[1]])
     tail = dense[:, 4 * width :]
     return (
         jnp.stack(results),

time: 621 us -> 600 us (0.966)
  Pallas kernels: 329 us -> 309 us
  starting transfers between devices: 91.2 us -> 83.7 us
  waiting for transfers between devices: 116 us -> 123 us
    pallas_call x2, Pallas kernels: 62.9 us -> 53.8 us  [backward(): pl.pallas_call(later(functools.partial(backward_kernel, near, part), near...]
    all_to_all x8, waiting for transfers between devices: 47 us -> 55.4 us  [around(): lax.all_to_all(blocks, 'expert', split_axis=0, concat_axis=0, axis_index_...]
    ppermute x40, starting transfers between devices: 50.4 us -> 43.1 us  [swap(): return lax.ppermute(value, axis, [(i, i ^ bit) for i in range(size)])]
  transfers between devices with their start and end apart: 50 -> 50, of which waited for: 19 -> 22; matrix products, arithmetic and copies ran while one was open for 7% -> 8% of each run, Pallas kernels for 51% -> 49%
where the time goes in v3:
time: 600 us; the launch traced here: 589 us
  Pallas kernels  309 us (52%)
  waiting for transfers between devices  123 us (20%)
  starting transfers between devices  83.7 us (14%)
  local copies, waits for them, and re-layouts  29 us (5%)
  other arithmetic  28 us (5%)
  between operations  15.2 us (3%)
    pallas_call x4, Pallas kernels, expert(): pl.pallas_call(later(functools.partial(expert_kernel, kind, near, alias,...  106 us
    ppermute x40, waiting for transfers between devices, swap(): return lax.ppermute(value, axis, [(i, i ^ bit) for i in range(size)])  67.6 us
    all_to_all x8, waiting for transfers between devices, around(): lax.all_to_all(blocks, 'expert', split_axis=0, concat_axis=0, axis_index_...  55.4 us
    pallas_call x2, Pallas kernels, backward(): pl.pallas_call(later(functools.partial(backward_kernel, near, part), near...  53.8 us
    ppermute x40, starting transfers between devices, swap(): return lax.ppermute(value, axis, [(i, i ^ bit) for i in range(size)])  43.1 us
    pallas_call x2, Pallas kernels, forward(): pl.pallas_call(later(functools.partial(forward_kernel, m), 7, len(after))...  38.3 us
    all_to_all x8, starting transfers between devices, around(): lax.all_to_all(blocks, 'expert', split_axis=0, concat_axis=0, axis_index_...  33.7 us
    pallas_call x2, Pallas kernels, first_grad(): pl.pallas_call(later(functools.partial(expert_grad_kernel, len(ups), Fals...  26 us
  transfers between devices with their start and end apart: 50, of which 22 were waited for; matrix products, arithmetic and copies ran while one was open for 8% of the time, Pallas kernels for 49%

profile of v3, /device:TPU:0, one launch (start us, length us, event | category | flops | bytes accessed | tf_op | source)
XLA Modules:
  0.0 589.5 jit_solution(4868500267539764413)
XLA Ops:
  11.2 6.8 %all-to-all-start = ((s32[8,2,2,512]{3,2,1,0:T(2,128)}), s32[8,2,2,512]{3,2,1,0:T(2,128)S(1)}, u32[]{:S(2)}, u32[]{:S(2)}) async-start(s32[8,2,2,512]{3,2,1,0:T(2,128)} %broadcast_in_dim.21), calls=%async_computation | async-start | bytes 131072 | tf_op jit(solution)/shard_map/all_to_all | solution.py:796
  57.2 19.1 %shard_map.215 = (bf16[512,2304]{1,0:T(8,128)(2,1)}, bf16[512,768]{1,0:T(8,128)(2,1)}, f32[512,128]{1,0:T(8,128)}, f32[512,768]{1,0:T(8,128)}, bf16[512,768]{1,0:T(8,128)(2,1)}, /*index=5*/bf16[4,192,768]{2,1,0:T(8,128)(2,1)}) custom-call(bf16[2,512,768]{2,1,0:T(8,128)(2,1)} %refs_16_.3, f32[2,768]{1,0:T(2,128)} %convert_bitcast_fusion.gains_ref.refs_1_.refs_9_, ...), custom_call_target="tpu_custom_call" | custom-call | flops 20132659200 | bytes 24000000 | tf_op jit(solution)/shard_map/pallas_call | solution.py:495
  77.7 8.4 %all-to-all-done.2.refs_1_ = bf16[4,384,768]{2,1,0:T(8,128)(2,1)S(1)} async-done(((bf16[4,384,768]{2,1,0:T(8,128)(2,1)}), bf16[4,384,768]{2,1,0:T(8,128)(2,1)S(1)}, u32[]{:S(2)}, u32[]{:S(2)}) %all-to-all-start.2) | async-done | bytes 2359328 | tf_op jit(solution)/shard_map/all_to_all | solution.py:785
  89.9 19.2 %shard_map.217 = (bf16[512,2304]{1,0:T(8,128)(2,1)}, bf16[512,768]{1,0:T(8,128)(2,1)}, f32[512,128]{1,0:T(8,128)}, f32[512,768]{1,0:T(8,128)}, bf16[512,768]{1,0:T(8,128)(2,1)}, /*index=5*/bf16[4,192,768]{2,1,0:T(8,128)(2,1)}) custom-call(bf16[2,512,768]{2,1,0:T(8,128)(2,1)} %refs_16_.3, f32[2,768]{1,0:T(2,128)} %convert_bitcast_fusion.gains_ref.refs_1_.refs_9_, ...), custom_call_target="tpu_custom_call" | custom-call | flops 20132659200 | bytes 24000000 | tf_op jit(solution)/shard_map/pallas_call | solution.py:495
  109.1 11.6 %collective-permute-done.4.refs_4_ = bf16[512,768]{1,0:T(8,128)(2,1)} collective-permute-done((bf16[512,768]{1,0:T(8,128)(2,1)}, bf16[512,768]{1,0:T(8,128)(2,1)}, u32[]{:S(2)}, u32[]{:S(2)}) %collective-permute-start.4) | collective-permute-done | bytes 786464 | tf_op jit(solution)/shard_map/ppermute | solution.py:715
  131.6 26.0 %shard_map.220 = (bf16[4,384,768]{2,1,0:T(8,128)(2,1)}, bf16[4,384,768]{2,1,0:T(8,128)(2,1)}, bf16[768,3072]{1,0:T(8,128)(2,1)}, bf16[768,3072]{1,0:T(8,128)(2,1...) custom-call(bf16[4,192,768]{2,1,0:T(8,128)(2,1)} %copy-done.17, bf16[4,384,768]{2,1,0:T(8,128)(2,1)} %copy-done.15, ...), custom_call_target="tpu_custom_call" | custom-call | flops 72477573120 | bytes 30000000 | tf_op jit(solution)/shard_map/pallas_call | solution.py:580
  157.6 10.0 %all-to-all-done.4.refs_0_.refs_2_ = bf16[4,192,768]{2,1,0:T(8,128)(2,1)S(1)} async-done(((bf16[4,192,768]{2,1,0:T(8,128)(2,1)}), bf16[4,192,768]{2,1,0:T(8,128)(2,1)S(1)}, u32[]{:S(2)}, u32[]{:S(2)}) %all-to-all-start.4) | async-done | bytes 1179680 | tf_op jit(solution)/shard_map/all_to_all | solution.py:785
  173.9 26.1 %shard_map.221 = (bf16[4,384,768]{2,1,0:T(8,128)(2,1)}, bf16[4,384,768]{2,1,0:T(8,128)(2,1)}, bf16[768,3072]{1,0:T(8,128)(2,1)}, bf16[768,3072]{1,0:T(8,128)(2,1...) custom-call(bf16[4,192,768]{2,1,0:T(8,128)(2,1)} %copy-done.18, ...), custom_call_target="tpu_custom_call", output_to_operand_aliasing={{0}: (8, {}), {1}: (9, {})} | custom-call | flops 72477573120 | bytes 30000000 | tf_op jit(solution)/shard_map/pallas_call | solution.py:580
  204.2 11.3 %all-to-all-done.3.refs_0_.refs_1_.refs_3_ = bf16[4,384,768]{2,1,0:T(8,128)(2,1)S(1)} async-done(((bf16[4,384,768]{2,1,0:T(8,128)(2,1)}), bf16[4,384,768]{2,1,0:T(8,128)(2,1)S(1)}, u32[]{:S(2)}, u32[]{:S(2)}) %all-to-all-start.3) | async-done | bytes 2359328 | tf_op jit(solution)/shard_map/all_to_all | solution.py:785
  221.6 26.9 %shard_map.223 = (bf16[192,768]{1,0:T(8,128)(2,1)}, bf16[192,768]{1,0:T(8,128)(2,1)}, bf16[192,768]{1,0:T(8,128)(2,1)}, bf16[192,768]{1,0:T(8,128)(2,1)}, bf16[4...) custom-call(bf16[4,384,768]{2,1,0:T(8,128)(2,1)} %copy-done.14, ...), custom_call_target="tpu_custom_call" | custom-call | flops 72477573120 | bytes 30000000 | tf_op jit(solution)/shard_map/pallas_call | solution.py:580
  260.1 27.0 %shard_map.224 = (bf16[192,768]{1,0:T(8,128)(2,1)}, bf16[192,768]{1,0:T(8,128)(2,1)}, bf16[192,768]{1,0:T(8,128)(2,1)}, bf16[192,768]{1,0:T(8,128)(2,1)}, bf16[4...) custom-call(bf16[4,384,768]{2,1,0:T(8,128)(2,1)} %all-to-all-done.6., ...), custom_call_target="tpu_custom_call", output_to_operand_aliasing={{4}: (8, {})} | custom-call | flops 72477573120 | bytes 30000000 | tf_op jit(solution)/shard_map/pallas_call | solution.py:580
  292.8 19.6 %all-to-all-done.5.refs_11_.refs_4_ = bf16[4,384,768]{2,1,0:T(8,128)(2,1)S(1)} async-done(((bf16[4,384,768]{2,1,0:T(8,128)(2,1)}), bf16[4,384,768]{2,1,0:T(8,128)(2,1)S(1)}, u32[]{:S(2)}, u32[]{:S(2)}) %all-to-all-start.5) | async-done | bytes 2359328 | tf_op jit(solution)/shard_map/all_to_all | solution.py:785
  320.3 12.6 %shard_map.225.refs_9_ = bf16[1536,768]{1,0:T(8,128)(2,1)} custom-call(s32[1]{0:T(128)S(6)} %sub.3.refs_0_, bf16[768,3072]{1,0:T(8,128)(2,1)} %get-tuple-element.119.refs_1_, bf16[768,3072]{1,0:T(8,128)(2,1)} %get-tuple-element.120.refs_2_, bf16[768,3072]{1,0:T(8,128)(2,1)} %get-tuple-element.121.refs_3_, bf16[768,3072]{1,0:T(8,128)(2,1)} %get-tuple-element.122.refs_4_, ...), custom_call_target="tpu_custom_call" | custom-call | flops 36238786560 | bytes 15000000 | tf_op jit(solution)/shard_map/pallas_call | solution.py:628
  332.9 12.8 %shard_map.226.refs_10_ = bf16[384,3072]{1,0:T(8,128)(2,1)} custom-call(s32[1]{0:T(128)S(6)} %sub.3.refs_0_, bf16[4,192,768]{2,1,0:T(8,128)(2,1)} %copy-done.17, bf16[4,192,768]{2,1,0:T(8,128)(2,1)} %copy-done.18, bf16[4,384,768]{2,1,0:T(8,128)(2,1)} %copy-done.14, bf16[4,384,768]{2,1,0:T(8,128)(2,1)} %all-to-all-done.6.refs_0_.refs_1_.refs_4_, ...), custom_call_target="tpu_custom_call" | custom-call | flops 36238786560 | bytes 25000000 | tf_op jit(solution)/shard_map/pallas_call | solution.py:653
  351.2 13.0 %shard_map.227.refs_10_ = bf16[1536,768]{1,0:T(8,128)(2,1)} custom-call(s32[1]{0:T(128)} %bitcast.23.refs_0_, bf16[768,3072]{1,0:T(8,128)(2,1)} %get-tuple-element.119.refs_1_, bf16[768,3072]{1,0:T(8,128)(2,1)} %get-tuple-element.120.refs_2_, bf16[768,3072]{1,0:T(8,128)(2,1)} %get-tuple-element.121.refs_3_, bf16[768,3072]{1,0:T(8,128)(2,1)} %get-tuple-element.122.refs_4_, ...), custom_call_target="tpu_custom_call" | custom-call | flops 36238786560 | bytes 15000000 | tf_op jit(solution)/shard_map/pallas_call | solution.py:628
  368.4 13.1 %shard_map.228.refs_17_ = bf16[384,3072]{1,0:T(8,128)(2,1)} custom-call(s32[1]{0:T(128)} %bitcast.23.refs_0_, bf16[4,192,768]{2,1,0:T(8,128)(2,1)} %copy-done.17, bf16[4,192,768]{2,1,0:T(8,128)(2,1)} %copy-done.18, bf16[4,384,768]{2,1,0:T(8,128)(2,1)} %copy-done.14, bf16[4,384,768]{2,1,0:T(8,128)(2,1)} %all-to-all-done.6.refs_0_.refs_1_.refs_4_, ...), custom_call_target="tpu_custom_call" | custom-call | flops 36238786560 | bytes 25000000 | tf_op jit(solution)/shard_map/pallas_call | solution.py:653
  387.5 26.8 %shard_map.229 = (bf16[512,768]{1,0:T(8,128)(2,1)}, bf16[512,768]{1,0:T(8,128)(2,1)}, bf16[512,2304]{1,0:T(8,128)(2,1)}, bf16[512,768]{1,0:T(8,128)(2,1)}, f32[2,768]{1,0:T(2,128)}, /*index=5*/f32[12,1024]{1,0:T(8,128)}) custom-call(bf16[192,768]{1,0:T(8,128)(2,1)} %copy-done.35, bf16[192,768]{1,0:T(8,128)(2,1)} %copy-done.36, ...), custom_call_target="tpu_custom_call" | custom-call | flops 38252052480 | bytes 30000000 | tf_op jit(solution)/shard_map/pallas_call | solution.py:524
  426.3 27.0 %shard_map.231 = (bf16[512,768]{1,0:T(8,128)(2,1)}, bf16[512,768]{1,0:T(8,128)(2,1)}, bf16[512,2304]{1,0:T(8,128)(2,1)}, bf16[512,768]{1,0:T(8,128)(2,1)}, f32[2,768]{1,0:T(2,128)}, /*index=5*/f32[12,1024]{1,0:T(8,128)}) custom-call(bf16[192,768]{1,0:T(8,128)(2,1)} %copy-done.34, bf16[192,768]{1,0:T(8,128)(2,1)} %collective-permute-done.15.refs_19_.refs_1_, ...), custom_call_target="tpu_custom_call" | custom-call | flops 38252052480 | bytes 30000000 | tf_op jit(solution)/shard_map/pallas_call | solution.py:524
  456.3 6.0 %all-to-all-done.8.refs_14_.refs_0_ = bf16[4,384,768]{2,1,0:T(8,128)(2,1)S(1)} async-done(((bf16[4,384,768]{2,1,0:T(8,128)(2,1)}), bf16[4,384,768]{2,1,0:T(8,128)(2,1)S(1)}, u32[]{:S(2)}, u32[]{:S(2)}) %all-to-all-start.8) | async-done | bytes 2359328 | tf_op jit(solution)/shard_map/all_to_all | solution.py:785
  463.7 10.2 %shard_map.232 = (bf16[768,1536]{1,0:T(8,128)(2,1)}, bf16[768,1664]{1,0:T(8,128)(2,1)}) custom-call(bf16[512,768]{1,0:T(8,128)(2,1)} %get-tuple-element.129.refs_0_, bf16[512,768]{1,0:T(8,128)(2,1)} %get-tuple-element.141.refs_1_, bf16[512,2304]{1,0:T(8,128)(2,1)} %get-tuple-element.142.refs_2_, bf16[512,2304]{1,0:T(8,128)(2,1)} %get-tuple-element.143.refs_3_, ...), custom_call_target="tpu_custom_call" | custom-call | flops 24159191040 | bytes 20000000 | tf_op jit(solution)/shard_map/pallas_call | solution.py:686
  491.0 7.6 %shard_map.233.refs_6_ = f32[3072,768]{1,0:T(8,128)} custom-call(s32[1]{0:T(128)} %bitcast.23.refs_0_, bf16[1536,768]{1,0:T(8,128)(2,1)} %pad_maximum_fusion.refs_1_, bf16[1536,768]{1,0:T(8,128)(2,1)} %collective-permute-done.31.refs_2_, bf16[768,1536]{1,0:T(8,128)(2,1)} %get-tuple-element.156.refs_3_.refs_5_), custom_call_target="tpu_custom_call" | custom-call | flops 5898240 | bytes 20000000 | tf_op jit(solution)/shard_map/pallas_call | solution.py:670
  548.8 6.8 %collective-permute-done.37 = bf16[48,3200]{1,0:T(8,128)(2,1)S(1)} collective-permute-done((bf16[48,3200]{1,0:T(8,128)(2,1)S(1)}, bf16[48,3200]{1,0:T(8,128)(2,1)S(1)}, u32[]{:S(2)}, u32[]{:S(2)}) %collective-permute-start.37) | collective-permute-done | bytes 307232 | tf_op jit(solution)/shard_map/ppermute | solution.py:715
  559.2 10.6 %collective-permute-done.38 = bf16[96,3200]{1,0:T(8,128)(2,1)S(1)} collective-permute-done((bf16[96,3200]{1,0:T(8,128)(2,1)S(1)}, bf16[96,3200]{1,0:T(8,128)(2,1)S(1)}, u32[]{:S(2)}, u32[]{:S(2)}) %collective-permute-start.38) | collective-permute-done | bytes 614432 | tf_op jit(solution)/shard_map/ppermute | solution.py:715
  574.8 7.4 %shard_map.236 = f32[768,3072]{1,0:T(8,128)} custom-call(s32[1]{0:T(128)} %bitcast.23.refs_0_, bf16[384,3072]{1,0:T(8,128)(2,1)} %pad_maximum_fusion.1.refs_1_, bf16[384,3072]{1,0:T(8,128)(2,1)} %collective-permute-done.39.refs_2_, bf16[512,768]{1,0:T(8,128)(2,1)} %shard_map.235.refs_3_), custom_call_target="tpu_custom_call" | custom-call | flops 5898240 | bytes 20000000 | tf_op jit(solution)/shard_map/pallas_call | solution.py:670
  (262 shorter events, 208.2 us)
Async XLA Ops:
  7.2 49.9 %all-gather.2.cloned.1.call-start = ((), (), s32[]{:S(2)}) async-start(), calls=%async_computation.9 | async-start | bytes 5898240 | tf_op jit(solution)/shard_map/all_gather | solution.py:811
  46.0 40.2 %all-to-all-start.2 = ((bf16[4,384,768]{2,1,0:T(8,128)(2,1)}), bf16[4,384,768]{2,1,0:T(8,128)(2,1)S(1)}, u32[]{:S(2)}, u32[]{:S(2)}) async-start(bf16[4,384,768]{2,1,0:T(8,128)(2,1)} %shard_map.219), calls=%async_computation.2 | async-start | bytes 4718592 | tf_op jit(solution)/shard_map/all_to_all | solution.py:785
  49.7 40.2 %collective-permute-start.1 = (bf16[256,768]{1,0:T(8,128)(2,1)}, bf16[256,768]{1,0:T(8,128)(2,1)}, u32[]{:S(2)}, u32[]{:S(2)}) collective-permute-start(bf16[256,768]{1,0:T(8,128)(2,1)} %get-tuple-element.227), channel_id=1, source_target_pairs={{0,4},{1,5},{2,6},{3,7},{4,0},{5,1},{6,2},{7,3},{8,12},{9,13},{10,... | collective-permute-start | bytes 1179656 | tf_op jit(solution)/shard_map/ppermute | solution.py:715
  76.3 44.5 %collective-permute-start.4 = (bf16[512,768]{1,0:T(8,128)(2,1)}, bf16[512,768]{1,0:T(8,128)(2,1)}, u32[]{:S(2)}, u32[]{:S(2)}) collective-permute-start(bf16[512,768]{1,0:T(8,128)(2,1)} %get-tuple-element.92), channel_id=1, source_target_pairs={{0,4},{1,5},{2,6},{3,7},{4,0},{5,1},{6,2},{7,3},{8,12},{9,13},{10,... | collective-permute-start | bytes 2359304 | tf_op jit(solution)/shard_map/ppermute | solution.py:715
  86.2 41.6 %all-to-all-start.1 = ((bf16[4,192,768]{2,1,0:T(8,128)(2,1)}), bf16[4,192,768]{2,1,0:T(8,128)(2,1)S(1)}, u32[]{:S(2)}, u32[]{:S(2)}) async-start(bf16[4,192,768]{2,1,0:T(8,128)(2,1)} %get-tuple-element.94.refs_7_), calls=%async_computation.1 | async-start | bytes 2359296 | tf_op jit(solution)/shard_map/all_to_all | solution.py:785
  120.7 79.2 %collective-permute-start.5 = (bf16[512,768]{1,0:T(8,128)(2,1)}, bf16[512,768]{1,0:T(8,128)(2,1)}, u32[]{:S(2)}, u32[]{:S(2)}) collective-permute-start(bf16[512,768]{1,0:T(8,128)(2,1)} %slice_bitcast_fusion), channel_id=1, source_target_pairs={{0,4},{1,5},{2,6},{3,7},{4,0},{5,1},{6,2},{7,3},{8,12},{9,13},{10,... | collective-permute-start | bytes 2359304 | tf_op jit(solution)/shard_map/ppermute | solution.py:715
  120.7 79.3 %collective-permute-start.6 = (bf16[512,768]{1,0:T(8,128)(2,1)}, bf16[512,768]{1,0:T(8,128)(2,1)}, u32[]{:S(2)}, u32[]{:S(2)}) collective-permute-start(bf16[512,768]{1,0:T(8,128)(2,1)} %get-tuple-element.101), channel_id=1, source_target_pairs={{0,4},{1,5},{2,6},{3,7},{4,0},{5,1},{6,2},{7,3},{8,12},{9,13},{10,... | collective-permute-start | bytes 2359304 | tf_op jit(solution)/shard_map/ppermute | solution.py:715
  127.8 39.8 %all-to-all-start.4 = ((bf16[4,192,768]{2,1,0:T(8,128)(2,1)}), bf16[4,192,768]{2,1,0:T(8,128)(2,1)S(1)}, u32[]{:S(2)}, u32[]{:S(2)}) async-start(bf16[4,192,768]{2,1,0:T(8,128)(2,1)} %get-tuple-element.95.refs_5_), calls=%async_computation.4 | async-start | bytes 2359296 | tf_op jit(solution)/shard_map/all_to_all | solution.py:785
  168.6 46.9 %all-to-all-start.3 = ((bf16[4,384,768]{2,1,0:T(8,128)(2,1)}), bf16[4,384,768]{2,1,0:T(8,128)(2,1)S(1)}, u32[]{:S(2)}, u32[]{:S(2)}) async-start(bf16[4,384,768]{2,1,0:T(8,128)(2,1)} %shard_map.218.refs_8_), calls=%async_computation.3 | async-start | bytes 4718592 | tf_op jit(solution)/shard_map/all_to_all | solution.py:785
  216.9 39.3 %all-to-all-start.6 = ((bf16[4,384,768]{2,1,0:T(8,128)(2,1)}), bf16[4,384,768]{2,1,0:T(8,128)(2,1)}, u32[]{:S(2)}, u32[]{:S(2)}) async-start(bf16[4,384,768]{2,1,0:T(8,128)(2,1)} %shard_map.222.refs_8_), calls=%async_computation.6 | async-start | bytes 4718592 | tf_op jit(solution)/shard_map/all_to_all | solution.py:785
  248.5 41.9 %collective-permute-start.7 = (bf16[192,768]{1,0:T(8,128)(2,1)}, bf16[192,768]{1,0:T(8,128)(2,1)S(1)}, u32[]{:S(2)}, u32[]{:S(2)}) collective-permute-start(bf16[192,768]{1,0:T(8,128)(2,1)} %get-tuple-element.104), channel_id=1, source_target_pairs={{0,4},{1,5},{2,6},{3,7},{4,0},{5,1},{6,2},{7,3},{8,12},{9,13},{10,... | collective-permute-start | bytes 884744 | tf_op jit(solution)/shard_map/ppermute | solution.py:715
  249.6 69.3 %collective-permute-start.8 = (bf16[192,768]{1,0:T(8,128)(2,1)}, bf16[192,768]{1,0:T(8,128)(2,1)S(1)}, u32[]{:S(2)}, u32[]{:S(2)}) collective-permute-start(bf16[192,768]{1,0:T(8,128)(2,1)} %get-tuple-element.105), channel_id=1, source_target_pairs={{0,5},{1,4},{2,7},{3,6},{4,1},{5,0},{6,3},{7,2},{8,13},{9,12},{10,... | collective-permute-start | bytes 884744 | tf_op jit(solution)/shard_map/ppermute | solution.py:715
  252.9 79.9 %collective-permute-start.9 = (bf16[192,768]{1,0:T(8,128)(2,1)}, bf16[192,768]{1,0:T(8,128)(2,1)}, u32[]{:S(2)}, u32[]{:S(2)}) collective-permute-start(bf16[192,768]{1,0:T(8,128)(2,1)} %get-tuple-element.106), channel_id=1, source_target_pairs={{0,6},{1,7},{2,4},{3,5},{4,2},{5,3},{6,0},{7,1},{8,14},{9,15},{10,... | collective-permute-start | bytes 884744 | tf_op jit(solution)/shard_map/ppermute | solution.py:715
  255.2 90.6 %collective-permute-start.10 = (bf16[192,768]{1,0:T(8,128)(2,1)}, bf16[192,768]{1,0:T(8,128)(2,1)}, u32[]{:S(2)}, u32[]{:S(2)}) collective-permute-start(bf16[192,768]{1,0:T(8,128)(2,1)} %get-tuple-element.107), channel_id=1, source_target_pairs={{0,7},{1,6},{2,5},{3,4},{4,3},{5,2},{6,1},{7,0},{8,15},{9,14},{10,... | collective-permute-start | bytes 884744 | tf_op jit(solution)/shard_map/ppermute | solution.py:715
  256.2 56.2 %all-to-all-start.5 = ((bf16[4,384,768]{2,1,0:T(8,128)(2,1)}), bf16[4,384,768]{2,1,0:T(8,128)(2,1)S(1)}, u32[]{:S(2)}, u32[]{:S(2)}) async-start(bf16[4,384,768]{2,1,0:T(8,128)(2,1)} %get-tuple-element.109), calls=%async_computation.5 | async-start | bytes 4718592 | tf_op jit(solution)/shard_map/all_to_all | solution.py:785
  287.0 79.9 %collective-permute-start.13 = (bf16[192,768]{1,0:T(8,128)(2,1)}, bf16[192,768]{1,0:T(8,128)(2,1)S(1)}, u32[]{:S(2)}, u32[]{:S(2)}) collective-permute-start(bf16[192,768]{1,0:T(8,128)(2,1)} %get-tuple-element.127), channel_id=1, source_target_pairs={{0,4},{1,5},{2,6},{3,7},{4,0},{5,1},{6,2},{7,3},{8,12},{9,13},{10,... | collective-permute-start | bytes 884744 | tf_op jit(solution)/shard_map/ppermute | solution.py:715
  290.4 95.0 %collective-permute-start.15 = (bf16[192,768]{1,0:T(8,128)(2,1)}, bf16[192,768]{1,0:T(8,128)(2,1)}, u32[]{:S(2)}, u32[]{:S(2)}) collective-permute-start(bf16[192,768]{1,0:T(8,128)(2,1)} %get-tuple-element.128), channel_id=1, source_target_pairs={{0,5},{1,4},{2,7},{3,6},{4,1},{5,0},{6,3},{7,2},{8,13},{9,12},{10,... | collective-permute-start | bytes 884744 | tf_op jit(solution)/shard_map/ppermute | solution.py:715
  313.9 100.4 %all-to-all-start.7 = ((bf16[4,384,768]{2,1,0:T(8,128)(2,1)}), bf16[4,384,768]{2,1,0:T(8,128)(2,1)}, u32[]{:S(2)}, u32[]{:S(2)}) async-start(bf16[4,384,768]{2,1,0:T(8,128)(2,1)} %get-tuple-element.138), calls=%async_computation.7 | async-start | bytes 4718592 | tf_op jit(solution)/shard_map/all_to_all | solution.py:785
  318.9 103.4 %collective-permute-start.16 = (bf16[192,768]{1,0:T(8,128)(2,1)}, bf16[192,768]{1,0:T(8,128)(2,1)}, u32[]{:S(2)}, u32[]{:S(2)}) collective-permute-start(bf16[192,768]{1,0:T(8,128)(2,1)} %get-tuple-element.130), channel_id=1, source_target_pairs={{0,6},{1,7},{2,4},{3,5},{4,2},{5,3},{6,0},{7,1},{8,14},{9,15},{10,... | collective-permute-start | bytes 884744 | tf_op jit(solution)/shard_map/ppermute | solution.py:715
  345.7 77.7 %collective-permute-start.17 = (bf16[192,768]{1,0:T(8,128)(2,1)}, bf16[192,768]{1,0:T(8,128)(2,1)}, u32[]{:S(2)}, u32[]{:S(2)}) collective-permute-start(bf16[192,768]{1,0:T(8,128)(2,1)} %get-tuple-element.131), channel_id=1, source_target_pairs={{0,7},{1,6},{2,5},{3,4},{4,3},{5,2},{6,1},{7,0},{8,15},{9,14},{10,... | collective-permute-start | bytes 884744 | tf_op jit(solution)/shard_map/ppermute | solution.py:715
  384.7 77.6 %collective-permute-start.21 = (bf16[96,3072]{1,0:T(8,128)(2,1)}, bf16[96,3072]{1,0:T(8,128)(2,1)}, u32[]{:S(2)}, u32[]{:S(2)}) collective-permute-start(bf16[96,3072]{1,0:T(8,128)(2,1)} %get-tuple-element.218), channel_id=1, source_target_pairs={{0,16},{8,24},{16,0},{24,8},{1,17},{9,25},{17,1},{25,9},{2,18},{10... | collective-permute-start | bytes 1769480 | tf_op jit(solution)/shard_map/ppermute | solution.py:715
  386.7 39.5 %collective-permute-start.19 = (bf16[384,768]{1,0:T(8,128)(2,1)}, bf16[384,768]{1,0:T(8,128)(2,1)}, u32[]{:S(2)}, u32[]{:S(2)}) collective-permute-start(bf16[384,768]{1,0:T(8,128)(2,1)} %get-tuple-element.224), channel_id=1, source_target_pairs={{0,16},{8,24},{16,0},{24,8},{1,17},{9,25},{17,1},{25,9},{2,18},{10... | collective-permute-start | bytes 1769480 | tf_op jit(solution)/shard_map/ppermute | solution.py:715
  414.3 47.9 %all-to-all-start.8 = ((bf16[4,384,768]{2,1,0:T(8,128)(2,1)}), bf16[4,384,768]{2,1,0:T(8,128)(2,1)S(1)}, u32[]{:S(2)}, u32[]{:S(2)}) async-start(bf16[4,384,768]{2,1,0:T(8,128)(2,1)} %get-tuple-element.155.refs_4_), calls=%async_computation.8 | async-start | bytes 4718592 | tf_op jit(solution)/shard_map/all_to_all | solution.py:785
  422.2 40.1 %collective-permute-start.22 = (bf16[96,3072]{1,0:T(8,128)(2,1)}, bf16[96,3072]{1,0:T(8,128)(2,1)}, u32[]{:S(2)}, u32[]{:S(2)}) collective-permute-start(bf16[96,3072]{1,0:T(8,128)(2,1)} %get-tuple-element.217), channel_id=1, source_target_pairs={{0,16},{8,24},{16,0},{24,8},{1,17},{9,25},{17,1},{25,9},{2,18},{10... | collective-permute-start | bytes 1769480 | tf_op jit(solution)/shard_map/ppermute | solution.py:715
  (65 other events, 756.2 us)
Sparse Core Ops, SparseCore 0:
  10.2 42.2 all-gather.1

commit v4 on v3

--- a/solution.py
+++ b/solution.py
@@ -205,11 +205,11 @@
 ):
     _, length, width = cot_ref.shape
     scale = HEAD ** (-0.5)
-    near, capacity = own_ref.shape[0], own_ref.shape[1] // 2
+    near, capacity, _ = own_ref.shape
     mine = mine_ref[0, 0]
     base = mine // near * near
     for d in range(near):
-        own = own_ref[d, part * capacity : (part + 1) * capacity, :]
+        own = own_ref[d]
         back_ref[pl.ds(pl.multiple_of((base + d) * capacity, 16), capacity), :] = own
         back_ref[pl.ds(pl.multiple_of((mine ^ (near | d)) * capacity, 16), capacity), :] = far_refs[d][...]
     fill_pick(col_ref, pick_ref)
@@ -383,7 +383,7 @@
                         back_refs[e][...] = back
             else:
                 back_ref[at, :] = back
-                copies.append(pltpu.make_async_copy(back_ref.at[at, :], back_refs[0].at[d, here, :], sem.at[1, d]))
+                copies.append(pltpu.make_async_copy(back_ref.at[at, :], back_refs[0].at[d], sem.at[1, d]))
                 copies[-1].start()
         both = dot_tn(jnp.concatenate(parts, axis=0), rows)
         grad_router_ref[...] = both[:LANES] + both[LANES:]
@@ -519,7 +519,7 @@
 ):
     _, length, width = x.shape
     heads = width // HEAD
-    near, capacity = own.shape[0], own.shape[1] // 2
+    near, capacity, _ = own.shape
     total = 2 * near * capacity
     return pl.pallas_call(
         later(functools.partial(backward_kernel, near, part), near + 13, len(after)),
@@ -573,10 +573,10 @@
         back_specs = tuple(whole((capacity, width)) for _ in range(near))
         back_shapes = tuple(shaped((capacity, width), BF16) for _ in range(near))
     else:
-        back_specs, back_shapes = (anywhere,), (shared,)
+        back_specs, back_shapes = (anywhere,), (shaped((near, capacity, width), BF16),)
     count = len(back_specs)
     alias = len(earlier)
-    targets = (count,) if kind else (0, 1)
+    targets = (count,)
     outs = pl.pallas_call(
         later(functools.partial(expert_kernel, kind, near, alias, part), 8 + alias, len(after)),
         grid=(inner // step,),
@@ -728,9 +728,9 @@
     return pair_sum(kept, swap(sent, name, size, bit))
 
 
-def unite(value, name, size, bit):
+def unite(value, name, size, bit, after=lambda step, value: value):
     odd = (lax.axis_index(name) & bit) > 0
-    other = swap(value, name, size, bit)
+    other = after(20, swap(value, name, size, bit))
     return jnp.concatenate([jnp.where(odd, other, value), jnp.where(odd, value, other)], axis=0)
 
 
@@ -747,6 +747,7 @@
         return value
 
     left, right = split(left), split(right)
+    after(-1, left)
     left = after(0, along_dp(left))
     right = halve(right, 1, "expert", experts, 1)
     left = halve(left, 1, "expert", experts, 1)
@@ -758,7 +759,7 @@
         step, bit = step + 1, bit * 2
     while bit > 1:
         bit //= 2
-        rows = unite(rows, "expert", experts, bit)
+        rows = unite(rows, "expert", experts, bit, *([after] if bit == 1 else []))
         rows = after({4: 8, 2: 9}.get(bit), rows)
     return rows.astype(F32)
 
@@ -847,12 +848,12 @@
         near, capacity, (places[0][1], [(cot0_top, None), (cot0_end, None)]), (places[0][1], [(second0_far, None)]),
         after=[send1],
     )
-    back_own, out_own, kept0_own = expert(
+    back0_own, out_own, kept0_own = expert(
         0, 0, (own0, 0), (cot_own, 0), ids_all[0], *common, (), [far0_send]
     )
     far0 = around(order(far0_send, out_own)[0])
-    back_own, out_own, kept1_own = expert(
-        0, 1, (own1, 0), (cot_own, 1), ids_all[1], *common, (back_own, out_own), []
+    back1_own, out_own, kept1_own = expert(
+        0, 1, (own1, 0), (cot_own, 1), ids_all[1], *common, (out_own,), []
     )
     far1_send = scatter(
         near, capacity, (places[1][1], [(cot1_far, None)]), (places[1][1], [(second1_far, None)]), after=[out_own],
@@ -860,8 +861,8 @@
     far1 = around(far1_send)
     back0_far, out_far, kept0_far = expert(1, 0, (far0, 1), (far0, 0), ids_all[0], *common, (), [far1_send])
     back1_far, out_far, kept1_far = expert(1, 1, (far1, 1), (far1, 0), ids_all[1], *common, (out_far,), [])
-    back_own, out_own, _ = order(back_own, out_own, back0_far[0])
-    back_own, out_own, out_far = around(back_own), around(out_own), around(out_far)
+    back0_own, _ = order(back0_own, back0_far[0])
+    back0_own, out_far = around(back0_own), around(out_far)
     home = [
         [cross(block, near | d) for d, block in enumerate(back0_far)],
         [cross(block, near | d) for d, block in enumerate(back1_far)],
@@ -875,13 +876,16 @@
 
     home0, home1 = home
     other = 1 - odd
-    last_part = last_grad(other, acts, scaled, None, home0[: 2 * quarter] + [back_own])
+    last_part = last_grad(other, acts, scaled, None, home0[: 2 * quarter] + [back0_own])
     last_got = swap(last_part, "dp", dp, 1)
     first_part = first_grad(other, rows, ups, None, [last_part] + home0[2 * quarter : 3 * quarter])
     first_got = swap(first_part, "dp", dp, 1)
     last_sum = last_grad(odd, acts, scaled, last_got, [first_part] + home0[3 * quarter :])
     first_sum = first_grad(odd, rows, ups, first_got, [last_sum] + home1[:quarter])
     first_whole = first_sum
+    back1_own = around(order(back1_own, first_sum)[0])
+    out_own = around(order(out_own, back1_own)[0])
+    back_own = [back0_own, back1_own]
 
     def over_dp(value):
         bit = 2
@@ -902,13 +906,14 @@
     def layer_back(m, after):
         proj, mixed, totals, hidden, block_row, block_col = kept[m]
         return backward(
-            m, back_own, home[m], mine, places[m][2], cotangent, hidden, gains, packed, proj, totals, strip,
+            m, back_own[m], home[m], mine, places[m][2], cotangent, hidden, gains, packed, proj, totals, strip,
             block_row, block_col, inputs, after,
         )
 
     back_outs = [layer_back(0, [first_whole, last_came[0]] + home1[quarter : 2 * quarter])]
     out_sums = gather((places[0][3], places[1][3]), mine, out_far, [back_outs[0][1]])
-    out0_far, out1_far = cross(out_sums[0], near), cross(out_sums[1], near)
+    out0_top, out0_end = cross(out_sums[0][:middle], near), cross(out_sums[0][middle:], near)
+    out1_far = cross(out_sums[1], near)
     back_outs.append(layer_back(1, [last_came[1], last_came[2], out_sums[0]]))
 
     gain_grads = back_outs[0][4] + back_outs[1][4]
@@ -923,20 +928,29 @@
     left, right = dense_grad(
         back_outs[0][3], back_outs[1][3], back_outs[0][2], back_outs[1][2],
         kept[0][1], kept[1][1], back_outs[0][1], back_outs[1][1], small_grad,
-        after=[last_came[3], *first_came, out0_far, out_own],
-    )
-    results = [combine(out_own, 0, out0_far, mine, places[0][2], kept[0][3], [left])]
+        after=[last_came[3], *first_came, out0_top, out_own],
+    )
     last_sum = jnp.concatenate(last_sum, axis=0)
-    grad_last = join(odd, last_sum, swap(last_sum, "dp", dp, 1), [left])
+    grad_last = None
+
+    results, grad_first = [], None
 
     def after(step, value):
-        nonlocal grad_last, out1_far
+        nonlocal grad_first, grad_last, out0_end, out1_far
+        if step == -1:
+            grad_last = join(odd, last_sum, swap(last_sum, "dp", dp, 1), [value])
         if step == 1:
-            value, grad_last, out1_far, *rest = order(value, grad_last, out1_far, *first_sum[3:])
+            value, grad_last, out0_end, out1_far, *rest = order(value, grad_last, out0_end, out1_far, *first_sum[3:])
+            out0_far = jnp.concatenate([out0_top, out0_end], axis=0)
+            results.append(combine(out_own, 0, out0_far, mine, places[0][2], kept[0][3], [grad_last]))
             results.append(combine(out_own, 1, out1_far, mine, places[1][2], kept[1][3], [results[0], grad_last]))
             rest, came = zip(*[over_dp(piece) for piece in rest])
             first_sum[3:] = rest
             first_came.extend(came)
+        if step == 20:
+            whole = jnp.concatenate(first_sum, axis=0)
+            grad_first = join(odd, whole, swap(whole, "dp", dp, 1), [results[1]])
+            value, grad_first = order(value, grad_first)
         if step == 2:
             value, results[0] = order(value, results[0])
         if step == 3:
@@ -946,8 +960,6 @@
         return value
 
     dense = dense_sum(left, right, dp, experts, after)
-    first_sum = jnp.concatenate(first_sum, axis=0)
-    grad_first = join(odd, first_sum, swap(first_sum, "dp", dp, 1), [results[1]])
     tail = dense[:, 4 * width :]
     return (
         jnp.stack(results),

time: 600 us -> 583 us (0.972)
  waiting for transfers between devices: 123 us -> 89.6 us
  starting transfers between devices: 83.7 us -> 96.8 us
    all_to_all x8 -> x9, waiting for transfers between devices: 55.4 us -> 36.6 us  [around(): lax.all_to_all(blocks, 'expert', split_axis=0, concat_axis=0, axis_index_...]
    ppermute x40 -> x41, waiting for transfers between devices: 67.6 us -> 52.9 us  [swap(): return lax.ppermute(value, axis, [(i, i ^ bit) for i in range(size)])]
    ppermute x40 -> x41, starting transfers between devices: 43.1 us -> 51.7 us  [swap(): return lax.ppermute(value, axis, [(i, i ^ bit) for i in range(size)])]
    all_to_all x8 -> x9, starting transfers between devices: 33.7 us -> 38.2 us  [around(): lax.all_to_all(blocks, 'expert', split_axis=0, concat_axis=0, axis_index_...]
    unnamed x84 -> x104, local copies, waits for them, and re-layouts: 11 us -> 13.8 us
  transfers between devices with their start and end apart: 50 -> 52, of which waited for: 22 -> 15; matrix products, arithmetic and copies ran while one was open for 8% -> 8% of each run, Pallas kernels for 49% -> 54%
where the time goes in v4:
time: 583 us; the launch traced here: 573 us
  Pallas kernels  308 us (53%)
  starting transfers between devices  96.8 us (17%)
  waiting for transfers between devices  89.6 us (15%)
  local copies, waits for them, and re-layouts  34 us (6%)
  other arithmetic  28 us (5%)
  between operations  15.3 us (3%)
    pallas_call x4, Pallas kernels, expert(): pl.pallas_call(later(functools.partial(expert_kernel, kind, near, alias,...  106 us
    ppermute x41, waiting for transfers between devices, swap(): return lax.ppermute(value, axis, [(i, i ^ bit) for i in range(size)])  52.9 us
    pallas_call x2, Pallas kernels, backward(): pl.pallas_call(later(functools.partial(backward_kernel, near, part), near...  52.7 us
    ppermute x41, starting transfers between devices, swap(): return lax.ppermute(value, axis, [(i, i ^ bit) for i in range(size)])  51.7 us
    pallas_call x2, Pallas kernels, forward(): pl.pallas_call(later(functools.partial(forward_kernel, m), 7, len(after))...  38.2 us
    all_to_all x9, starting transfers between devices, around(): lax.all_to_all(blocks, 'expert', split_axis=0, concat_axis=0, axis_index_...  38.2 us
    all_to_all x9, waiting for transfers between devices, around(): lax.all_to_all(blocks, 'expert', split_axis=0, concat_axis=0, axis_index_...  36.6 us
    pallas_call x2, Pallas kernels, first_grad(): pl.pallas_call(later(functools.partial(expert_grad_kernel, len(ups), Fals...  26 us
  transfers between devices with their start and end apart: 52, of which 15 were waited for; matrix products, arithmetic and copies ran while one was open for 8% of the time, Pallas kernels for 54%

profile of v4, /device:TPU:0, one launch (start us, length us, event | category | flops | bytes accessed | tf_op | source)
XLA Modules:
  0.0 573.4 jit_solution(894580442797375636)
XLA Ops:
  11.2 6.8 %all-to-all-start = ((s32[8,2,2,512]{3,2,1,0:T(2,128)}), s32[8,2,2,512]{3,2,1,0:T(2,128)S(1)}, u32[]{:S(2)}, u32[]{:S(2)}) async-start(s32[8,2,2,512]{3,2,1,0:T(2,128)} %broadcast_in_dim.21), calls=%async_computation | async-start | bytes 131072 | tf_op jit(solution)/shard_map/all_to_all | solution.py:797
  57.1 19.1 %shard_map.215 = (bf16[512,2304]{1,0:T(8,128)(2,1)}, bf16[512,768]{1,0:T(8,128)(2,1)}, f32[512,128]{1,0:T(8,128)}, f32[512,768]{1,0:T(8,128)}, bf16[512,768]{1,0:T(8,128)(2,1)}, /*index=5*/bf16[4,192,768]{2,1,0:T(8,128)(2,1)}) custom-call(bf16[2,512,768]{2,1,0:T(8,128)(2,1)} %refs_16_.3, f32[2,768]{1,0:T(2,128)} %convert_bitcast_fusion.gains_ref.refs_1_.refs_9_, ...), custom_call_target="tpu_custom_call" | custom-call | flops 20132659200 | bytes 24000000 | tf_op jit(solution)/shard_map/pallas_call | solution.py:495
  77.8 8.4 %all-to-all-done.2.refs_1_ = bf16[4,384,768]{2,1,0:T(8,128)(2,1)S(1)} async-done(((bf16[4,384,768]{2,1,0:T(8,128)(2,1)}), bf16[4,384,768]{2,1,0:T(8,128)(2,1)S(1)}, u32[]{:S(2)}, u32[]{:S(2)}) %all-to-all-start.2) | async-done | bytes 2359328 | tf_op jit(solution)/shard_map/all_to_all | solution.py:786
  90.0 19.1 %shard_map.217 = (bf16[512,2304]{1,0:T(8,128)(2,1)}, bf16[512,768]{1,0:T(8,128)(2,1)}, f32[512,128]{1,0:T(8,128)}, f32[512,768]{1,0:T(8,128)}, bf16[512,768]{1,0:T(8,128)(2,1)}, /*index=5*/bf16[4,192,768]{2,1,0:T(8,128)(2,1)}) custom-call(bf16[2,512,768]{2,1,0:T(8,128)(2,1)} %refs_16_.3, f32[2,768]{1,0:T(2,128)} %convert_bitcast_fusion.gains_ref.refs_1_.refs_9_, ...), custom_call_target="tpu_custom_call" | custom-call | flops 20132659200 | bytes 24000000 | tf_op jit(solution)/shard_map/pallas_call | solution.py:495
  109.1 11.6 %collective-permute-done.4.refs_4_ = bf16[512,768]{1,0:T(8,128)(2,1)} collective-permute-done((bf16[512,768]{1,0:T(8,128)(2,1)}, bf16[512,768]{1,0:T(8,128)(2,1)}, u32[]{:S(2)}, u32[]{:S(2)}) %collective-permute-start.4) | collective-permute-done | bytes 786464 | tf_op jit(solution)/shard_map/ppermute | solution.py:715
  131.9 26.0 %shard_map.220 = (bf16[4,192,768]{2,1,0:T(8,128)(2,1)}, bf16[4,384,768]{2,1,0:T(8,128)(2,1)}, bf16[768,3072]{1,0:T(8,128)(2,1)}, bf16[768,3072]{1,0:T(8,128)(2,1...) custom-call(bf16[4,192,768]{2,1,0:T(8,128)(2,1)} %copy-done.22, bf16[4,384,768]{2,1,0:T(8,128)(2,1)} %copy-done.19, ...), custom_call_target="tpu_custom_call" | custom-call | flops 72477573120 | bytes 30000000 | tf_op jit(solution)/shard_map/pallas_call | solution.py:580
  157.9 9.6 %all-to-all-done.4.refs_0_.refs_2_ = bf16[4,192,768]{2,1,0:T(8,128)(2,1)S(1)} async-done(((bf16[4,192,768]{2,1,0:T(8,128)(2,1)}), bf16[4,192,768]{2,1,0:T(8,128)(2,1)S(1)}, u32[]{:S(2)}, u32[]{:S(2)}) %all-to-all-start.4) | async-done | bytes 1179680 | tf_op jit(solution)/shard_map/all_to_all | solution.py:786
  173.6 26.1 %shard_map.221 = (bf16[4,192,768]{2,1,0:T(8,128)(2,1)}, bf16[4,384,768]{2,1,0:T(8,128)(2,1)}, bf16[768,3072]{1,0:T(8,128)(2,1)}, bf16[768,3072]{1,0:T(8,128)(2,1...) custom-call(bf16[4,192,768]{2,1,0:T(8,128)(2,1)} %copy-done.23, ...), custom_call_target="tpu_custom_call", output_to_operand_aliasing={{1}: (8, {})} | custom-call | flops 72477573120 | bytes 30000000 | tf_op jit(solution)/shard_map/pallas_call | solution.py:580
  204.0 11.5 %all-to-all-done.3.refs_0_.refs_1_.refs_3_ = bf16[4,384,768]{2,1,0:T(8,128)(2,1)S(1)} async-done(((bf16[4,384,768]{2,1,0:T(8,128)(2,1)}), bf16[4,384,768]{2,1,0:T(8,128)(2,1)S(1)}, u32[]{:S(2)}, u32[]{:S(2)}) %all-to-all-start.3) | async-done | bytes 2359328 | tf_op jit(solution)/shard_map/all_to_all | solution.py:786
  221.7 26.9 %shard_map.223 = (bf16[192,768]{1,0:T(8,128)(2,1)}, bf16[192,768]{1,0:T(8,128)(2,1)}, bf16[192,768]{1,0:T(8,128)(2,1)}, bf16[192,768]{1,0:T(8,128)(2,1)}, bf16[4...) custom-call(bf16[4,384,768]{2,1,0:T(8,128)(2,1)} %copy-done.18, ...), custom_call_target="tpu_custom_call" | custom-call | flops 72477573120 | bytes 30000000 | tf_op jit(solution)/shard_map/pallas_call | solution.py:580
  260.1 27.0 %shard_map.224 = (bf16[192,768]{1,0:T(8,128)(2,1)}, bf16[192,768]{1,0:T(8,128)(2,1)}, bf16[192,768]{1,0:T(8,128)(2,1)}, bf16[192,768]{1,0:T(8,128)(2,1)}, bf16[4...) custom-call(bf16[4,384,768]{2,1,0:T(8,128)(2,1)} %all-to-all-done.6., ...), custom_call_target="tpu_custom_call", output_to_operand_aliasing={{4}: (8, {})} | custom-call | flops 72477573120 | bytes 30000000 | tf_op jit(solution)/shard_map/pallas_call | solution.py:580
  292.9 5.6 all-to-all-done.5.refs_11_.refs_4_
  307.1 12.6 %shard_map.225.refs_9_ = bf16[1536,768]{1,0:T(8,128)(2,1)} custom-call(s32[1]{0:T(128)S(6)} %sub.3.refs_0_, bf16[768,3072]{1,0:T(8,128)(2,1)} %get-tuple-element.122.refs_1_, bf16[768,3072]{1,0:T(8,128)(2,1)} %get-tuple-element.123.refs_2_, bf16[768,3072]{1,0:T(8,128)(2,1)} %get-tuple-element.124.refs_3_, bf16[768,3072]{1,0:T(8,128)(2,1)} %get-tuple-element.125.refs_4_, ...), custom_call_target="tpu_custom_call" | custom-call | flops 36238786560 | bytes 15000000 | tf_op jit(solution)/shard_map/pallas_call | solution.py:628
  320.4 12.9 %shard_map.226.refs_10_ = bf16[384,3072]{1,0:T(8,128)(2,1)} custom-call(s32[1]{0:T(128)S(6)} %sub.3.refs_0_, bf16[4,192,768]{2,1,0:T(8,128)(2,1)} %copy-done.22, bf16[4,192,768]{2,1,0:T(8,128)(2,1)} %copy-done.23, bf16[4,384,768]{2,1,0:T(8,128)(2,1)} %copy-done.18, bf16[4,384,768]{2,1,0:T(8,128)(2,1)} %all-to-all-done.6.refs_0_.refs_1_.refs_4_, ...), custom_call_target="tpu_custom_call" | custom-call | flops 36238786560 | bytes 25000000 | tf_op jit(solution)/shard_map/pallas_call | solution.py:653
  336.1 13.1 %shard_map.227.refs_10_ = bf16[1536,768]{1,0:T(8,128)(2,1)} custom-call(s32[1]{0:T(128)} %bitcast.23.refs_0_, bf16[768,3072]{1,0:T(8,128)(2,1)} %get-tuple-element.122.refs_1_, bf16[768,3072]{1,0:T(8,128)(2,1)} %get-tuple-element.123.refs_2_, bf16[768,3072]{1,0:T(8,128)(2,1)} %get-tuple-element.124.refs_3_, bf16[768,3072]{1,0:T(8,128)(2,1)} %get-tuple-element.125.refs_4_, ...), custom_call_target="tpu_custom_call" | custom-call | flops 36238786560 | bytes 15000000 | tf_op jit(solution)/shard_map/pallas_call | solution.py:628
  354.9 13.1 %shard_map.228.refs_17_ = bf16[384,3072]{1,0:T(8,128)(2,1)} custom-call(s32[1]{0:T(128)} %bitcast.23.refs_0_, bf16[4,192,768]{2,1,0:T(8,128)(2,1)} %copy-done.22, bf16[4,192,768]{2,1,0:T(8,128)(2,1)} %copy-done.23, bf16[4,384,768]{2,1,0:T(8,128)(2,1)} %copy-done.18, bf16[4,384,768]{2,1,0:T(8,128)(2,1)} %all-to-all-done.6.refs_0_.refs_1_.refs_4_, ...), custom_call_target="tpu_custom_call" | custom-call | flops 36238786560 | bytes 25000000 | tf_op jit(solution)/shard_map/pallas_call | solution.py:653
  377.4 26.3 %shard_map.229 = (bf16[512,768]{1,0:T(8,128)(2,1)}, bf16[512,768]{1,0:T(8,128)(2,1)}, bf16[512,2304]{1,0:T(8,128)(2,1)}, bf16[512,768]{1,0:T(8,128)(2,1)}, f32[2,768]{1,0:T(2,128)}, /*index=5*/f32[12,1024]{1,0:T(8,128)}) custom-call(bf16[192,768]{1,0:T(8,128)(2,1)} %copy-done.44, bf16[192,768]{1,0:T(8,128)(2,1)} %copy-done.45, bf16[192,768]{1,0:T(8,128)(2,1)} %copy-done.46, ...), custom_call_target="tpu_custom_call" | custom-call | flops 38252052480 | bytes 30000000 | tf_op jit(solution)/shard_map/pallas_call | solution.py:524
  423.6 26.4 %shard_map.231 = (bf16[512,768]{1,0:T(8,128)(2,1)}, bf16[512,768]{1,0:T(8,128)(2,1)}, bf16[512,2304]{1,0:T(8,128)(2,1)}, bf16[512,768]{1,0:T(8,128)(2,1)}, f32[2,768]{1,0:T(2,128)}, /*index=5*/f32[12,1024]{1,0:T(8,128)}) custom-call(bf16[192,768]{1,0:T(8,128)(2,1)} %collective-permute-done.13.refs_11_.refs_0_, ...), custom_call_target="tpu_custom_call" | custom-call | flops 38252052480 | bytes 30000000 | tf_op jit(solution)/shard_map/pallas_call | solution.py:524
  458.8 10.3 %shard_map.232 = (bf16[768,1536]{1,0:T(8,128)(2,1)}, bf16[768,1664]{1,0:T(8,128)(2,1)}) custom-call(bf16[512,768]{1,0:T(8,128)(2,1)} %get-tuple-element.132.refs_0_, bf16[512,768]{1,0:T(8,128)(2,1)} %get-tuple-element.146.refs_1_, bf16[512,2304]{1,0:T(8,128)(2,1)} %get-tuple-element.147.refs_2_, bf16[512,2304]{1,0:T(8,128)(2,1)} %get-tuple-element.148.refs_3_, ...), custom_call_target="tpu_custom_call" | custom-call | flops 24159191040 | bytes 20000000 | tf_op jit(solution)/shard_map/pallas_call | solution.py:686
  479.1 7.7 %shard_map.233.refs_5_.refs_6_ = f32[3072,768]{1,0:T(8,128)} custom-call(s32[1]{0:T(128)} %bitcast.23.refs_0_, bf16[1536,768]{1,0:T(8,128)(2,1)} %pad_maximum_fusion.refs_1_, bf16[1536,768]{1,0:T(8,128)(2,1)} %collective-permute-done.31.refs_2_, bf16[2,192,1536]{2,1,0:T(8,128)(2,1)} %bitcast.80), custom_call_target="tpu_custom_call" | custom-call | flops 5898240 | bytes 20000000 | tf_op jit(solution)/shard_map/pallas_call | solution.py:670
  496.4 9.6 %collective-permute-done.29 = bf16[2,96,1664]{2,1,0:T(8,128)(2,1)S(1)} collective-permute-done((bf16[2,96,1664]{2,1,0:T(8,128)(2,1)S(1)}, bf16[2,96,1664]{2,1,0:T(8,128)(2,1)S(1)}, u32[]{:S(2)}, u32[]{:S(2)}) %collective-permute-start.29) | collective-permute-done | bytes 639008 | tf_op jit(solution)/shard_map/ppermute | solution.py:715
  533.2 7.4 %collective-permute-done.36 = bf16[24,3200]{1,0:T(8,128)(2,1)S(1)} collective-permute-done((bf16[24,3200]{1,0:T(8,128)(2,1)S(1)}, bf16[24,3200]{1,0:T(8,128)(2,1)S(1)}, u32[]{:S(2)}, u32[]{:S(2)}) %collective-permute-start.36) | collective-permute-done | bytes 153632 | tf_op jit(solution)/shard_map/ppermute | solution.py:715
  541.0 6.5 %collective-permute-done.38 = bf16[48,3200]{1,0:T(8,128)(2,1)S(1)} collective-permute-done((bf16[48,3200]{1,0:T(8,128)(2,1)S(1)}, bf16[48,3200]{1,0:T(8,128)(2,1)S(1)}, u32[]{:S(2)}, u32[]{:S(2)}) %collective-permute-start.38) | collective-permute-done | bytes 307232 | tf_op jit(solution)/shard_map/ppermute | solution.py:715
  553.8 7.4 %shard_map.236 = f32[768,3072]{1,0:T(8,128)} custom-call(s32[1]{0:T(128)} %bitcast.23.refs_0_, bf16[384,3072]{1,0:T(8,128)(2,1)} %copy-done.6, bf16[384,3072]{1,0:T(8,128)(2,1)} %copy-done.20, bf16[512,768]{1,0:T(8,128)(2,1)} %shard_map.235.refs_3_), custom_call_target="tpu_custom_call" | custom-call | flops 5898240 | bytes 20000000 | tf_op jit(solution)/shard_map/pallas_call | solution.py:670
  (288 shorter events, 207.0 us)
Async XLA Ops:
  7.2 49.9 %all-gather.2.cloned.1.call-start = ((), (), s32[]{:S(2)}) async-start(), calls=%async_computation.10 | async-start | bytes 5898240 | tf_op jit(solution)/shard_map/all_gather | solution.py:812
  49.7 40.3 %collective-permute-start.1 = (bf16[256,768]{1,0:T(8,128)(2,1)}, bf16[256,768]{1,0:T(8,128)(2,1)}, u32[]{:S(2)}, u32[]{:S(2)}) collective-permute-start(bf16[256,768]{1,0:T(8,128)(2,1)} %get-tuple-element.235), channel_id=1, source_target_pairs={{0,4},{1,5},{2,6},{3,7},{4,0},{5,1},{6,2},{7,3},{8,12},{9,13},{10,... | collective-permute-start | bytes 1179656 | tf_op jit(solution)/shard_map/ppermute | solution.py:715
  76.3 44.5 %collective-permute-start.4 = (bf16[512,768]{1,0:T(8,128)(2,1)}, bf16[512,768]{1,0:T(8,128)(2,1)}, u32[]{:S(2)}, u32[]{:S(2)}) collective-permute-start(bf16[512,768]{1,0:T(8,128)(2,1)} %get-tuple-element.96), channel_id=1, source_target_pairs={{0,4},{1,5},{2,6},{3,7},{4,0},{5,1},{6,2},{7,3},{8,12},{9,13},{10,... | collective-permute-start | bytes 2359304 | tf_op jit(solution)/shard_map/ppermute | solution.py:715
  86.2 41.7 %all-to-all-start.1 = ((bf16[4,192,768]{2,1,0:T(8,128)(2,1)}), bf16[4,192,768]{2,1,0:T(8,128)(2,1)S(1)}, u32[]{:S(2)}, u32[]{:S(2)}) async-start(bf16[4,192,768]{2,1,0:T(8,128)(2,1)} %get-tuple-element.98.refs_7_), calls=%async_computation.1 | async-start | bytes 2359296 | tf_op jit(solution)/shard_map/all_to_all | solution.py:786
  120.7 79.0 %collective-permute-start.5 = (bf16[512,768]{1,0:T(8,128)(2,1)}, bf16[512,768]{1,0:T(8,128)(2,1)}, u32[]{:S(2)}, u32[]{:S(2)}) collective-permute-start(bf16[512,768]{1,0:T(8,128)(2,1)} %slice_bitcast_fusion.2), channel_id=1, source_target_pairs={{0,4},{1,5},{2,6},{3,7},{4,0},{5,1},{6,2},{7,3},{8,12},{9,13},{10,... | collective-permute-start | bytes 2359304 | tf_op jit(solution)/shard_map/ppermute | solution.py:715
  120.7 79.0 %collective-permute-start.6 = (bf16[512,768]{1,0:T(8,128)(2,1)}, bf16[512,768]{1,0:T(8,128)(2,1)}, u32[]{:S(2)}, u32[]{:S(2)}) collective-permute-start(bf16[512,768]{1,0:T(8,128)(2,1)} %get-tuple-element.105), channel_id=1, source_target_pairs={{0,4},{1,5},{2,6},{3,7},{4,0},{5,1},{6,2},{7,3},{8,12},{9,13},{10,... | collective-permute-start | bytes 2359304 | tf_op jit(solution)/shard_map/ppermute | solution.py:715
  168.6 46.9 %all-to-all-start.3 = ((bf16[4,384,768]{2,1,0:T(8,128)(2,1)}), bf16[4,384,768]{2,1,0:T(8,128)(2,1)S(1)}, u32[]{:S(2)}, u32[]{:S(2)}) async-start(bf16[4,384,768]{2,1,0:T(8,128)(2,1)} %shard_map.218.refs_8_), calls=%async_computation.3 | async-start | bytes 4718592 | tf_op jit(solution)/shard_map/all_to_all | solution.py:786
  248.6 41.9 %collective-permute-start.7 = (bf16[192,768]{1,0:T(8,128)(2,1)}, bf16[192,768]{1,0:T(8,128)(2,1)S(1)}, u32[]{:S(2)}, u32[]{:S(2)}) collective-permute-start(bf16[192,768]{1,0:T(8,128)(2,1)} %get-tuple-element.107), channel_id=1, source_target_pairs={{0,4},{1,5},{2,6},{3,7},{4,0},{5,1},{6,2},{7,3},{8,12},{9,13},{10,... | collective-permute-start | bytes 884744 | tf_op jit(solution)/shard_map/ppermute | solution.py:715
  249.7 54.8 %collective-permute-start.8 = (bf16[192,768]{1,0:T(8,128)(2,1)}, bf16[192,768]{1,0:T(8,128)(2,1)S(1)}, u32[]{:S(2)}, u32[]{:S(2)}) collective-permute-start(bf16[192,768]{1,0:T(8,128)(2,1)} %get-tuple-element.108), channel_id=1, source_target_pairs={{0,5},{1,4},{2,7},{3,6},{4,1},{5,0},{6,3},{7,2},{8,13},{9,12},{10,... | collective-permute-start | bytes 884744 | tf_op jit(solution)/shard_map/ppermute | solution.py:715
  253.0 66.7 %collective-permute-start.9 = (bf16[192,768]{1,0:T(8,128)(2,1)}, bf16[192,768]{1,0:T(8,128)(2,1)S(1)}, u32[]{:S(2)}, u32[]{:S(2)}) collective-permute-start(bf16[192,768]{1,0:T(8,128)(2,1)} %get-tuple-element.109), channel_id=1, source_target_pairs={{0,6},{1,7},{2,4},{3,5},{4,2},{5,3},{6,0},{7,1},{8,14},{9,15},{10,... | collective-permute-start | bytes 884744 | tf_op jit(solution)/shard_map/ppermute | solution.py:715
  255.3 78.0 %collective-permute-start.10 = (bf16[192,768]{1,0:T(8,128)(2,1)}, bf16[192,768]{1,0:T(8,128)(2,1)}, u32[]{:S(2)}, u32[]{:S(2)}) collective-permute-start(bf16[192,768]{1,0:T(8,128)(2,1)} %get-tuple-element.110), channel_id=1, source_target_pairs={{0,7},{1,6},{2,5},{3,4},{4,3},{5,2},{6,1},{7,0},{8,15},{9,14},{10,... | collective-permute-start | bytes 884744 | tf_op jit(solution)/shard_map/ppermute | solution.py:715
  256.3 42.1 %all-to-all-start.5 = ((bf16[4,192,768]{2,1,0:T(8,128)(2,1)}), bf16[4,192,768]{2,1,0:T(8,128)(2,1)S(1)}, u32[]{:S(2)}, u32[]{:S(2)}) async-start(bf16[4,192,768]{2,1,0:T(8,128)(2,1)} %get-tuple-element.112), calls=%async_computation.5 | async-start | bytes 2359296 | tf_op jit(solution)/shard_map/all_to_all | solution.py:786
  287.1 65.0 %collective-permute-start.13 = (bf16[192,768]{1,0:T(8,128)(2,1)}, bf16[192,768]{1,0:T(8,128)(2,1)}, u32[]{:S(2)}, u32[]{:S(2)}) collective-permute-start(bf16[192,768]{1,0:T(8,128)(2,1)} %get-tuple-element.130), channel_id=1, source_target_pairs={{0,4},{1,5},{2,6},{3,7},{4,0},{5,1},{6,2},{7,3},{8,12},{9,13},{10,... | collective-permute-start | bytes 884744 | tf_op jit(solution)/shard_map/ppermute | solution.py:715
  290.6 81.1 %collective-permute-start.15 = (bf16[192,768]{1,0:T(8,128)(2,1)}, bf16[192,768]{1,0:T(8,128)(2,1)}, u32[]{:S(2)}, u32[]{:S(2)}) collective-permute-start(bf16[192,768]{1,0:T(8,128)(2,1)} %get-tuple-element.131), channel_id=1, source_target_pairs={{0,5},{1,4},{2,7},{3,6},{4,1},{5,0},{6,3},{7,2},{8,13},{9,12},{10,... | collective-permute-start | bytes 884744 | tf_op jit(solution)/shard_map/ppermute | solution.py:715
  299.5 74.1 %all-to-all-start.8 = ((bf16[4,384,768]{2,1,0:T(8,128)(2,1)}), bf16[4,384,768]{2,1,0:T(8,128)(2,1)}, u32[]{:S(2)}, u32[]{:S(2)}) async-start(bf16[4,384,768]{2,1,0:T(8,128)(2,1)} %get-tuple-element.143), calls=%async_computation.8 | async-start | bytes 4718592 | tf_op jit(solution)/shard_map/all_to_all | solution.py:786
  304.5 118.2 %collective-permute-start.16 = (bf16[192,768]{1,0:T(8,128)(2,1)}, bf16[192,768]{1,0:T(8,128)(2,1)}, u32[]{:S(2)}, u32[]{:S(2)}) collective-permute-start(bf16[192,768]{1,0:T(8,128)(2,1)} %get-tuple-element.133), channel_id=1, source_target_pairs={{0,6},{1,7},{2,4},{3,5},{4,2},{5,3},{6,0},{7,1},{8,14},{9,15},{10,... | collective-permute-start | bytes 884744 | tf_op jit(solution)/shard_map/ppermute | solution.py:715
  333.3 89.5 %collective-permute-start.17 = (bf16[192,768]{1,0:T(8,128)(2,1)}, bf16[192,768]{1,0:T(8,128)(2,1)}, u32[]{:S(2)}, u32[]{:S(2)}) collective-permute-start(bf16[192,768]{1,0:T(8,128)(2,1)} %get-tuple-element.134), channel_id=1, source_target_pairs={{0,7},{1,6},{2,5},{3,4},{4,3},{5,2},{6,1},{7,0},{8,15},{9,14},{10,... | collective-permute-start | bytes 884744 | tf_op jit(solution)/shard_map/ppermute | solution.py:715
  373.6 43.7 %all-to-all-start.7 = ((bf16[4,192,768]{2,1,0:T(8,128)(2,1)}), bf16[4,192,768]{2,1,0:T(8,128)(2,1)S(1)}, u32[]{:S(2)}, u32[]{:S(2)}) async-start(bf16[4,192,768]{2,1,0:T(8,128)(2,1)} %get-tuple-element.136), calls=%async_computation.7 | async-start | bytes 2359296 | tf_op jit(solution)/shard_map/all_to_all | solution.py:786
  410.2 42.9 %collective-permute-start.21 = (bf16[96,3072]{1,0:T(8,128)(2,1)}, bf16[96,3072]{1,0:T(8,128)(2,1)}, u32[]{:S(2)}, u32[]{:S(2)}) collective-permute-start(bf16[96,3072]{1,0:T(8,128)(2,1)} %get-tuple-element.226), channel_id=1, source_target_pairs={{0,16},{8,24},{16,0},{24,8},{1,17},{9,25},{17,1},{25,9},{2,18},{10... | collective-permute-start | bytes 1769480 | tf_op jit(solution)/shard_map/ppermute | solution.py:715
  411.6 43.6 %collective-permute-start.22 = (bf16[96,3072]{1,0:T(8,128)(2,1)}, bf16[96,3072]{1,0:T(8,128)(2,1)}, u32[]{:S(2)}, u32[]{:S(2)}) collective-permute-start(bf16[96,3072]{1,0:T(8,128)(2,1)} %get-tuple-element.225), channel_id=1, source_target_pairs={{0,16},{8,24},{16,0},{24,8},{1,17},{9,25},{17,1},{25,9},{2,18},{10... | collective-permute-start | bytes 1769480 | tf_op jit(solution)/shard_map/ppermute | solution.py:715
  412.2 43.8 %collective-permute-start.23 = (bf16[96,3072]{1,0:T(8,128)(2,1)}, bf16[96,3072]{1,0:T(8,128)(2,1)}, u32[]{:S(2)}, u32[]{:S(2)}) collective-permute-start(bf16[96,3072]{1,0:T(8,128)(2,1)} %get-tuple-element.224), channel_id=1, source_target_pairs={{0,16},{8,24},{16,0},{24,8},{1,17},{9,25},{17,1},{25,9},{2,18},{10... | collective-permute-start | bytes 1769480 | tf_op jit(solution)/shard_map/ppermute | solution.py:715
  422.7 56.4 %collective-permute-start.31 = (bf16[1536,768]{1,0:T(8,128)(2,1)}, bf16[1536,768]{1,0:T(8,128)(2,1)}, u32[]{:S(2)}, u32[]{:S(2)}) collective-permute-start(bf16[1536,768]{1,0:T(8,128)(2,1)} %pad_maximum_fusion.refs_1_), channel_id=1, source_target_pairs={{0,8},{8,0},{16,24},{24,16},{1,9},{9,1},{17,25},{25,17},{2,10},{10... | collective-permute-start | bytes 7077896 | tf_op jit(solution)/shard_map/ppermute | solution.py:715
  453.1 61.4 %collective-permute-start.32 = (bf16[256,768]{1,0:T(8,128)(2,1)S(1)}, bf16[256,768]{1,0:T(8,128)(2,1)}, u32[]{:S(2)}, u32[]{:S(2)}) collective-permute-start(bf16[256,768]{1,0:T(8,128)(2,1)S(1)} %copy-done.30), channel_id=1, source_target_pairs={{0,4},{1,5},{2,6},{3,7},{4,0},{5,1},{6,2},{7,3},{8,12},{9,13},{10,... | collective-permute-start | bytes 1179656 | tf_op jit(solution)/shard_map/ppermute | solution.py:715
  455.3 59.2 %collective-permute-start.33 = (bf16[512,768]{1,0:T(8,128)(2,1)}, bf16[512,768]{1,0:T(8,128)(2,1)}, u32[]{:S(2)}, u32[]{:S(2)}) collective-permute-start(bf16[512,768]{1,0:T(8,128)(2,1)} %get-tuple-element.163), channel_id=1, source_target_pairs={{0,4},{1,5},{2,6},{3,7},{4,0},{5,1},{6,2},{7,3},{8,12},{9,13},{10,... | collective-permute-start | bytes 2359304 | tf_op jit(solution)/shard_map/ppermute | solution.py:715
  (77 other events, 943.7 us)
Sparse Core Ops, SparseCore 0:
  10.2 42.2 all-gather.1

commit v5 on v4

--- a/solution.py
+++ b/solution.py
@@ -407,9 +407,13 @@
     out_ref[...] = jnp.where(own, mine_ref[...], other_ref[...]).astype(F32)
 
 
-def dense_grad_kernel(n0, n1, g0, g1, m0, m1, b0, b1, small, left_ref, right_ref):
+def left_grad_kernel(n0, n1, g0, g1, left_ref):
+    columns = left_ref.shape[1]
+    left_ref[...] = (dot_tn(n0[...], g0[:, :columns]) + dot_tn(n1[...], g1[:, :columns])).astype(BF16)
+
+
+def right_grad_kernel(n0, n1, g0, g1, m0, m1, b0, b1, small, right_ref):
     width = n0.shape[1]
-    left_ref[...] = (dot_tn(n0[...], g0[:, : 2 * width]) + dot_tn(n1[...], g1[:, : 2 * width])).astype(BF16)
     right_ref[:, :width] = (dot_tn(n0[...], g0[:, 2 * width :]) + dot_tn(n1[...], g1[:, 2 * width :])).astype(BF16)
     right_ref[:, width : 2 * width] = (dot_tn(m0[...], b0[...]) + dot_tn(m1[...], b1[...])).astype(BF16)
     right_ref[:, 2 * width :] = small[...]
@@ -681,15 +685,19 @@
 
 def dense_grad(*arrays, after):
     small = arrays[-1]
-    width = arrays[0].shape[1]
-    length = arrays[0].shape[0]
-    return pl.pallas_call(
-        later(dense_grad_kernel, len(arrays), len(after)),
-        in_specs=[VECTOR] * len(arrays) + [ANYWHERE] * len(after),
-        out_shape=(shaped((width, 2 * width), BF16), shaped((width, 2 * width + small.shape[1]), BF16)),
-        compiler_params=params(),
-        cost_estimate=cost(4 * length * width * 4 * width, 20e6),
-    )(*arrays, *after)
+    length, width = arrays[0].shape
+
+    def call(kernel, inputs, columns, ties):
+        return pl.pallas_call(
+            later(kernel, len(inputs), len(ties)),
+            in_specs=[VECTOR] * len(inputs) + [ANYWHERE] * len(ties),
+            out_shape=shaped((width, columns), BF16),
+            compiler_params=params(),
+            cost_estimate=cost(4 * length * width * columns, 10e6),
+        )(*inputs, *ties)
+
+    left = call(left_grad_kernel, arrays[:4], 2 * width, after)
+    return left, call(right_grad_kernel, arrays, 2 * width + small.shape[1], [left])
 
 
 def combine(out_rows, part, far, mine, col, hidden, after):

time: 583 us -> 589 us (1.010)
    pallas_call x1 -> x2, Pallas kernels: 10.3 us -> 14.8 us  [call(): pl.pallas_call(later(kernel, len(inputs), len(ties)), in_specs=[VECTOR] *...]
where the time goes in v5:
time: 589 us; the launch traced here: 579 us
  Pallas kernels  312 us (53%)
  starting transfers between devices  97.9 us (17%)
  waiting for transfers between devices  89.5 us (15%)
  local copies, waits for them, and re-layouts  32.6 us (6%)
  other arithmetic  29.9 us (5%)
  between operations  15.3 us (3%)
    pallas_call x4, Pallas kernels, expert(): pl.pallas_call(later(functools.partial(expert_kernel, kind, near, alias,...  106 us
    ppermute x41, starting transfers between devices, swap(): return lax.ppermute(value, axis, [(i, i ^ bit) for i in range(size)])  52.9 us
    pallas_call x2, Pallas kernels, backward(): pl.pallas_call(later(functools.partial(backward_kernel, near, part), near...  52.7 us
    ppermute x41, waiting for transfers between devices, swap(): return lax.ppermute(value, axis, [(i, i ^ bit) for i in range(size)])  52.5 us
    pallas_call x2, Pallas kernels, forward(): pl.pallas_call(later(functools.partial(forward_kernel, m), 7, len(after))...  38.2 us
    all_to_all x9, starting transfers between devices, around(): lax.all_to_all(blocks, 'expert', split_axis=0, concat_axis=0, axis_index_...  38.2 us
    all_to_all x9, waiting for transfers between devices, around(): lax.all_to_all(blocks, 'expert', split_axis=0, concat_axis=0, axis_index_...  36.9 us
    pallas_call x2, Pallas kernels, first_grad(): pl.pallas_call(later(functools.partial(expert_grad_kernel, len(ups), Fals...  25.9 us
  transfers between devices with their start and end apart: 52, of which 15 were waited for; matrix products, arithmetic and copies ran while one was open for 8% of the time, Pallas kernels for 54%

profile of v5, /device:TPU:0, one launch (start us, length us, event | category | flops | bytes accessed | tf_op | source)
XLA Modules:
  0.0 579.3 jit_solution(9575948717006244876)
XLA Ops:
  11.2 6.8 %all-to-all-start = ((s32[8,2,2,512]{3,2,1,0:T(2,128)}), s32[8,2,2,512]{3,2,1,0:T(2,128)S(1)}, u32[]{:S(2)}, u32[]{:S(2)}) async-start(s32[8,2,2,512]{3,2,1,0:T(2,128)} %broadcast_in_dim.21), calls=%async_computation | async-start | bytes 131072 | tf_op jit(solution)/shard_map/all_to_all | solution.py:805
  57.1 19.1 %shard_map.215 = (bf16[512,2304]{1,0:T(8,128)(2,1)}, bf16[512,768]{1,0:T(8,128)(2,1)}, f32[512,128]{1,0:T(8,128)}, f32[512,768]{1,0:T(8,128)}, bf16[512,768]{1,0:T(8,128)(2,1)}, /*index=5*/bf16[4,192,768]{2,1,0:T(8,128)(2,1)}) custom-call(bf16[2,512,768]{2,1,0:T(8,128)(2,1)} %refs_16_.3, f32[2,768]{1,0:T(2,128)} %convert_bitcast_fusion.gains_ref.refs_1_.refs_9_, ...), custom_call_target="tpu_custom_call" | custom-call | flops 20132659200 | bytes 24000000 | tf_op jit(solution)/shard_map/pallas_call | solution.py:499
  77.7 8.5 %all-to-all-done.2.refs_1_ = bf16[4,384,768]{2,1,0:T(8,128)(2,1)S(1)} async-done(((bf16[4,384,768]{2,1,0:T(8,128)(2,1)}), bf16[4,384,768]{2,1,0:T(8,128)(2,1)S(1)}, u32[]{:S(2)}, u32[]{:S(2)}) %all-to-all-start.2) | async-done | bytes 2359328 | tf_op jit(solution)/shard_map/all_to_all | solution.py:794
  90.0 19.1 %shard_map.217 = (bf16[512,2304]{1,0:T(8,128)(2,1)}, bf16[512,768]{1,0:T(8,128)(2,1)}, f32[512,128]{1,0:T(8,128)}, f32[512,768]{1,0:T(8,128)}, bf16[512,768]{1,0:T(8,128)(2,1)}, /*index=5*/bf16[4,192,768]{2,1,0:T(8,128)(2,1)}) custom-call(bf16[2,512,768]{2,1,0:T(8,128)(2,1)} %refs_16_.3, f32[2,768]{1,0:T(2,128)} %convert_bitcast_fusion.gains_ref.refs_1_.refs_9_, ...), custom_call_target="tpu_custom_call" | custom-call | flops 20132659200 | bytes 24000000 | tf_op jit(solution)/shard_map/pallas_call | solution.py:499
  109.1 11.6 %collective-permute-done.4.refs_4_ = bf16[512,768]{1,0:T(8,128)(2,1)} collective-permute-done((bf16[512,768]{1,0:T(8,128)(2,1)}, bf16[512,768]{1,0:T(8,128)(2,1)}, u32[]{:S(2)}, u32[]{:S(2)}) %collective-permute-start.4) | collective-permute-done | bytes 786464 | tf_op jit(solution)/shard_map/ppermute | solution.py:723
  131.9 26.0 %shard_map.220 = (bf16[4,192,768]{2,1,0:T(8,128)(2,1)}, bf16[4,384,768]{2,1,0:T(8,128)(2,1)}, bf16[768,3072]{1,0:T(8,128)(2,1)}, bf16[768,3072]{1,0:T(8,128)(2,1...) custom-call(bf16[4,192,768]{2,1,0:T(8,128)(2,1)} %copy-done.22, bf16[4,384,768]{2,1,0:T(8,128)(2,1)} %copy-done.19, ...), custom_call_target="tpu_custom_call" | custom-call | flops 72477573120 | bytes 30000000 | tf_op jit(solution)/shard_map/pallas_call | solution.py:584
  157.9 9.6 %all-to-all-done.4.refs_0_.refs_2_ = bf16[4,192,768]{2,1,0:T(8,128)(2,1)S(1)} async-done(((bf16[4,192,768]{2,1,0:T(8,128)(2,1)}), bf16[4,192,768]{2,1,0:T(8,128)(2,1)S(1)}, u32[]{:S(2)}, u32[]{:S(2)}) %all-to-all-start.4) | async-done | bytes 1179680 | tf_op jit(solution)/shard_map/all_to_all | solution.py:794
  173.6 26.0 %shard_map.221 = (bf16[4,192,768]{2,1,0:T(8,128)(2,1)}, bf16[4,384,768]{2,1,0:T(8,128)(2,1)}, bf16[768,3072]{1,0:T(8,128)(2,1)}, bf16[768,3072]{1,0:T(8,128)(2,1...) custom-call(bf16[4,192,768]{2,1,0:T(8,128)(2,1)} %copy-done.23, ...), custom_call_target="tpu_custom_call", output_to_operand_aliasing={{1}: (8, {})} | custom-call | flops 72477573120 | bytes 30000000 | tf_op jit(solution)/shard_map/pallas_call | solution.py:584
  203.8 11.7 %all-to-all-done.3.refs_0_.refs_1_.refs_3_ = bf16[4,384,768]{2,1,0:T(8,128)(2,1)S(1)} async-done(((bf16[4,384,768]{2,1,0:T(8,128)(2,1)}), bf16[4,384,768]{2,1,0:T(8,128)(2,1)S(1)}, u32[]{:S(2)}, u32[]{:S(2)}) %all-to-all-start.3) | async-done | bytes 2359328 | tf_op jit(solution)/shard_map/all_to_all | solution.py:794
  221.7 26.9 %shard_map.223 = (bf16[192,768]{1,0:T(8,128)(2,1)}, bf16[192,768]{1,0:T(8,128)(2,1)}, bf16[192,768]{1,0:T(8,128)(2,1)}, bf16[192,768]{1,0:T(8,128)(2,1)}, bf16[4...) custom-call(bf16[4,384,768]{2,1,0:T(8,128)(2,1)} %copy-done.18, ...), custom_call_target="tpu_custom_call" | custom-call | flops 72477573120 | bytes 30000000 | tf_op jit(solution)/shard_map/pallas_call | solution.py:584
  260.1 26.9 %shard_map.224 = (bf16[192,768]{1,0:T(8,128)(2,1)}, bf16[192,768]{1,0:T(8,128)(2,1)}, bf16[192,768]{1,0:T(8,128)(2,1)}, bf16[192,768]{1,0:T(8,128)(2,1)}, bf16[4...) custom-call(bf16[4,384,768]{2,1,0:T(8,128)(2,1)} %all-to-all-done.6., ...), custom_call_target="tpu_custom_call", output_to_operand_aliasing={{4}: (8, {})} | custom-call | flops 72477573120 | bytes 30000000 | tf_op jit(solution)/shard_map/pallas_call | solution.py:584
  307.1 12.6 %shard_map.225.refs_9_ = bf16[1536,768]{1,0:T(8,128)(2,1)} custom-call(s32[1]{0:T(128)S(6)} %sub.3.refs_0_, bf16[768,3072]{1,0:T(8,128)(2,1)} %get-tuple-element.120.refs_1_, bf16[768,3072]{1,0:T(8,128)(2,1)} %get-tuple-element.121.refs_2_, bf16[768,3072]{1,0:T(8,128)(2,1)} %get-tuple-element.122.refs_3_, bf16[768,3072]{1,0:T(8,128)(2,1)} %get-tuple-element.123.refs_4_, ...), custom_call_target="tpu_custom_call" | custom-call | flops 36238786560 | bytes 15000000 | tf_op jit(solution)/shard_map/pallas_call | solution.py:632
  320.4 12.8 %shard_map.226.refs_10_ = bf16[384,3072]{1,0:T(8,128)(2,1)} custom-call(s32[1]{0:T(128)S(6)} %sub.3.refs_0_, bf16[4,192,768]{2,1,0:T(8,128)(2,1)} %copy-done.22, bf16[4,192,768]{2,1,0:T(8,128)(2,1)} %copy-done.23, bf16[4,384,768]{2,1,0:T(8,128)(2,1)} %copy-done.18, bf16[4,384,768]{2,1,0:T(8,128)(2,1)} %all-to-all-done.6.refs_0_.refs_1_.refs_4_, ...), custom_call_target="tpu_custom_call" | custom-call | flops 36238786560 | bytes 25000000 | tf_op jit(solution)/shard_map/pallas_call | solution.py:657
  336.0 13.0 %shard_map.227.refs_10_ = bf16[1536,768]{1,0:T(8,128)(2,1)} custom-call(s32[1]{0:T(128)} %bitcast.23.refs_0_, bf16[768,3072]{1,0:T(8,128)(2,1)} %get-tuple-element.120.refs_1_, bf16[768,3072]{1,0:T(8,128)(2,1)} %get-tuple-element.121.refs_2_, bf16[768,3072]{1,0:T(8,128)(2,1)} %get-tuple-element.122.refs_3_, bf16[768,3072]{1,0:T(8,128)(2,1)} %get-tuple-element.123.refs_4_, ...), custom_call_target="tpu_custom_call" | custom-call | flops 36238786560 | bytes 15000000 | tf_op jit(solution)/shard_map/pallas_call | solution.py:632
  354.8 13.1 %shard_map.228.refs_17_ = bf16[384,3072]{1,0:T(8,128)(2,1)} custom-call(s32[1]{0:T(128)} %bitcast.23.refs_0_, bf16[4,192,768]{2,1,0:T(8,128)(2,1)} %copy-done.22, bf16[4,192,768]{2,1,0:T(8,128)(2,1)} %copy-done.23, bf16[4,384,768]{2,1,0:T(8,128)(2,1)} %copy-done.18, bf16[4,384,768]{2,1,0:T(8,128)(2,1)} %all-to-all-done.6.refs_0_.refs_1_.refs_4_, ...), custom_call_target="tpu_custom_call" | custom-call | flops 36238786560 | bytes 25000000 | tf_op jit(solution)/shard_map/pallas_call | solution.py:657
  377.2 26.3 %shard_map.229 = (bf16[512,768]{1,0:T(8,128)(2,1)}, bf16[512,768]{1,0:T(8,128)(2,1)}, bf16[512,2304]{1,0:T(8,128)(2,1)}, bf16[512,768]{1,0:T(8,128)(2,1)}, f32[2,768]{1,0:T(2,128)}, /*index=5*/f32[12,1024]{1,0:T(8,128)}) custom-call(bf16[192,768]{1,0:T(8,128)(2,1)} %copy-done.44, bf16[192,768]{1,0:T(8,128)(2,1)} %copy-done.45, bf16[192,768]{1,0:T(8,128)(2,1)} %copy-done.46, ...), custom_call_target="tpu_custom_call" | custom-call | flops 38252052480 | bytes 30000000 | tf_op jit(solution)/shard_map/pallas_call | solution.py:528
  423.4 26.4 %shard_map.231 = (bf16[512,768]{1,0:T(8,128)(2,1)}, bf16[512,768]{1,0:T(8,128)(2,1)}, bf16[512,2304]{1,0:T(8,128)(2,1)}, bf16[512,768]{1,0:T(8,128)(2,1)}, f32[2,768]{1,0:T(2,128)}, /*index=5*/f32[12,1024]{1,0:T(8,128)}) custom-call(bf16[192,768]{1,0:T(8,128)(2,1)} %collective-permute-done.13.refs_11_.refs_0_, ...), custom_call_target="tpu_custom_call" | custom-call | flops 38252052480 | bytes 30000000 | tf_op jit(solution)/shard_map/pallas_call | solution.py:528
  458.6 7.0 %shard_map.232.refs_9_ = bf16[768,1536]{1,0:T(8,128)(2,1)} custom-call(bf16[512,768]{1,0:T(8,128)(2,1)} %get-tuple-element.130.refs_0_, bf16[512,768]{1,0:T(8,128)(2,1)} %get-tuple-element.144.refs_1_, bf16[512,2304]{1,0:T(8,128)(2,1)} %get-tuple-element.145.refs_2_, bf16[512,2304]{1,0:T(8,128)(2,1)} %get-tuple-element.146.refs_3_, ...), custom_call_target="tpu_custom_call" | custom-call | flops 12079595520 | bytes 10000000 | tf_op jit(solution)/shard_map/pallas_call | solution.py:691
  467.4 7.8 %shard_map.233 = bf16[768,1664]{1,0:T(8,128)(2,1)} custom-call(bf16[512,768]{1,0:T(8,128)(2,1)} %get-tuple-element.130.refs_0_, bf16[512,768]{1,0:T(8,128)(2,1)} %get-tuple-element.144.refs_1_, bf16[512,2304]{1,0:T(8,128)(2,1)} %get-tuple-element.145.refs_2_, bf16[512,2304]{1,0:T(8,128)(2,1)} %get-tuple-element.146.refs_3_, ...), custom_call_target="tpu_custom_call" | custom-call | flops 13086228480 | bytes 10000000 | tf_op jit(solution)/shard_map/pallas_call | solution.py:691
  484.5 7.8 %shard_map.234.refs_5_.refs_6_ = f32[3072,768]{1,0:T(8,128)} custom-call(s32[1]{0:T(128)} %bitcast.23.refs_0_, bf16[1536,768]{1,0:T(8,128)(2,1)} %pad_maximum_fusion.refs_1_, bf16[1536,768]{1,0:T(8,128)(2,1)} %collective-permute-done.31.refs_2_, bf16[2,192,1536]{2,1,0:T(8,128)(2,1)} %bitcast.80), custom_call_target="tpu_custom_call" | custom-call | flops 5898240 | bytes 20000000 | tf_op jit(solution)/shard_map/pallas_call | solution.py:674
  501.8 9.8 %collective-permute-done.29 = bf16[2,96,1664]{2,1,0:T(8,128)(2,1)S(1)} collective-permute-done((bf16[2,96,1664]{2,1,0:T(8,128)(2,1)S(1)}, bf16[2,96,1664]{2,1,0:T(8,128)(2,1)S(1)}, u32[]{:S(2)}, u32[]{:S(2)}) %collective-permute-start.29) | collective-permute-done | bytes 639008 | tf_op jit(solution)/shard_map/ppermute | solution.py:723
  538.6 7.4 %collective-permute-done.36 = bf16[24,3200]{1,0:T(8,128)(2,1)S(1)} collective-permute-done((bf16[24,3200]{1,0:T(8,128)(2,1)S(1)}, bf16[24,3200]{1,0:T(8,128)(2,1)S(1)}, u32[]{:S(2)}, u32[]{:S(2)}) %collective-permute-start.36) | collective-permute-done | bytes 153632 | tf_op jit(solution)/shard_map/ppermute | solution.py:723
  546.2 6.8 %collective-permute-done.38 = bf16[48,3200]{1,0:T(8,128)(2,1)S(1)} collective-permute-done((bf16[48,3200]{1,0:T(8,128)(2,1)S(1)}, bf16[48,3200]{1,0:T(8,128)(2,1)S(1)}, u32[]{:S(2)}, u32[]{:S(2)}) %collective-permute-start.38) | collective-permute-done | bytes 307232 | tf_op jit(solution)/shard_map/ppermute | solution.py:723
  559.7 7.4 %shard_map.237 = f32[768,3072]{1,0:T(8,128)} custom-call(s32[1]{0:T(128)} %bitcast.23.refs_0_, bf16[384,3072]{1,0:T(8,128)(2,1)} %copy-done.6, bf16[384,3072]{1,0:T(8,128)(2,1)} %copy-done.20, bf16[512,768]{1,0:T(8,128)(2,1)} %shard_map.236.refs_3_), custom_call_target="tpu_custom_call" | custom-call | flops 5898240 | bytes 20000000 | tf_op jit(solution)/shard_map/pallas_call | solution.py:674
  (289 shorter events, 213.4 us)
Async XLA Ops:
  7.2 49.9 %all-gather.2.cloned.1.call-start = ((), (), s32[]{:S(2)}) async-start(), calls=%async_computation.10 | async-start | bytes 5898240 | tf_op jit(solution)/shard_map/all_gather | solution.py:820
  49.7 40.3 %collective-permute-start.1 = (bf16[256,768]{1,0:T(8,128)(2,1)}, bf16[256,768]{1,0:T(8,128)(2,1)}, u32[]{:S(2)}, u32[]{:S(2)}) collective-permute-start(bf16[256,768]{1,0:T(8,128)(2,1)} %get-tuple-element.231), channel_id=1, source_target_pairs={{0,4},{1,5},{2,6},{3,7},{4,0},{5,1},{6,2},{7,3},{8,12},{9,13},{10,... | collective-permute-start | bytes 1179656 | tf_op jit(solution)/shard_map/ppermute | solution.py:723
  76.2 44.5 %collective-permute-start.4 = (bf16[512,768]{1,0:T(8,128)(2,1)}, bf16[512,768]{1,0:T(8,128)(2,1)}, u32[]{:S(2)}, u32[]{:S(2)}) collective-permute-start(bf16[512,768]{1,0:T(8,128)(2,1)} %get-tuple-element.94), channel_id=1, source_target_pairs={{0,4},{1,5},{2,6},{3,7},{4,0},{5,1},{6,2},{7,3},{8,12},{9,13},{10,... | collective-permute-start | bytes 2359304 | tf_op jit(solution)/shard_map/ppermute | solution.py:723
  86.2 41.6 %all-to-all-start.1 = ((bf16[4,192,768]{2,1,0:T(8,128)(2,1)}), bf16[4,192,768]{2,1,0:T(8,128)(2,1)S(1)}, u32[]{:S(2)}, u32[]{:S(2)}) async-start(bf16[4,192,768]{2,1,0:T(8,128)(2,1)} %get-tuple-element.96.refs_7_), calls=%async_computation.1 | async-start | bytes 2359296 | tf_op jit(solution)/shard_map/all_to_all | solution.py:794
  120.7 78.9 %collective-permute-start.5 = (bf16[512,768]{1,0:T(8,128)(2,1)}, bf16[512,768]{1,0:T(8,128)(2,1)}, u32[]{:S(2)}, u32[]{:S(2)}) collective-permute-start(bf16[512,768]{1,0:T(8,128)(2,1)} %slice_bitcast_fusion.2), channel_id=1, source_target_pairs={{0,4},{1,5},{2,6},{3,7},{4,0},{5,1},{6,2},{7,3},{8,12},{9,13},{10,... | collective-permute-start | bytes 2359304 | tf_op jit(solution)/shard_map/ppermute | solution.py:723
  120.7 78.9 %collective-permute-start.6 = (bf16[512,768]{1,0:T(8,128)(2,1)}, bf16[512,768]{1,0:T(8,128)(2,1)}, u32[]{:S(2)}, u32[]{:S(2)}) collective-permute-start(bf16[512,768]{1,0:T(8,128)(2,1)} %get-tuple-element.103), channel_id=1, source_target_pairs={{0,4},{1,5},{2,6},{3,7},{4,0},{5,1},{6,2},{7,3},{8,12},{9,13},{10,... | collective-permute-start | bytes 2359304 | tf_op jit(solution)/shard_map/ppermute | solution.py:723
  168.6 46.9 %all-to-all-start.3 = ((bf16[4,384,768]{2,1,0:T(8,128)(2,1)}), bf16[4,384,768]{2,1,0:T(8,128)(2,1)S(1)}, u32[]{:S(2)}, u32[]{:S(2)}) async-start(bf16[4,384,768]{2,1,0:T(8,128)(2,1)} %shard_map.218.refs_8_), calls=%async_computation.3 | async-start | bytes 4718592 | tf_op jit(solution)/shard_map/all_to_all | solution.py:794
  248.6 41.9 %collective-permute-start.7 = (bf16[192,768]{1,0:T(8,128)(2,1)}, bf16[192,768]{1,0:T(8,128)(2,1)S(1)}, u32[]{:S(2)}, u32[]{:S(2)}) collective-permute-start(bf16[192,768]{1,0:T(8,128)(2,1)} %get-tuple-element.105), channel_id=1, source_target_pairs={{0,4},{1,5},{2,6},{3,7},{4,0},{5,1},{6,2},{7,3},{8,12},{9,13},{10,... | collective-permute-start | bytes 884744 | tf_op jit(solution)/shard_map/ppermute | solution.py:723
  249.7 54.8 %collective-permute-start.8 = (bf16[192,768]{1,0:T(8,128)(2,1)}, bf16[192,768]{1,0:T(8,128)(2,1)S(1)}, u32[]{:S(2)}, u32[]{:S(2)}) collective-permute-start(bf16[192,768]{1,0:T(8,128)(2,1)} %get-tuple-element.106), channel_id=1, source_target_pairs={{0,5},{1,4},{2,7},{3,6},{4,1},{5,0},{6,3},{7,2},{8,13},{9,12},{10,... | collective-permute-start | bytes 884744 | tf_op jit(solution)/shard_map/ppermute | solution.py:723
  253.0 66.6 %collective-permute-start.9 = (bf16[192,768]{1,0:T(8,128)(2,1)}, bf16[192,768]{1,0:T(8,128)(2,1)S(1)}, u32[]{:S(2)}, u32[]{:S(2)}) collective-permute-start(bf16[192,768]{1,0:T(8,128)(2,1)} %get-tuple-element.107), channel_id=1, source_target_pairs={{0,6},{1,7},{2,4},{3,5},{4,2},{5,3},{6,0},{7,1},{8,14},{9,15},{10,... | collective-permute-start | bytes 884744 | tf_op jit(solution)/shard_map/ppermute | solution.py:723
  255.2 78.0 %collective-permute-start.10 = (bf16[192,768]{1,0:T(8,128)(2,1)}, bf16[192,768]{1,0:T(8,128)(2,1)}, u32[]{:S(2)}, u32[]{:S(2)}) collective-permute-start(bf16[192,768]{1,0:T(8,128)(2,1)} %get-tuple-element.108), channel_id=1, source_target_pairs={{0,7},{1,6},{2,5},{3,4},{4,3},{5,2},{6,1},{7,0},{8,15},{9,14},{10,... | collective-permute-start | bytes 884744 | tf_op jit(solution)/shard_map/ppermute | solution.py:723
  256.3 42.1 %all-to-all-start.5 = ((bf16[4,192,768]{2,1,0:T(8,128)(2,1)}), bf16[4,192,768]{2,1,0:T(8,128)(2,1)S(1)}, u32[]{:S(2)}, u32[]{:S(2)}) async-start(bf16[4,192,768]{2,1,0:T(8,128)(2,1)} %get-tuple-element.110), calls=%async_computation.5 | async-start | bytes 2359296 | tf_op jit(solution)/shard_map/all_to_all | solution.py:794
  287.0 64.9 %collective-permute-start.13 = (bf16[192,768]{1,0:T(8,128)(2,1)}, bf16[192,768]{1,0:T(8,128)(2,1)}, u32[]{:S(2)}, u32[]{:S(2)}) collective-permute-start(bf16[192,768]{1,0:T(8,128)(2,1)} %get-tuple-element.128), channel_id=1, source_target_pairs={{0,4},{1,5},{2,6},{3,7},{4,0},{5,1},{6,2},{7,3},{8,12},{9,13},{10,... | collective-permute-start | bytes 884744 | tf_op jit(solution)/shard_map/ppermute | solution.py:723
  290.4 81.0 %collective-permute-start.15 = (bf16[192,768]{1,0:T(8,128)(2,1)}, bf16[192,768]{1,0:T(8,128)(2,1)}, u32[]{:S(2)}, u32[]{:S(2)}) collective-permute-start(bf16[192,768]{1,0:T(8,128)(2,1)} %get-tuple-element.129), channel_id=1, source_target_pairs={{0,5},{1,4},{2,7},{3,6},{4,1},{5,0},{6,3},{7,2},{8,13},{9,12},{10,... | collective-permute-start | bytes 884744 | tf_op jit(solution)/shard_map/ppermute | solution.py:723
  299.5 74.0 %all-to-all-start.8 = ((bf16[4,384,768]{2,1,0:T(8,128)(2,1)}), bf16[4,384,768]{2,1,0:T(8,128)(2,1)}, u32[]{:S(2)}, u32[]{:S(2)}) async-start(bf16[4,384,768]{2,1,0:T(8,128)(2,1)} %get-tuple-element.141), calls=%async_computation.8 | async-start | bytes 4718592 | tf_op jit(solution)/shard_map/all_to_all | solution.py:794
  304.5 118.1 %collective-permute-start.16 = (bf16[192,768]{1,0:T(8,128)(2,1)}, bf16[192,768]{1,0:T(8,128)(2,1)}, u32[]{:S(2)}, u32[]{:S(2)}) collective-permute-start(bf16[192,768]{1,0:T(8,128)(2,1)} %get-tuple-element.131), channel_id=1, source_target_pairs={{0,6},{1,7},{2,4},{3,5},{4,2},{5,3},{6,0},{7,1},{8,14},{9,15},{10,... | collective-permute-start | bytes 884744 | tf_op jit(solution)/shard_map/ppermute | solution.py:723
  333.2 89.5 %collective-permute-start.17 = (bf16[192,768]{1,0:T(8,128)(2,1)}, bf16[192,768]{1,0:T(8,128)(2,1)}, u32[]{:S(2)}, u32[]{:S(2)}) collective-permute-start(bf16[192,768]{1,0:T(8,128)(2,1)} %get-tuple-element.132), channel_id=1, source_target_pairs={{0,7},{1,6},{2,5},{3,4},{4,3},{5,2},{6,1},{7,0},{8,15},{9,14},{10,... | collective-permute-start | bytes 884744 | tf_op jit(solution)/shard_map/ppermute | solution.py:723
  373.5 43.7 %all-to-all-start.7 = ((bf16[4,192,768]{2,1,0:T(8,128)(2,1)}), bf16[4,192,768]{2,1,0:T(8,128)(2,1)S(1)}, u32[]{:S(2)}, u32[]{:S(2)}) async-start(bf16[4,192,768]{2,1,0:T(8,128)(2,1)} %get-tuple-element.134), calls=%async_computation.7 | async-start | bytes 2359296 | tf_op jit(solution)/shard_map/all_to_all | solution.py:794
  410.0 42.8 %collective-permute-start.21 = (bf16[96,3072]{1,0:T(8,128)(2,1)}, bf16[96,3072]{1,0:T(8,128)(2,1)}, u32[]{:S(2)}, u32[]{:S(2)}) collective-permute-start(bf16[96,3072]{1,0:T(8,128)(2,1)} %get-tuple-element.222), channel_id=1, source_target_pairs={{0,16},{8,24},{16,0},{24,8},{1,17},{9,25},{17,1},{25,9},{2,18},{10... | collective-permute-start | bytes 1769480 | tf_op jit(solution)/shard_map/ppermute | solution.py:723
  411.5 43.7 %collective-permute-start.22 = (bf16[96,3072]{1,0:T(8,128)(2,1)}, bf16[96,3072]{1,0:T(8,128)(2,1)}, u32[]{:S(2)}, u32[]{:S(2)}) collective-permute-start(bf16[96,3072]{1,0:T(8,128)(2,1)} %get-tuple-element.221), channel_id=1, source_target_pairs={{0,16},{8,24},{16,0},{24,8},{1,17},{9,25},{17,1},{25,9},{2,18},{10... | collective-permute-start | bytes 1769480 | tf_op jit(solution)/shard_map/ppermute | solution.py:723
  412.0 43.7 %collective-permute-start.23 = (bf16[96,3072]{1,0:T(8,128)(2,1)}, bf16[96,3072]{1,0:T(8,128)(2,1)}, u32[]{:S(2)}, u32[]{:S(2)}) collective-permute-start(bf16[96,3072]{1,0:T(8,128)(2,1)} %get-tuple-element.220), channel_id=1, source_target_pairs={{0,16},{8,24},{16,0},{24,8},{1,17},{9,25},{17,1},{25,9},{2,18},{10... | collective-permute-start | bytes 1769480 | tf_op jit(solution)/shard_map/ppermute | solution.py:723
  422.6 61.9 %collective-permute-start.31 = (bf16[1536,768]{1,0:T(8,128)(2,1)}, bf16[1536,768]{1,0:T(8,128)(2,1)}, u32[]{:S(2)}, u32[]{:S(2)}) collective-permute-start(bf16[1536,768]{1,0:T(8,128)(2,1)} %pad_maximum_fusion.refs_1_), channel_id=1, source_target_pairs={{0,8},{8,0},{16,24},{24,16},{1,9},{9,1},{17,25},{25,17},{2,10},{10... | collective-permute-start | bytes 7077896 | tf_op jit(solution)/shard_map/ppermute | solution.py:723
  452.8 66.9 %collective-permute-start.32 = (bf16[256,768]{1,0:T(8,128)(2,1)S(1)}, bf16[256,768]{1,0:T(8,128)(2,1)}, u32[]{:S(2)}, u32[]{:S(2)}) collective-permute-start(bf16[256,768]{1,0:T(8,128)(2,1)S(1)} %copy-done.30), channel_id=1, source_target_pairs={{0,4},{1,5},{2,6},{3,7},{4,0},{5,1},{6,2},{7,3},{8,12},{9,13},{10,... | collective-permute-start | bytes 1179656 | tf_op jit(solution)/shard_map/ppermute | solution.py:723
  455.2 64.6 %collective-permute-start.33 = (bf16[512,768]{1,0:T(8,128)(2,1)}, bf16[512,768]{1,0:T(8,128)(2,1)}, u32[]{:S(2)}, u32[]{:S(2)}) collective-permute-start(bf16[512,768]{1,0:T(8,128)(2,1)} %get-tuple-element.159), channel_id=1, source_target_pairs={{0,4},{1,5},{2,6},{3,7},{4,0},{5,1},{6,2},{7,3},{8,12},{9,13},{10,... | collective-permute-start | bytes 2359304 | tf_op jit(solution)/shard_map/ppermute | solution.py:723
  (77 other events, 960.9 us)
Sparse Core Ops, SparseCore 0:
  10.2 42.2 all-gather.1
